TPU v7x, 32 devices: a whole 2x2x4 slice. The times are simulated.
32 devices in a mesh: grp: 8 (over y, x, core), blk: 4 (over z).
Axes of the slice: x: 2, y: 2, z: 4, core: 2. Of those that a mesh axis runs over, the one named last changes fastest.
Arguments:
- patches: bfloat16 [256, 64, 1152], P(('grp', 'blk')), may hold values from -200 to 200
- probe: bfloat16 [1152], replicated, may hold values from -4 to 4
- w_key: bfloat16 [1152, 1152], P('grp'), may hold values from -0.125 to 1.125
- w_value: bfloat16 [1152, 1152], P('grp'), may hold values from -0.1875 to 0.1875
- w_out: bfloat16 [1152, 1152], P('grp'), may hold values from -0.1875 to 0.1875
- texts: bfloat16 [256, 1152], P(('grp', 'blk')), may hold values from -4 to 4
Outputs:
- grad_image: float32 [256, 1152], P(('grp', 'blk'))
- grad_text: float32 [256, 1152], P(('grp', 'blk'))
All inputs are finite; a program needn't handle non-finite values.
Results may differ from a plain program's by a relative error of at most 0.0095.
Values may be sent and summed in bfloat16 or wider, within the bound.
No kernel may reach another device: no remote copies, remote signals or barrier semaphores. Data moves between devices by JAX's collectives and lax.ppermute only.
A program may use at most 64 MiB of HBM per device.

v0:
```python
import math

import jax
import jax.numpy as jnp
from jax import lax
from jax.sharding import PartitionSpec as P

HEADS = 16


def shifted(array, axis, by):
    devices = lax.axis_size(axis)
    return lax.ppermute(array, axis, [(i, (i + by) % devices) for i in range(devices)])


def head_table(width, heads):
    owner = jnp.arange(width, dtype=jnp.int32) // (width // heads)
    return (owner[:, None] == jnp.arange(heads, dtype=jnp.int32)[None, :]).astype(jnp.float32)


def unit_rows(values):
    inverse = lax.rsqrt(jnp.sum(values * values, axis=1, keepdims=True) + 1e-06)
    return (values * inverse, inverse)


def chain_back(grad_unit, unit_f, inverse):
    inner = jnp.sum(unit_f * grad_unit, axis=1, keepdims=True)
    return (grad_unit - unit_f * inner) * inverse


def pool_weights(scores):
    top = jnp.max(scores, axis=1, keepdims=True)
    expo = jnp.exp(scores - top)
    return expo / jnp.sum(expo, axis=1, keepdims=True)


def cross_rows(left, right):
    return lax.dot_general(
        left, right, (((1,), (1,)), ((), ())), preferred_element_type=jnp.float32
    )


def cross_columns(left, right):
    return lax.dot_general(
        left, right, (((0,), (0,)), ((), ())), preferred_element_type=jnp.float32
    )


def local(patches, probe, w_key, w_value, w_out, texts):
    rows, patch_count, width = patches.shape
    heads = HEADS
    head_size = width // heads
    scaling = 1.0 / math.sqrt(head_size)
    query_table = head_table(width, heads) * probe.astype(jnp.float32)[:, None]
    flat = patches.reshape(rows * patch_count, width)
    columns = flat
    keys = jnp.dot(
        columns,
        lax.all_gather(w_key, "grp", axis=0, tiled=True),
        preferred_element_type=jnp.float32,
    )
    values = jnp.dot(
        columns,
        lax.all_gather(w_value, "grp", axis=0, tiled=True),
        preferred_element_type=jnp.float32,
    )
    scores = (
        jnp.dot(keys, query_table, precision=lax.Precision.HIGHEST).reshape(
            rows, patch_count, heads
        )
        * scaling
    )
    weights = pool_weights(scores)
    pooled = jnp.einsum(
        "rph,rphk->rhk",
        weights,
        values.reshape(rows, patch_count, heads, head_size),
        precision=lax.Precision.HIGHEST,
    ).reshape(rows, width)
    pooled_b = pooled.astype(jnp.bfloat16)
    columns = pooled_b
    embed = jnp.dot(
        columns,
        lax.all_gather(w_out, "grp", axis=0, tiled=True),
        preferred_element_type=jnp.float32,
    )
    unit_image, inverse_image = unit_rows(embed)
    unit_image_b = unit_image.astype(jnp.bfloat16)
    unit_text, inverse_text = unit_rows(texts.astype(jnp.float32))
    unit_text_b = unit_text.astype(jnp.bfloat16)
    cycle = lax.axis_size("blk")
    zero_rows = jnp.zeros((rows, width), jnp.float32)
    diagonal = jnp.eye(rows, dtype=jnp.float32)

    def lap_step(turn, carry):
        visiting, partial_value, grad_unit = carry
        logits = 10.0 * cross_rows(unit_image_b, visiting) - 2.0
        target = diagonal * (turn == 0).astype(jnp.float32)
        slopes = (jax.nn.sigmoid(logits) - target).astype(jnp.bfloat16)
        grad_unit = grad_unit + jnp.dot(slopes, visiting, preferred_element_type=jnp.float32)
        partial_value = partial_value + cross_columns(slopes, unit_image_b)
        visiting = shifted(visiting, "blk", 1)
        partial_value = shifted(partial_value, "blk", 1)
        return (visiting, partial_value, grad_unit)

    _, grad_unit_text, grad_unit_image = lax.fori_loop(
        0, cycle, lap_step, (unit_text_b, zero_rows, zero_rows)
    )
    grad_image = chain_back(10.0 * grad_unit_image, unit_image, inverse_image)
    grad_text = chain_back(10.0 * grad_unit_text, unit_text, inverse_text)
    return (grad_image, grad_text)


def solution(mesh):
    in_specs = (
        P(("grp", "blk"), None, None),
        P(),
        P("grp", None),
        P("grp", None),
        P("grp", None),
        P(("grp", "blk"), None),
    )
    out_specs = (P(("grp", "blk"), None), P(("grp", "blk"), None))
    return jax.shard_map(local, mesh=mesh, in_specs=in_specs, out_specs=out_specs, check_vma=False)
```

profile of v0, /device:TPU:0, one launch (start us, length us, event | category | flops | bytes accessed | tf_op | source)
XLA Modules:
  0.0 144.0 jit_solution(4493853095481265499)
XLA Ops:
  10.1 0.8 fusion.26
  11.0 31.9 %all-gather.4.cloned.1.call-done = bf16[1152,1152]{1,0:T(8,128)(2,1)} async-done(((bf16[144,1152]{1,0:T(8,128)(2,1)}), bf16[1152,1152]{1,0:T(8,128)(2,1)}) %all-gather.4.cloned.1.call-update) | async-done | bytes 2654224 | tf_op jit(solution)/shard_map/all_gather | solution.py:59
  42.9 3.6 %fusion.32 = f32[512,1152]{1,0:T(8,128)S(1)} fusion(bf16[512,1152]{1,0:T(8,128)(2,1)S(1)} %bitcast.43, bf16[1152,1152]{1,0:T(8,128)(2,1)} %all-gather.4.cloned.1.call-done), kind=kOutput, calls=%fused_computation.50 | convolution fusion | flops 1358954496 | bytes 6193152 | tf_op jit(solution)/shard_map/dot_general | solution.py:57
  46.5 2.3 %convolution_multiply_fusion.1 = f32[512,16]{0,1:T(8,128)S(1)} fusion(f32[512,1152]{1,0:T(8,128)S(1)} %fusion.32, f32[1152]{0:T(1024)S(1)} %convert_element_type.44, s32[1152]{0:T(1024)S(1)} %add_select_fusion), kind=kOutput, calls=%fused_computation.17 | convolution fusion | flops 113291264 | bytes 2401280 | tf_op jit(solution)/shard_map/dot_general | solution.py:68
  48.9 26.2 %all-gather.6.cloned.1.call-done = bf16[1152,1152]{1,0:T(8,128)(2,1)} async-done(((bf16[144,1152]{1,0:T(8,128)(2,1)}), bf16[1152,1152]{1,0:T(8,128)(2,1)}) %all-gather.6.cloned.1.call-update) | async-done | bytes 2654224 | tf_op jit(solution)/shard_map/all_gather | solution.py:64
  75.0 5.2 %copy.9 = bf16[1152,1152]{0,1:T(8,128)(2,1)} copy(bf16[1152,1152]{1,0:T(8,128)(2,1)} %all-gather.6.cloned.1.call-done) | data formatting | bytes 5308416 | tf_op jit(solution)/shard_map/all_gather | solution.py:64
  80.3 2.6 %fusion.31 = (f32[8,16]{0,1:T(8,128)S(1)}, f32[8,64,16]{1,0,2:T(8,128)S(1)}) fusion(f32[8,64,16]{1,0,2:T(8,128)S(1)} %mul.116), kind=kOutput, calls=%fused_computation.49 | output fusion | flops 16447 | bytes 66048 | tf_op jit(solution)/shard_map/sub | solution.py:33
  83.0 4.8 %fusion.10 = f32[8,64,16,72]{3,1,2,0:T(8,128)S(1)} fusion(bf16[16,72,1152,1]{2,1,0,3:T(8,128)(2,1)} %bitcast.44, bf16[8,64,1152]{2,1,0:T(8,128)(2,1)S(1)} %copy-done), kind=kOutput, calls=%fused_computation.13 | convolution fusion | flops 1358954496 | bytes 6193152 | tf_op jit(solution)/shard_map/dot_general | solution.py:62
  87.7 3.6 %fusion.18 = f32[8,16,1,72]{3,2,1,0:T(1,128)S(1)} fusion(f32[8,64,16,72]{3,1,2,0:T(8,128)S(1)} %fusion.10, f32[8,64,16,1]{1,0,2,3:T(8,128)S(1)} %divide_bitcast_fusion), kind=kOutput, calls=%fused_computation.23 | convolution fusion | flops 7077888 | bytes 2428928 | tf_op jit(solution)/shard_map/rph,rphk->rhk/dot_general | solution.py:74
  91.5 15.8 %all-gather.8.cloned.1.call-done = bf16[1152,1152]{1,0:T(8,128)(2,1)} async-done(((bf16[144,1152]{1,0:T(8,128)(2,1)}), bf16[1152,1152]{1,0:T(8,128)(2,1)}) %all-gather.8.cloned.1.call-update) | async-done | bytes 2654224 | tf_op jit(solution)/shard_map/all_gather | solution.py:84
  107.3 2.3 %multiply_reduce_fusion.1 = (f32[8]{0:T(128)S(1)}, f32[8,1152]{1,0:T(8,128)S(1)}) fusion(bf16[8,1152]{1,0:T(8,128)(2,1)S(1)} %convert_element_type.46, bf16[1152,1152]{1,0:T(8,128)(2,1)} %all-gather.8.cloned.1.call-done), kind=kOutput, calls=%fused_computation.37 | convolution fusion | flops 21252088 | bytes 2709536 | tf_op jit(solution)/shard_map/dot_general | solution.py:82
  109.7 26.0 %while.20 = (s32[]{:T(128)}, bf16[8,1152]{1,0:T(8,128)(2,1)S(1)}, f32[8,1152]{1,0:T(8,128)S(1)}, f32[8,1152]{1,0:T(8,128)S(1)}, bf16[8,1152]{1,0:T(8,128)(2,1)S(1)}, /*index=5*/s32[]{:T(128)}, s32[]{:T(128)}) while((s32[]{:T(128)}, bf16[8,1152]{1,0:T(8,128)(2,1)S(1)}, f32[8,1152]{1,0:T(8,128)S(1)}, f32[8,1152]{1,0:T(8,128)S(1)}, ...), condition=%wide.region_5.6_spmd.clone, body=%wide.region_4.5_spmd.clone.sunk | while | flops 470596 | bytes 479792 | solution.py:106
  109.8 1.5 %collective-permute-start = (bf16[8,1152]{1,0:T(8,128)(2,1)S(1)}, bf16[8,1152]{1,0:T(8,128)(2,1)S(1)}, u32[]{:S(2)}, u32[]{:S(2)}) collective-permute-start(bf16[8,1152]{1,0:T(8,128)(2,1)S(1)} %copy.20), channel_id=1, source_target_pairs={{0,1},{1,2},{2,3},{3,0},{4,5},{5,6},{6,7},{7,4},{8,9},{9,10},{10,1... | collective-permute-start | bytes 55304 | tf_op jit(solution)/shard_map/while/body/eval_jaxpr/ppermute | solution.py:13
  111.6 1.5 %collective-permute-start.1 = (f32[8,1152]{1,0:T(8,128)S(1)}, f32[8,1152]{1,0:T(8,128)S(1)}, u32[]{:S(2)}, u32[]{:S(2)}) collective-permute-start(f32[8,1152]{1,0:T(8,128)S(1)} %convolution_add_fusion.4), channel_id=1, source_target_pairs={{0,1},{1,2},{2,3},{3,0},{4,5},{5,6},{6,7},{7,4},{8,9},{9,10},{10,1... | collective-permute-start | bytes 110600 | tf_op jit(solution)/shard_map/while/body/eval_jaxpr/ppermute | solution.py:13
  113.3 2.1 %collective-permute-done = bf16[8,1152]{1,0:T(8,128)(2,1)S(1)} collective-permute-done((bf16[8,1152]{1,0:T(8,128)(2,1)S(1)}, bf16[8,1152]{1,0:T(8,128)(2,1)S(1)}, u32[]{:S(2)}, u32[]{:S(2)}) %collective-permute-start) | collective-permute-done | bytes 18464 | tf_op jit(solution)/shard_map/while/body/eval_jaxpr/ppermute | solution.py:13
  115.4 2.0 %collective-permute-done.1 = f32[8,1152]{1,0:T(8,128)S(1)} collective-permute-done((f32[8,1152]{1,0:T(8,128)S(1)}, f32[8,1152]{1,0:T(8,128)S(1)}, u32[]{:S(2)}, u32[]{:S(2)}) %collective-permute-start.1) | collective-permute-done | bytes 36896 | tf_op jit(solution)/shard_map/while/body/eval_jaxpr/ppermute | solution.py:13
  117.7 1.2 collective-permute-start.1
  119.0 3.9 %collective-permute-done = bf16[8,1152]{1,0:T(8,128)(2,1)S(1)} collective-permute-done((bf16[8,1152]{1,0:T(8,128)(2,1)S(1)}, bf16[8,1152]{1,0:T(8,128)(2,1)S(1)}, u32[]{:S(2)}, u32[]{:S(2)}) %collective-permute-start) | collective-permute-done | bytes 18464 | tf_op jit(solution)/shard_map/while/body/eval_jaxpr/ppermute | solution.py:13
  123.8 0.8 collective-permute-start.1
  124.8 4.3 %collective-permute-done = bf16[8,1152]{1,0:T(8,128)(2,1)S(1)} collective-permute-done((bf16[8,1152]{1,0:T(8,128)(2,1)S(1)}, bf16[8,1152]{1,0:T(8,128)(2,1)S(1)}, u32[]{:S(2)}, u32[]{:S(2)}) %collective-permute-start) | collective-permute-done | bytes 18464 | tf_op jit(solution)/shard_map/while/body/eval_jaxpr/ppermute | solution.py:13
  129.9 1.4 collective-permute-start.1
  131.4 3.7 %collective-permute-done = bf16[8,1152]{1,0:T(8,128)(2,1)S(1)} collective-permute-done((bf16[8,1152]{1,0:T(8,128)(2,1)S(1)}, bf16[8,1152]{1,0:T(8,128)(2,1)S(1)}, u32[]{:S(2)}, u32[]{:S(2)}) %collective-permute-start) | collective-permute-done | bytes 18464 | tf_op jit(solution)/shard_map/while/body/eval_jaxpr/ppermute | solution.py:13
  135.9 0.7 fusion.25
  136.8 0.7 subtract_multiply_fusion
  (45 shorter events, 7.1 us)
Async XLA Ops:
  7.2 35.7 %copy-start = (bf16[8,64,1152]{2,1,0:T(8,128)(2,1)S(1)}, bf16[8,64,1152]{2,1,0:T(8,128)(2,1)}, u32[]{:S(2)}) copy-start(bf16[8,64,1152]{2,1,0:T(8,128)(2,1)} %param.8) | copy-start | bytes 3538948
  7.2 35.7 %all-gather.4.cloned.1.call-start = ((), (), s32[]{:S(2)}) async-start(), calls=%async_computation | async-start | bytes 2985984 | tf_op jit(solution)/shard_map/all_gather | solution.py:59
  7.9 67.1 %all-gather.6.cloned.1.call-start = ((), (), s32[]{:S(2)}) async-start(), calls=%async_computation.1 | async-start | bytes 2985984 | tf_op jit(solution)/shard_map/all_gather | solution.py:64
  8.7 98.7 %all-gather.8.cloned.1.call-start = ((), (), s32[]{:S(2)}) async-start(), calls=%async_computation.2 | async-start | bytes 2985984 | tf_op jit(solution)/shard_map/all_gather | solution.py:84
  87.7 21.9 %copy-start.1 = (bf16[8,1152]{1,0:T(8,128)(2,1)S(1)}, bf16[8,1152]{1,0:T(8,128)(2,1)}, u32[]{:S(2)}) copy-start(bf16[8,1152]{1,0:T(8,128)(2,1)} %param.13) | copy-start | bytes 55300
  109.8 5.6 %collective-permute-start = (bf16[8,1152]{1,0:T(8,128)(2,1)S(1)}, bf16[8,1152]{1,0:T(8,128)(2,1)S(1)}, u32[]{:S(2)}, u32[]{:S(2)}) collective-permute-start(bf16[8,1152]{1,0:T(8,128)(2,1)S(1)} %copy.20), channel_id=1, source_target_pairs={{0,1},{1,2},{2,3},{3,0},{4,5},{5,6},{6,7},{7,4},{8,9},{9,10},{10,1... | collective-permute-start | bytes 55304 | tf_op jit(solution)/shard_map/while/body/eval_jaxpr/ppermute | solution.py:13
  111.6 5.8 %collective-permute-start.1 = (f32[8,1152]{1,0:T(8,128)S(1)}, f32[8,1152]{1,0:T(8,128)S(1)}, u32[]{:S(2)}, u32[]{:S(2)}) collective-permute-start(f32[8,1152]{1,0:T(8,128)S(1)} %convolution_add_fusion.4), channel_id=1, source_target_pairs={{0,1},{1,2},{2,3},{3,0},{4,5},{5,6},{6,7},{7,4},{8,9},{9,10},{10,1... | collective-permute-start | bytes 110600 | tf_op jit(solution)/shard_map/while/body/eval_jaxpr/ppermute | solution.py:13
  117.4 5.6 %collective-permute-start = (bf16[8,1152]{1,0:T(8,128)(2,1)S(1)}, bf16[8,1152]{1,0:T(8,128)(2,1)S(1)}, u32[]{:S(2)}, u32[]{:S(2)}) collective-permute-start(bf16[8,1152]{1,0:T(8,128)(2,1)S(1)} %copy.20), channel_id=1, source_target_pairs={{0,1},{1,2},{2,3},{3,0},{4,5},{5,6},{6,7},{7,4},{8,9},{9,10},{10,1... | collective-permute-start | bytes 55304 | tf_op jit(solution)/shard_map/while/body/eval_jaxpr/ppermute | solution.py:13
  117.7 5.8 %collective-permute-start.1 = (f32[8,1152]{1,0:T(8,128)S(1)}, f32[8,1152]{1,0:T(8,128)S(1)}, u32[]{:S(2)}, u32[]{:S(2)}) collective-permute-start(f32[8,1152]{1,0:T(8,128)S(1)} %convolution_add_fusion.4), channel_id=1, source_target_pairs={{0,1},{1,2},{2,3},{3,0},{4,5},{5,6},{6,7},{7,4},{8,9},{9,10},{10,1... | collective-permute-start | bytes 110600 | tf_op jit(solution)/shard_map/while/body/eval_jaxpr/ppermute | solution.py:13
  123.5 5.6 %collective-permute-start = (bf16[8,1152]{1,0:T(8,128)(2,1)S(1)}, bf16[8,1152]{1,0:T(8,128)(2,1)S(1)}, u32[]{:S(2)}, u32[]{:S(2)}) collective-permute-start(bf16[8,1152]{1,0:T(8,128)(2,1)S(1)} %copy.20), channel_id=1, source_target_pairs={{0,1},{1,2},{2,3},{3,0},{4,5},{5,6},{6,7},{7,4},{8,9},{9,10},{10,1... | collective-permute-start | bytes 55304 | tf_op jit(solution)/shard_map/while/body/eval_jaxpr/ppermute | solution.py:13
  123.8 5.8 %collective-permute-start.1 = (f32[8,1152]{1,0:T(8,128)S(1)}, f32[8,1152]{1,0:T(8,128)S(1)}, u32[]{:S(2)}, u32[]{:S(2)}) collective-permute-start(f32[8,1152]{1,0:T(8,128)S(1)} %convolution_add_fusion.4), channel_id=1, source_target_pairs={{0,1},{1,2},{2,3},{3,0},{4,5},{5,6},{6,7},{7,4},{8,9},{9,10},{10,1... | collective-permute-start | bytes 110600 | tf_op jit(solution)/shard_map/while/body/eval_jaxpr/ppermute | solution.py:13
  129.6 5.6 %collective-permute-start = (bf16[8,1152]{1,0:T(8,128)(2,1)S(1)}, bf16[8,1152]{1,0:T(8,128)(2,1)S(1)}, u32[]{:S(2)}, u32[]{:S(2)}) collective-permute-start(bf16[8,1152]{1,0:T(8,128)(2,1)S(1)} %copy.20), channel_id=1, source_target_pairs={{0,1},{1,2},{2,3},{3,0},{4,5},{5,6},{6,7},{7,4},{8,9},{9,10},{10,1... | collective-permute-start | bytes 55304 | tf_op jit(solution)/shard_map/while/body/eval_jaxpr/ppermute | solution.py:13
  129.9 5.8 %collective-permute-start.1 = (f32[8,1152]{1,0:T(8,128)S(1)}, f32[8,1152]{1,0:T(8,128)S(1)}, u32[]{:S(2)}, u32[]{:S(2)}) collective-permute-start(f32[8,1152]{1,0:T(8,128)S(1)} %convolution_add_fusion.4), channel_id=1, source_target_pairs={{0,1},{1,2},{2,3},{3,0},{4,5},{5,6},{6,7},{7,4},{8,9},{9,10},{10,1... | collective-permute-start | bytes 110600 | tf_op jit(solution)/shard_map/while/body/eval_jaxpr/ppermute | solution.py:13
Sparse Core Ops, SparseCore 0:
  9.9 32.9 all-gather.3
  44.8 30.2 all-gather.5
  76.9 30.3 all-gather.7
where the time goes:
time: 144 us
  waiting for transfers between devices  93.7 us (65%)
  matrix products  18.4 us (13%)
  between operations  13.8 us (10%)
  starting transfers between devices  6.56 us (5%)
  other arithmetic  6.12 us (4%)
  local copies, waits for them, and re-layouts  5.44 us (4%)
    all_gather x1, waiting for transfers between devices, local(): lax.all_gather(w_key, 'grp', axis=0, tiled=True)  31.9 us
    all_gather x1, waiting for transfers between devices, local(): lax.all_gather(w_value, 'grp', axis=0, tiled=True)  26.2 us
    ppermute x8, waiting for transfers between devices, shifted(): lax.ppermute(array, axis, [(i, (i + by) % devices) for i in range(devices)])  17.7 us
    all_gather x1, waiting for transfers between devices, local(): lax.all_gather(w_out, 'grp', axis=0, tiled=True)  15.8 us
    ppermute x8, starting transfers between devices, shifted(): lax.ppermute(array, axis, [(i, (i + by) % devices) for i in range(devices)])  6.45 us
    all_gather x1, local copies, waits for them, and re-layouts, local(): lax.all_gather(w_value, 'grp', axis=0, tiled=True)  5.21 us
    dot_general x1, matrix products, local(): jnp.dot(columns, lax.all_gather(w_value, 'grp', axis=0, tiled=True), pref...  4.77 us
    dot_general x1, matrix products, local(): jnp.einsum('rph,rphk->rhk', weights, values.reshape(rows, patch_count, he...  3.65 us
  transfers between devices with their start and end apart: 11, of which 11 were waited for; matrix products, arithmetic and copies ran while one was open for 18% of the time, Pallas kernels for 0%

commit v1 on v0

v1 whole, which is shorter than its diff:
```python
import functools
import math

import jax
import jax.numpy as jnp
from jax import lax
from jax.experimental import pallas as pl
from jax.experimental.pallas import tpu as pltpu
from jax.sharding import PartitionSpec as P

HEADS = 16
CORES = 2
F32 = jnp.float32
BF16 = jnp.bfloat16


def struct(shape, dtype):
    return jax.ShapeDtypeStruct(shape, dtype)


def call(body, out, *args, scratch=(), space=pltpu.VMEM):
    return pl.pallas_call(
        body,
        out_shape=out,
        in_specs=[pl.BlockSpec(memory_space=space)] * len(args),
        scratch_shapes=scratch,
        compiler_params=pltpu.CompilerParams(vmem_limit_bytes=24 * 2**20),
    )(*args)


def nt(left, right):
    return lax.dot_general(left, right, (((1,), (1,)), ((), ())), preferred_element_type=F32)


def nn(left, right):
    return jnp.dot(left, right, preferred_element_type=F32)


def unit_rows(values):
    inverse = lax.rsqrt(jnp.sum(values * values, axis=1, keepdims=True) + 1e-06)
    return values * inverse, inverse


def chain_back(grad_unit, unit_f, inverse):
    inner = jnp.sum(unit_f * grad_unit, axis=1, keepdims=True)
    return (grad_unit - unit_f * inner) * inverse


def slopes_of(left, right, place):
    logits = 10.0 * nt(left, right) - 2.0
    row = lax.broadcasted_iota(jnp.int32, logits.shape, 0)
    column = lax.broadcasted_iota(jnp.int32, logits.shape, 1)
    target = jnp.where(row + place == column, 1.0, 0.0)
    return (jax.nn.sigmoid(logits) - target).astype(BF16)


def split_terms(values):
    high = values.astype(BF16)
    rest = values - high.astype(F32)
    middle = rest.astype(BF16)
    return high, middle, (rest - middle.astype(F32)).astype(BF16)


def prepare_kernel(
    probe_hbm, w_key_hbm, w_value_hbm, out_ref, probe, w_key, w_value, sems
):
    part, width = w_key.shape
    devices, rows, _ = out_ref.shape
    copies = [
        pltpu.make_async_copy(source, target, sems.at[i])
        for i, (source, target) in enumerate(
            [(probe_hbm, probe), (w_key_hbm, w_key), (w_value_hbm, w_value)]
        )
    ]
    for copy in copies:
        copy.start()
    head = lax.broadcasted_iota(jnp.int32, (HEADS, width), 0)
    first = lax.broadcasted_iota(jnp.int32, (HEADS, width), 1) - head * (width // HEADS)
    inside = (first >= 0) & (first < width // HEADS)
    copies[0].wait()
    copies[1].wait()
    table = jnp.where(inside, probe[...].astype(F32).reshape(1, width), 0.0).astype(BF16)
    keys = [
        term[h * rows : (h + 1) * rows]
        for term in split_terms(nt(table, w_key[...]))
        for h in range(HEADS // rows)
    ]
    copies[2].wait()
    for k in range(devices):
        columns = w_value[:, k * part : (k + 1) * part]
        pieces = [columns[j * rows : (j + 1) * rows] for j in range(part // rows)]
        out_ref[k] = jnp.concatenate(pieces + keys, axis=1)


def shard_kernel(parts_ref, w_out_ref, out_ref):
    devices, rows, _ = parts_ref.shape
    part, width = w_out_ref.shape
    packed = part // rows * part
    out_ref[:devices, :, :packed] = parts_ref[:, :, :packed]
    out_ref[devices:, :, :width] = w_out_ref[...].reshape(part // rows, rows, width)


def attend_kernel(images, scaling, x_ref, parts_ref, *refs):
    outs, (table, every) = refs[:-2], refs[-2:]
    x = x_ref[...]
    width = x.shape[1]
    patches = x.shape[0] // images
    devices, rows, length = parts_ref.shape
    part = width // devices
    pieces = table.shape[0] // rows
    for j in range(pieces):
        first = length - (pieces - j) * part
        for k in range(devices):
            table[j * rows : (j + 1) * rows, k * part : (k + 1) * part] = parts_ref[
                k, :, first : first + part
            ]
    parts = nt(table[...], x)
    scores = (parts[:HEADS] + parts[HEADS : 2 * HEADS] + parts[2 * HEADS :]) * scaling
    image = lax.broadcasted_iota(jnp.int32, (images, x.shape[0]), 0)
    first = lax.broadcasted_iota(jnp.int32, (images, x.shape[0]), 1) - image * patches
    own = (first >= 0) & (first < patches)
    spread = jnp.where(own[None], scores[:, None, :], -jnp.inf)
    expo = jnp.exp(spread - jnp.max(spread, axis=2, keepdims=True))
    weights = expo / jnp.sum(expo, axis=2, keepdims=True)
    weights = weights.reshape(HEADS * images, x.shape[0])
    high = weights.astype(BF16)
    low = (weights - high.astype(F32)).astype(BF16)
    mixed = nn(jnp.concatenate([high, low], axis=0), x)
    mixed = (mixed[: HEADS * images] + mixed[HEADS * images :]).astype(BF16)
    every[...] = mixed.reshape(every.shape)
    chip = lax.axis_index("grp") // CORES
    for m, out_ref in enumerate(outs):
        out_ref[...] = every[chip ^ m]


def project_kernel(images, chips, *refs):
    mixed_refs, (parts_ref, w_out_ref, other_ref) = refs[:chips], refs[chips : chips + 3]
    out_refs, w_value = refs[chips + 3 : -1], refs[-1]
    _, rows, width = mixed_refs[0].shape
    devices = parts_ref.shape[0]
    part = w_out_ref.shape[0]
    heads = rows // images
    core = lax.rem(lax.axis_index("grp"), CORES)
    head = lax.broadcasted_iota(jnp.int32, (chips, images, part), 2)
    embed = jnp.zeros((chips * images, width), F32)
    for s, columns in enumerate((parts_ref, other_ref)):
        for k in range(devices):
            for j in range(part // rows):
                w_value[s, k * part + j * rows : k * part + (j + 1) * rows] = columns[
                    k, :, j * part : (j + 1) * part
                ]
        shard = core if s == 0 else 1 - core
        mixed = jnp.concatenate([ref[shard] for ref in mixed_refs], axis=0)
        every = nn(mixed, w_value[s]).reshape(chips, heads, images, part)
        pooled = every[:, 0]
        for h in range(1, heads):
            pooled = jnp.where(head >= h * (part // heads), every[:, h], pooled)
        pooled = pooled.reshape(chips * images, part).astype(BF16)
        rows_out = w_out_ref[...]
        if s == 1:
            rows_out = other_ref[devices:, :, :width].reshape(part, width)
        embed = embed + nn(pooled, rows_out)
    for m, out_ref in enumerate(out_refs):
        out_ref[...] = embed[m * images : (m + 1) * images].astype(BF16)


def unit_image_kernel(chips, *refs):
    text_ref, unit_ref, inverse_ref, both_ref = refs[chips:]
    embed = refs[0][...].astype(F32)
    for ref in refs[1:chips]:
        embed = embed + ref[...].astype(F32)
    unit, inverse = unit_rows(embed)
    unit_ref[...] = unit
    inverse_ref[...] = jnp.broadcast_to(inverse, inverse_ref.shape)
    for k in range(both_ref.shape[0]):
        both_ref[k, 0] = unit.astype(BF16)
        both_ref[k, 1] = text_ref[...]


def grads_kernel(unit_ref, inverse_ref, text_ref, both_ref, grad_image_ref, grad_text_ref):
    blocks, _, images, width = both_ref.shape
    place = lax.axis_index("blk") * images
    every = both_ref[...].astype(F32)
    all_images = every[:, 0].reshape(blocks * images, width).astype(BF16)
    all_texts = every[:, 1].reshape(blocks * images, width)
    words = unit_rows(all_texts)[0].astype(BF16)
    unit = unit_ref[...]
    slopes = slopes_of(unit.astype(BF16), words, place)
    grad_image_ref[...] = chain_back(10.0 * nn(slopes, words), unit, inverse_ref[:, :1])
    unit, inverse = unit_rows(text_ref[...].astype(F32))
    slopes = slopes_of(unit.astype(BF16), all_images, place)
    grad_text_ref[...] = chain_back(10.0 * nn(slopes, all_images), unit, inverse)


def swap(array, axis):
    return lax.all_to_all(array, axis, 0, 0, tiled=True)


def exchange(array, devices, flip):
    return lax.ppermute(array, "grp", [(i, i ^ flip) for i in range(devices)])


def exchange_chips(arrays, devices):
    return [array if m == 0 else exchange(array, devices, m * CORES) for m, array in enumerate(arrays)]


def local(patches, probe, w_key, w_value, w_out, texts):
    images, patch_count, width = patches.shape
    devices = lax.axis_size("grp")
    blocks = lax.axis_size("blk")
    part = w_key.shape[0]
    heads = HEADS // devices
    scaling = 1.0 / math.sqrt(width // HEADS)
    flat = patches.reshape(images * patch_count, width)

    rows = heads * images
    packed = part // rows * part
    chips = devices // CORES
    parts = call(
        prepare_kernel,
        struct((devices, rows, packed + 3 * HEADS // rows * part), BF16),
        *[pltpu.with_memory_space_constraint(a, pltpu.HBM) for a in (probe, w_key, w_value)],
        scratch=[
            pltpu.VMEM(probe.shape, BF16),
            pltpu.VMEM(w_key.shape, BF16),
            pltpu.VMEM(w_value.shape, BF16),
            pltpu.SemaphoreType.DMA((3,)),
        ],
        space=pltpu.HBM,
    )
    parts = swap(parts, "grp")
    shard = call(
        shard_kernel,
        struct((devices + part // rows, rows, max(packed, width)), BF16),
        parts,
        w_out,
    )
    other = exchange(shard, devices, 1)
    mixed = call(
        functools.partial(attend_kernel, images, scaling),
        [struct((CORES, rows, width), BF16)] * chips,
        flat,
        parts,
        scratch=[
            pltpu.VMEM((3 * HEADS, width), BF16),
            pltpu.VMEM((chips, CORES, rows, width), BF16),
        ],
    )
    partial_embed = call(
        functools.partial(project_kernel, images, chips),
        [struct((images, width), BF16)] * chips,
        *exchange_chips(mixed, devices),
        parts,
        w_out,
        other,
        scratch=[pltpu.VMEM((CORES, width, part), BF16)],
    )
    unit, inverse, both = call(
        functools.partial(unit_image_kernel, chips),
        (
            struct((images, width), F32),
            struct((images, 128), F32),
            struct((blocks, 2, images, width), BF16),
        ),
        *exchange_chips(partial_embed, devices),
        texts,
    )
    return call(
        grads_kernel,
        (struct((images, width), F32), struct((images, width), F32)),
        unit,
        inverse,
        texts,
        swap(both, "blk"),
    )


def solution(mesh):
    in_specs = (
        P(("grp", "blk"), None, None),
        P(),
        P("grp", None),
        P("grp", None),
        P("grp", None),
        P(("grp", "blk"), None),
    )
    out_specs = (P(("grp", "blk"), None), P(("grp", "blk"), None))
    return jax.shard_map(local, mesh=mesh, in_specs=in_specs, out_specs=out_specs, check_vma=False)
```

time: 144 us -> 45.4 us (0.32)
  waiting for transfers between devices: 93.7 us -> 6.99 us
  blocking collectives: 0 us -> 25.5 us
  matrix products: 18.4 us -> 0 us
  between operations: 13.8 us -> 0.71 us
  other arithmetic: 6.12 us -> 0 us
  local copies, waits for them, and re-layouts: 5.44 us -> 0.02 us
  Pallas kernels: 0 us -> 4.83 us
    all_gather x3 -> x0, waiting for transfers between devices: 73.9 us -> none  [the longest x1 31.9 us: local(): lax.all_gather(w_key, 'grp', axis=0, tiled=True)]
    all_to_all x0 -> x2, blocking collectives: none -> 25.5 us  [swap(): return lax.all_to_all(array, axis, 0, 0, tiled=True)]
    dot_general x17 -> x0, matrix products: 18.4 us -> none  [the longest x1 4.77 us: local(): jnp.dot(columns, lax.all_gather(w_value, 'grp', axis=0, tiled=True), pref...]
    ppermute x8 -> x7, waiting for transfers between devices: 17.7 us -> 6.99 us  [exchange(): return lax.ppermute(array, 'grp', [(i, i ^ flip) for i in range(devices)])]
    all_gather x1 -> x0, local copies, waits for them, and re-layouts: 5.21 us -> none  [local(): lax.all_gather(w_value, 'grp', axis=0, tiled=True)]
    pallas_call x0 -> x6, Pallas kernels: none -> 4.83 us  [call(): pl.pallas_call(body, out_shape=out, in_specs=[pl.BlockSpec(memory_space=s...]
    sub x1 -> x0, other arithmetic: 2.6 us -> none  [pool_weights(): expo = jnp.exp(scores - top)]
    unnamed x3 -> x0, waiting for transfers between devices: 2.06 us -> none
  transfers between devices with their start and end apart: 11 -> 7, of which waited for: 11 -> 5; matrix products, arithmetic and copies ran while one was open for 18% -> 0% of each run, Pallas kernels for 0% -> 3%
where the time goes in v1:
time: 45.4 us; the launch traced here: 45.2 us
  blocking collectives  25.5 us (56%)
  starting transfers between devices  7.18 us (16%)
  waiting for transfers between devices  6.99 us (15%)
  Pallas kernels  4.83 us (11%)
  between operations  0.71 us (2%)
    all_to_all x2, blocking collectives, swap(): return lax.all_to_all(array, axis, 0, 0, tiled=True)  25.5 us
    ppermute x7, starting transfers between devices, exchange(): return lax.ppermute(array, 'grp', [(i, i ^ flip) for i in range(devices)])  7.18 us
    ppermute x7, waiting for transfers between devices, exchange(): return lax.ppermute(array, 'grp', [(i, i ^ flip) for i in range(devices)])  6.99 us
    pallas_call x6, Pallas kernels, call(): pl.pallas_call(body, out_shape=out, in_specs=[pl.BlockSpec(memory_space=s...  4.83 us
  transfers between devices with their start and end apart: 7, of which 5 were waited for; matrix products, arithmetic and copies ran while one was open for 0% of the time, Pallas kernels for 3%

profile of v1, /device:TPU:0, one launch (start us, length us, event | category | flops | bytes accessed | tf_op | source)
XLA Modules:
  0.0 45.2 jit_solution(8894391775342455314)
XLA Ops:
  0.6 1.5 %shard_map.77 = bf16[8,16,1728]{2,1,0:T(8,128)(2,1)S(1)} custom-call(bf16[1152]{0:T(1024)(128)(2,1)} %probe_hbm.1, bf16[144,1152]{1,0:T(8,128)(2,1)} %w_key_hbm.1, bf16[144,1152]{1,0:T(8,128)(2,1)} %w_value_hbm.1), custom_call_target="tpu_custom_call" | custom-call | tf_op jit(solution)/shard_map/pallas_call | solution.py:22
  2.2 0.0 copy-start.1
  2.2 14.1 %all_to_all.10.parts_ref.refs_4_ = bf16[8,16,1728]{2,1,0:T(8,128)(2,1)S(1)} all-to-all(bf16[8,16,1728]{2,1,0:T(8,128)(2,1)S(1)} %shard_map.77), channel_id=1, replica_groups=mesh['grp'=8,'blk'=4] {'grp'}, dimensions={0} | all-to-all | bytes 884736 | tf_op jit(solution)/shard_map/all_to_all | solution.py:196
  16.3 0.1 shard_map.79
  16.4 0.1 collective-permute-start.3
  16.5 1.2 %shard_map.78 = (bf16[2,16,1152]{2,1,0:T(8,128)(2,1)S(1)}, bf16[2,16,1152]{2,1,0:T(8,128)(2,1)S(1)}, bf16[2,16,1152]{2,1,0:T(8,128)(2,1)S(1)}, bf16[2,16,1152]{2,1,0:T(8,128)(2,1)S(1)}) custom-call(bf16[512,1152]{1,0:T(8,128)(2,1)S(1)} %bitcast.1, bf16[8,16,1728]{2,1,0:T(8,128)(2,1)S(1)} %all_to_all.10.parts_ref.refs_4_), custom_call_target="tpu_custom_call" | custom-call | tf_op jit(solution)/shard_map/pallas_call | solution.py:22
  17.6 0.0 copy-start.2
  17.6 0.6 %collective-permute-start = (bf16[2,16,1152]{2,1,0:T(8,128)(2,1)S(1)}, bf16[2,16,1152]{2,1,0:T(8,128)(2,1)S(1)}, u32[]{:S(2)}, u32[]{:S(2)}) collective-permute-start(bf16[2,16,1152]{2,1,0:T(8,128)(2,1)S(1)} %get-tuple-element.14), channel_id=1, source_target_pairs={{0,8},{4,12},{8,0},{12,4},{16,24},{20,28},{24,16},{28,20},{1,9},{5... | collective-permute-start | bytes 221192 | tf_op jit(solution)/shard_map/ppermute | solution.py:200
  18.3 0.6 %collective-permute-start.1 = (bf16[2,16,1152]{2,1,0:T(8,128)(2,1)S(1)}, bf16[2,16,1152]{2,1,0:T(8,128)(2,1)S(1)}, u32[]{:S(2)}, u32[]{:S(2)}) collective-permute-start(bf16[2,16,1152]{2,1,0:T(8,128)(2,1)S(1)} %get-tuple-element.15), channel_id=1, source_target_pairs={{0,16},{4,20},{8,24},{12,28},{16,0},{20,4},{24,8},{28,12},{1,17},{... | collective-permute-start | bytes 221192 | tf_op jit(solution)/shard_map/ppermute | solution.py:200
  18.8 2.4 %collective-permute-start.2 = (bf16[2,16,1152]{2,1,0:T(8,128)(2,1)S(1)}, bf16[2,16,1152]{2,1,0:T(8,128)(2,1)S(1)}, u32[]{:S(2)}, u32[]{:S(2)}) collective-permute-start(bf16[2,16,1152]{2,1,0:T(8,128)(2,1)S(1)} %get-tuple-element.16), channel_id=1, source_target_pairs={{0,24},{4,28},{8,16},{12,20},{16,8},{20,12},{24,0},{28,4},{1,25},{... | collective-permute-start | bytes 221192 | tf_op jit(solution)/shard_map/ppermute | solution.py:200
  21.2 1.3 %collective-permute-done.refs_1_ = bf16[2,16,1152]{2,1,0:T(8,128)(2,1)S(1)} collective-permute-done((bf16[2,16,1152]{2,1,0:T(8,128)(2,1)S(1)}, bf16[2,16,1152]{2,1,0:T(8,128)(2,1)S(1)}, u32[]{:S(2)}, u32[]{:S(2)}) %collective-permute-start) | collective-permute-done | bytes 73760 | tf_op jit(solution)/shard_map/ppermute | solution.py:200
  22.5 1.7 %collective-permute-done.1.refs_2_ = bf16[2,16,1152]{2,1,0:T(8,128)(2,1)S(1)} collective-permute-done((bf16[2,16,1152]{2,1,0:T(8,128)(2,1)S(1)}, bf16[2,16,1152]{2,1,0:T(8,128)(2,1)S(1)}, u32[]{:S(2)}, u32[]{:S(2)}) %collective-permute-start.1) | collective-permute-done | bytes 73760 | tf_op jit(solution)/shard_map/ppermute | solution.py:200
  24.2 0.0 collective-permute-done.2.refs_3_
  24.2 0.0 collective-permute-done.3.refs_6_
  24.2 0.7 %shard_map.80 = (bf16[8,1152]{1,0:T(8,128)(2,1)S(1)}, bf16[8,1152]{1,0:T(8,128)(2,1)S(1)}, bf16[8,1152]{1,0:T(8,128)(2,1)S(1)}, bf16[8,1152]{1,0:T(8,128)(2,1)S(1)}) custom-call(bf16[2,16,1152]{2,1,0:T(8,128)(2,1)S(1)} %get-tuple-element.13.refs_0_, bf16[2,16,1152]{2,1,0:T(8,128)(2,1)S(1)} %collective-permute-done.refs_1_, ...), custom_call_target="tpu_custom_call" | custom-call | tf_op jit(solution)/shard_map/pallas_call | solution.py:22
  25.0 1.5 %collective-permute-start.4 = (bf16[8,1152]{1,0:T(8,128)(2,1)S(1)}, bf16[8,1152]{1,0:T(8,128)(2,1)S(1)}, u32[]{:S(2)}, u32[]{:S(2)}) collective-permute-start(bf16[8,1152]{1,0:T(8,128)(2,1)S(1)} %get-tuple-element.18), channel_id=1, source_target_pairs={{0,8},{4,12},{8,0},{12,4},{16,24},{20,28},{24,16},{28,20},{1,9},{5... | collective-permute-start | bytes 55304 | tf_op jit(solution)/shard_map/ppermute | solution.py:200
  26.5 1.3 %collective-permute-start.5 = (bf16[8,1152]{1,0:T(8,128)(2,1)S(1)}, bf16[8,1152]{1,0:T(8,128)(2,1)S(1)}, u32[]{:S(2)}, u32[]{:S(2)}) collective-permute-start(bf16[8,1152]{1,0:T(8,128)(2,1)S(1)} %get-tuple-element.19), channel_id=1, source_target_pairs={{0,16},{4,20},{8,24},{12,28},{16,0},{20,4},{24,8},{28,12},{1,17},{... | collective-permute-start | bytes 55304 | tf_op jit(solution)/shard_map/ppermute | solution.py:200
  27.8 0.7 %collective-permute-start.6 = (bf16[8,1152]{1,0:T(8,128)(2,1)S(1)}, bf16[8,1152]{1,0:T(8,128)(2,1)S(1)}, u32[]{:S(2)}, u32[]{:S(2)}) collective-permute-start(bf16[8,1152]{1,0:T(8,128)(2,1)S(1)} %get-tuple-element.20), channel_id=1, source_target_pairs={{0,24},{4,28},{8,16},{12,20},{16,8},{20,12},{24,0},{28,4},{1,25},{... | collective-permute-start | bytes 55304 | tf_op jit(solution)/shard_map/ppermute | solution.py:200
  28.5 0.3 collective-permute-done.4.refs_1_
  28.8 1.4 %collective-permute-done.5.refs_2_ = bf16[8,1152]{1,0:T(8,128)(2,1)S(1)} collective-permute-done((bf16[8,1152]{1,0:T(8,128)(2,1)S(1)}, bf16[8,1152]{1,0:T(8,128)(2,1)S(1)}, u32[]{:S(2)}, u32[]{:S(2)}) %collective-permute-start.5) | collective-permute-done | bytes 18464 | tf_op jit(solution)/shard_map/ppermute | solution.py:200
  30.2 2.2 %collective-permute-done.6.refs_3_ = bf16[8,1152]{1,0:T(8,128)(2,1)S(1)} collective-permute-done((bf16[8,1152]{1,0:T(8,128)(2,1)S(1)}, bf16[8,1152]{1,0:T(8,128)(2,1)S(1)}, u32[]{:S(2)}, u32[]{:S(2)}) %collective-permute-start.6) | collective-permute-done | bytes 18464 | tf_op jit(solution)/shard_map/ppermute | solution.py:200
  32.5 0.1 shard_map.81
  32.6 11.3 %all_to_all.11.both_ref = bf16[4,2,8,1152]{3,2,1,0:T(8,128)(2,1)S(1)} all-to-all(bf16[4,2,8,1152]{3,2,1,0:T(8,128)(2,1)S(1)} %get-tuple-element.23), channel_id=1, replica_groups=mesh['grp'=8,'blk'=4] {'blk'}, dimensions={0} | all-to-all | bytes 294912 | tf_op jit(solution)/shard_map/all_to_all | solution.py:196
  43.9 1.3 %shard_map.82 = (f32[8,1152]{1,0:T(8,128)}, f32[8,1152]{1,0:T(8,128)}) custom-call(f32[8,1152]{1,0:T(8,128)S(1)} %get-tuple-element.21.unit_ref, f32[8,128]{1,0:T(8,128)S(1)} %get-tuple-element.22.inverse_ref, bf16[8,1152]{1,0:T(8,128)(2,1)S(1)} %copy-done.2, bf16[4,2,8,1152]{3,2,1,0:T(8,128)(2,1)S(1)} %all_to_all.11.both_ref), custom_call_target="tpu_custom_call" | custom-call | tf_op jit(solution)/shard_map/pallas_call | solution.py:22
  (4 shorter events, 0.0 us)
Async XLA Ops:
  0.6 15.7 %copy-start = (bf16[144,1152]{1,0:T(8,128)(2,1)S(1)}, bf16[144,1152]{1,0:T(8,128)(2,1)}, u32[]{:S(2)}) copy-start(bf16[144,1152]{1,0:T(8,128)(2,1)} %refs_5_.1) | copy-start | bytes 995332
  2.2 14.3 %copy-start.1 = (bf16[8,64,1152]{2,1,0:T(8,128)(2,1)S(1)}, bf16[8,64,1152]{2,1,0:T(8,128)(2,1)}, u32[]{:S(2)}) copy-start(bf16[8,64,1152]{2,1,0:T(8,128)(2,1)} %param.6) | copy-start | bytes 3538948
  16.4 7.9 %collective-permute-start.3 = (bf16[17,16,1296]{2,1,0:T(8,128)(2,1)S(1)}, bf16[17,16,1296]{2,1,0:T(8,128)(2,1)S(1)}, u32[]{:S(2)}, u32[]{:S(2)}) collective-permute-start(bf16[17,16,1296]{2,1,0:T(8,128)(2,1)S(1)} %shard_map.79), channel_id=1, source_target_pairs={{0,4},{4,0},{8,12},{12,8},{16,20},{20,16},{24,28},{28,24},{1,5},{5... | collective-permute-start | bytes 2115080 | tf_op jit(solution)/shard_map/ppermute | solution.py:200
  17.6 14.8 %copy-start.2 = (bf16[8,1152]{1,0:T(8,128)(2,1)S(1)}, bf16[8,1152]{1,0:T(8,128)(2,1)}, u32[]{:S(2)}) copy-start(bf16[8,1152]{1,0:T(8,128)(2,1)} %text_ref.1) | copy-start | bytes 55300
  17.6 4.8 %collective-permute-start = (bf16[2,16,1152]{2,1,0:T(8,128)(2,1)S(1)}, bf16[2,16,1152]{2,1,0:T(8,128)(2,1)S(1)}, u32[]{:S(2)}, u32[]{:S(2)}) collective-permute-start(bf16[2,16,1152]{2,1,0:T(8,128)(2,1)S(1)} %get-tuple-element.14), channel_id=1, source_target_pairs={{0,8},{4,12},{8,0},{12,4},{16,24},{20,28},{24,16},{28,20},{1,9},{5... | collective-permute-start | bytes 221192 | tf_op jit(solution)/shard_map/ppermute | solution.py:200
  18.3 6.0 %collective-permute-start.1 = (bf16[2,16,1152]{2,1,0:T(8,128)(2,1)S(1)}, bf16[2,16,1152]{2,1,0:T(8,128)(2,1)S(1)}, u32[]{:S(2)}, u32[]{:S(2)}) collective-permute-start(bf16[2,16,1152]{2,1,0:T(8,128)(2,1)S(1)} %get-tuple-element.15), channel_id=1, source_target_pairs={{0,16},{4,20},{8,24},{12,28},{16,0},{20,4},{24,8},{28,12},{1,17},{... | collective-permute-start | bytes 221192 | tf_op jit(solution)/shard_map/ppermute | solution.py:200
  18.8 5.4 %collective-permute-start.2 = (bf16[2,16,1152]{2,1,0:T(8,128)(2,1)S(1)}, bf16[2,16,1152]{2,1,0:T(8,128)(2,1)S(1)}, u32[]{:S(2)}, u32[]{:S(2)}) collective-permute-start(bf16[2,16,1152]{2,1,0:T(8,128)(2,1)S(1)} %get-tuple-element.16), channel_id=1, source_target_pairs={{0,24},{4,28},{8,16},{12,20},{16,8},{20,12},{24,0},{28,4},{1,25},{... | collective-permute-start | bytes 221192 | tf_op jit(solution)/shard_map/ppermute | solution.py:200
  25.0 3.9 %collective-permute-start.4 = (bf16[8,1152]{1,0:T(8,128)(2,1)S(1)}, bf16[8,1152]{1,0:T(8,128)(2,1)S(1)}, u32[]{:S(2)}, u32[]{:S(2)}) collective-permute-start(bf16[8,1152]{1,0:T(8,128)(2,1)S(1)} %get-tuple-element.18), channel_id=1, source_target_pairs={{0,8},{4,12},{8,0},{12,4},{16,24},{20,28},{24,16},{28,20},{1,9},{5... | collective-permute-start | bytes 55304 | tf_op jit(solution)/shard_map/ppermute | solution.py:200
  26.5 3.8 %collective-permute-start.5 = (bf16[8,1152]{1,0:T(8,128)(2,1)S(1)}, bf16[8,1152]{1,0:T(8,128)(2,1)S(1)}, u32[]{:S(2)}, u32[]{:S(2)}) collective-permute-start(bf16[8,1152]{1,0:T(8,128)(2,1)S(1)} %get-tuple-element.19), channel_id=1, source_target_pairs={{0,16},{4,20},{8,24},{12,28},{16,0},{20,4},{24,8},{28,12},{1,17},{... | collective-permute-start | bytes 55304 | tf_op jit(solution)/shard_map/ppermute | solution.py:200
  27.8 4.7 %collective-permute-start.6 = (bf16[8,1152]{1,0:T(8,128)(2,1)S(1)}, bf16[8,1152]{1,0:T(8,128)(2,1)S(1)}, u32[]{:S(2)}, u32[]{:S(2)}) collective-permute-start(bf16[8,1152]{1,0:T(8,128)(2,1)S(1)} %get-tuple-element.20), channel_id=1, source_target_pairs={{0,24},{4,28},{8,16},{12,20},{16,8},{20,12},{24,0},{28,4},{1,25},{... | collective-permute-start | bytes 55304 | tf_op jit(solution)/shard_map/ppermute | solution.py:200

commit v2 on v1

v2 whole, which is shorter than its diff:
```python
import functools
import math

import jax
import jax.numpy as jnp
from jax import lax
from jax.experimental import pallas as pl
from jax.experimental.pallas import tpu as pltpu
from jax.sharding import PartitionSpec as P

HEADS = 16
CORES = 2
F32 = jnp.float32
BF16 = jnp.bfloat16


def struct(shape, dtype):
    return jax.ShapeDtypeStruct(shape, dtype)


def call(body, out, *args, scratch=(), space=pltpu.VMEM):
    return pl.pallas_call(
        body,
        out_shape=out,
        in_specs=[pl.BlockSpec(memory_space=space)] * len(args),
        scratch_shapes=scratch,
        compiler_params=pltpu.CompilerParams(vmem_limit_bytes=24 * 2**20),
    )(*args)


def nt(left, right):
    return lax.dot_general(left, right, (((1,), (1,)), ((), ())), preferred_element_type=F32)


def nn(left, right):
    return jnp.dot(left, right, preferred_element_type=F32)


def unit_rows(values):
    inverse = lax.rsqrt(jnp.sum(values * values, axis=1, keepdims=True) + 1e-06)
    return values * inverse, inverse


def chain_back(grad_unit, unit_f, inverse):
    inner = jnp.sum(unit_f * grad_unit, axis=1, keepdims=True)
    return (grad_unit - unit_f * inner) * inverse


def slopes_of(left, right):
    logits = 10.0 * nt(left, right) - 2.0
    row = lax.broadcasted_iota(jnp.int32, logits.shape, 0)
    column = lax.broadcasted_iota(jnp.int32, logits.shape, 1)
    target = jnp.where(row == column, 1.0, 0.0)
    return (jax.nn.sigmoid(logits) - target).astype(BF16)


def split_terms(values):
    high = values.astype(BF16)
    rest = values - high.astype(F32)
    middle = rest.astype(BF16)
    return high, middle, (rest - middle.astype(F32)).astype(BF16)


def chip_and_core():
    place = lax.axis_index("grp")
    return place // CORES, lax.rem(place, CORES)


def prepare_kernel(
    probe_hbm, w_key_hbm, w_value_hbm, keys_ref, table_ref, blocks_ref, probe, w_key, w_value, sems
):
    part, width = w_key.shape
    chips, rows, _ = blocks_ref.shape
    copies = [
        pltpu.make_async_copy(source, target, sems.at[i])
        for i, (source, target) in enumerate(
            [(probe_hbm, probe), (w_key_hbm, w_key), (w_value_hbm, w_value)]
        )
    ]
    for copy in copies:
        copy.start()
    head = lax.broadcasted_iota(jnp.int32, (HEADS, width), 0)
    first = lax.broadcasted_iota(jnp.int32, (HEADS, width), 1) - head * (width // HEADS)
    inside = (first >= 0) & (first < width // HEADS)
    copies[0].wait()
    table = jnp.where(inside, probe[...].astype(F32).reshape(1, width), 0.0).astype(BF16)
    table_ref[...] = table
    copies[1].wait()
    keys_ref[...] = nt(table, w_key[...])
    copies[2].wait()
    wide = width // chips
    for q in range(chips):
        columns = w_value[:, q * wide : (q + 1) * wide]
        pieces = [columns[j * rows : (j + 1) * rows] for j in range(part // rows)]
        blocks_ref[q] = jnp.concatenate(pieces, axis=1)


def keys_kernel(keys_ref, table_ref, blocks_ref, other_ref, *out_refs):
    _, rows, packed = blocks_ref.shape
    chip, core = chip_and_core()
    own, other = keys_ref[...], nt(table_ref[...], other_ref[...])
    keys = [jnp.where(core == 0, own, other), jnp.where(core == 0, other, own)]
    keys = [
        term[h * rows : (h + 1) * rows]
        for term in split_terms(jnp.concatenate(keys, axis=1))
        for h in range(HEADS // rows)
    ]
    keys = jnp.concatenate(keys, axis=1)
    for m, out_ref in enumerate(out_refs):
        out_ref[:, :packed] = blocks_ref[chip ^ m]
        out_ref[:, packed:] = keys


def shard_kernel(chips, *refs):
    w_out_ref, out_ref = refs[chips:]
    _, rows, length = out_ref.shape
    part, width = w_out_ref.shape
    for m in range(chips):
        out_ref[m] = refs[m][:, :length]
    fit = length // width
    for j in range(part // rows):
        first = j % fit * width
        out_ref[chips + j // fit, :, first : first + width] = w_out_ref[j * rows : (j + 1) * rows]


def attend_kernel(images, scaling, chips, x_ref, *refs):
    parts, outs, (placed, table, every) = refs[:chips], refs[chips:-3], refs[-3:]
    x = x_ref[...]
    width = x.shape[1]
    patches = x.shape[0] // images
    rows, length = parts[0].shape
    wide = width // chips
    pieces = table.shape[0] // rows
    chip, _ = chip_and_core()
    for m in range(chips):
        placed[chip ^ m] = parts[m][:, length - pieces * wide :]
    for j in range(pieces):
        for q in range(chips):
            table[j * rows : (j + 1) * rows, q * wide : (q + 1) * wide] = placed[
                q, :, j * wide : (j + 1) * wide
            ]
    parts = nt(table[...], x)
    scores = (parts[:HEADS] + parts[HEADS : 2 * HEADS] + parts[2 * HEADS :]) * scaling
    image = lax.broadcasted_iota(jnp.int32, (images, x.shape[0]), 0)
    first = lax.broadcasted_iota(jnp.int32, (images, x.shape[0]), 1) - image * patches
    own = (first >= 0) & (first < patches)
    spread = jnp.where(own[None], scores[:, None, :], -jnp.inf)
    expo = jnp.exp(spread - jnp.max(spread, axis=2, keepdims=True))
    weights = expo / jnp.sum(expo, axis=2, keepdims=True)
    weights = weights.reshape(HEADS * images, x.shape[0])
    high = weights.astype(BF16)
    low = (weights - high.astype(F32)).astype(BF16)
    mixed = nn(jnp.concatenate([high, low], axis=0), x)
    mixed = (mixed[: HEADS * images] + mixed[HEADS * images :]).astype(BF16)
    every[...] = mixed.reshape(every.shape)
    for m, out_ref in enumerate(outs):
        out_ref[...] = every[chip ^ m]


def project_kernel(images, chips, *refs):
    mixed_refs, parts = refs[:chips], refs[chips : 2 * chips]
    w_out_ref, other_ref = refs[2 * chips : 2 * chips + 2]
    out_refs, w_value = refs[2 * chips + 2 : -1], refs[-1]
    _, rows, width = mixed_refs[0].shape
    part = w_out_ref.shape[0]
    heads = rows // images
    chip, core = chip_and_core()
    for m in range(chips):
        for c, source in enumerate((parts[m], other_ref.at[m])):
            place = core if c == 0 else 1 - core
            for t in range(CORES):
                for j in range(part // rows):
                    first = (j * CORES + t) * part
                    w_value[t, chip ^ m, place, j * rows : (j + 1) * rows] = source[
                        :, first : first + part
                    ]
    fit = other_ref.shape[2] // width
    outs = [
        other_ref[chips + j // fit, :, j % fit * width : (j % fit + 1) * width]
        for j in range(part // rows)
    ]
    head = lax.broadcasted_iota(jnp.int32, (chips, images, part), 2)
    embed = jnp.zeros((chips * images, width), F32)
    for shard, rows_out in ((core, w_out_ref[...]), (1 - core, jnp.concatenate(outs, axis=0))):
        mixed = jnp.concatenate([ref[shard] for ref in mixed_refs], axis=0)
        columns = w_value[shard].reshape(width, part)
        every = nn(mixed, columns).reshape(chips, heads, images, part)
        pooled = every[:, 0]
        for h in range(1, heads):
            pooled = jnp.where(head >= h * (part // heads), every[:, h], pooled)
        pooled = pooled.reshape(chips * images, part).astype(BF16)
        embed = embed + nn(pooled, rows_out)
    for m, out_ref in enumerate(out_refs):
        out_ref[...] = embed[m * images : (m + 1) * images].astype(BF16)


def unit_text_kernel(blocks, *refs):
    words_ref, unit_ref, inverse_ref = refs[blocks:]
    images = unit_ref.shape[0]
    texts = jnp.concatenate([ref[...].astype(F32) for ref in refs[:blocks]], axis=0)
    units, inverses = unit_rows(texts)
    words_ref[...] = units.astype(BF16)
    unit_ref[...] = units[:images]
    inverse_ref[...] = jnp.broadcast_to(inverses[:images], inverse_ref.shape)


def unit_image_kernel(chips, *refs):
    unit_ref, inverse_ref, rounded_ref = refs[chips + 1 :]
    embed = refs[0][...].astype(F32)
    for ref in refs[1:chips]:
        embed = embed + ref[...].astype(F32)
    unit, inverse = unit_rows(embed)
    unit_ref[...] = unit
    inverse_ref[...] = jnp.broadcast_to(inverse, inverse_ref.shape)
    rounded_ref[...] = unit.astype(BF16)


def grad_kernel(unit_ref, inverse_ref, *refs):
    others = [ref[...].astype(F32) for ref in refs[:-1]]
    others = jnp.concatenate(others, axis=0).astype(BF16)
    unit = unit_ref[...]
    slopes = slopes_of(unit.astype(BF16), others)
    refs[-1][...] = chain_back(10.0 * nn(slopes, others), unit, inverse_ref[:, :1])


def exchange(array, devices, flip, axis="grp"):
    return lax.ppermute(array, axis, [(i, i ^ flip) for i in range(devices)])


def all_blocks(array, blocks):
    return [array] + [
        lax.ppermute(array, "blk", [(i, (i + by) % blocks) for i in range(blocks)])
        for by in range(1, blocks)
    ]


def exchange_chips(arrays, devices):
    return [array if m == 0 else exchange(array, devices, m * CORES) for m, array in enumerate(arrays)]


def local(patches, probe, w_key, w_value, w_out, texts):
    images, patch_count, width = patches.shape
    devices = lax.axis_size("grp")
    blocks = lax.axis_size("blk")
    part = w_key.shape[0]
    heads = HEADS // devices
    scaling = 1.0 / math.sqrt(width // HEADS)
    flat = patches.reshape(images * patch_count, width)

    rows = heads * images
    chips = devices // CORES
    wide = CORES * part
    packed = part // rows * wide
    fit = packed // width

    keys, table, columns = call(
        prepare_kernel,
        (
            struct((HEADS, part), F32),
            struct((HEADS, width), BF16),
            struct((chips, rows, packed), BF16),
        ),
        *[pltpu.with_memory_space_constraint(a, pltpu.HBM) for a in (probe, w_key, w_value)],
        scratch=[
            pltpu.VMEM(probe.shape, BF16),
            pltpu.VMEM(w_key.shape, BF16),
            pltpu.VMEM(w_value.shape, BF16),
            pltpu.SemaphoreType.DMA((3,)),
        ],
        space=pltpu.HBM,
    )
    parts = call(
        keys_kernel,
        [struct((rows, packed + 3 * HEADS // rows * wide), BF16)] * chips,
        keys,
        table,
        columns,
        exchange(w_key, devices, 1),
    )
    parts = exchange_chips(parts, devices)
    shard = call(
        functools.partial(shard_kernel, chips),
        struct((chips + pl.cdiv(part // rows, fit), rows, packed), BF16),
        *parts,
        w_out,
    )
    other = exchange(shard, devices, 1)
    mixed = call(
        functools.partial(attend_kernel, images, scaling, chips),
        [struct((CORES, rows, width), BF16)] * chips,
        flat,
        *parts,
        scratch=[
            pltpu.VMEM((chips, rows, 3 * HEADS // rows * wide), BF16),
            pltpu.VMEM((3 * HEADS, width), BF16),
            pltpu.VMEM((chips, CORES, rows, width), BF16),
        ],
    )
    partial_embed = call(
        functools.partial(project_kernel, images, chips),
        [struct((images, width), BF16)] * chips,
        *exchange_chips(mixed, devices),
        *parts,
        w_out,
        other,
        scratch=[pltpu.VMEM((CORES, chips, CORES, part, part), BF16)],
    )
    row, column = struct((images, width), F32), struct((images, 128), F32)
    words, unit_text, inverse_text = call(
        functools.partial(unit_text_kernel, blocks),
        (struct((blocks * images, width), BF16), row, column),
        *all_blocks(texts, blocks),
    )
    unit, inverse, rounded = call(
        functools.partial(unit_image_kernel, chips),
        (row, column, struct((images, width), BF16)),
        *exchange_chips(partial_embed, devices),
        inverse_text,
    )
    all_images = [rounded] + [exchange(rounded, blocks, m, "blk") for m in range(1, blocks)]
    grad_image = call(grad_kernel, row, unit, inverse, words)
    grad_text = call(grad_kernel, row, unit_text, inverse_text, *all_images)
    return grad_image, grad_text


def solution(mesh):
    in_specs = (
        P(("grp", "blk"), None, None),
        P(),
        P("grp", None),
        P("grp", None),
        P("grp", None),
        P(("grp", "blk"), None),
    )
    out_specs = (P(("grp", "blk"), None), P(("grp", "blk"), None))
    return jax.shard_map(local, mesh=mesh, in_specs=in_specs, out_specs=out_specs, check_vma=False)
```

time: 45.4 us -> 40.3 us (0.89)
  blocking collectives: 25.5 us -> 0 us
  starting transfers between devices: 7.18 us -> 22.8 us
  waiting for transfers between devices: 6.99 us -> 10.5 us
  Pallas kernels: 4.83 us -> 6.14 us
    all_to_all x2 -> x0, blocking collectives: 25.5 us -> none  [swap(): return lax.all_to_all(array, axis, 0, 0, tiled=True)]
    ppermute x7 -> x17, starting transfers between devices: 7.18 us -> 22.8 us  [the longest x14 16.9 us: exchange(): return lax.ppermute(array, axis, [(i, i ^ flip) for i in range(devices)])]
    ppermute x7 -> x17, waiting for transfers between devices: 6.99 us -> 10.5 us  [the longest x14 10.5 us: exchange(): return lax.ppermute(array, axis, [(i, i ^ flip) for i in range(devices)])]
    pallas_call x6 -> x9, Pallas kernels: 4.83 us -> 6.14 us  [call(): pl.pallas_call(body, out_shape=out, in_specs=[pl.BlockSpec(memory_space=s...]
  transfers between devices with their start and end apart: 7 -> 17, of which waited for: 5 -> 6; matrix products, arithmetic and copies ran while one was open for 0% -> 0% of each run, Pallas kernels for 3% -> 11%
where the time goes in v2:
time: 40.3 us; the launch traced here: 40.1 us
  starting transfers between devices  22.8 us (57%)
  waiting for transfers between devices  10.5 us (26%)
  Pallas kernels  6.14 us (15%)
  between operations  0.72 us (2%)
    ppermute x14, starting transfers between devices, exchange(): return lax.ppermute(array, axis, [(i, i ^ flip) for i in range(devices)])  16.9 us
    ppermute x14, waiting for transfers between devices, exchange(): return lax.ppermute(array, axis, [(i, i ^ flip) for i in range(devices)])  10.5 us
    pallas_call x9, Pallas kernels, call(): pl.pallas_call(body, out_shape=out, in_specs=[pl.BlockSpec(memory_space=s...  6.14 us
    ppermute x3, starting transfers between devices, all_blocks(): lax.ppermute(array, 'blk', [(i, (i + by) % blocks) for i in range(blocks)])  5.86 us
  transfers between devices with their start and end apart: 17, of which 6 were waited for; matrix products, arithmetic and copies ran while one was open for 0% of the time, Pallas kernels for 11%

profile of v2, /device:TPU:0, one launch (start us, length us, event | category | flops | bytes accessed | tf_op | source)
XLA Modules:
  0.0 40.1 jit_solution(15437290319704846575)
XLA Ops:
  0.6 0.5 %collective-permute-start = (bf16[144,1152]{1,0:T(8,128)(2,1)}, bf16[144,1152]{1,0:T(8,128)(2,1)S(1)}, u32[]{:S(2)}, u32[]{:S(2)}) collective-permute-start(bf16[144,1152]{1,0:T(8,128)(2,1)} %w_key_hbm.1), channel_id=1, source_target_pairs={{0,4},{4,0},{8,12},{12,8},{16,20},{20,16},{24,28},{28,24},{1,5},{5... | collective-permute-start | bytes 995336 | tf_op jit(solution)/shard_map/ppermute | solution.py:227
  1.2 1.4 %shard_map.77 = (f32[16,144]{1,0:T(8,128)S(1)}, bf16[16,1152]{1,0:T(8,128)(2,1)S(1)}, bf16[4,16,2592]{2,1,0:T(8,128)(2,1)S(1)}) custom-call(bf16[1152]{0:T(1024)(128)(2,1)} %probe_hbm.1, bf16[144,1152]{1,0:T(8,128)(2,1)} %w_key_hbm.1, bf16[144,1152]{1,0:T(8,128)(2,1)} %w_value_hbm.1), custom_call_target="tpu_custom_call" | custom-call | tf_op jit(solution)/shard_map/pallas_call | solution.py:22
  3.1 2.9 %collective-permute-start.1 = (bf16[16,3456]{1,0:T(8,128)(2,1)S(1)}, bf16[16,3456]{1,0:T(8,128)(2,1)S(1)}, u32[]{:S(2)}, u32[]{:S(2)}) collective-permute-start(bf16[16,3456]{1,0:T(8,128)(2,1)S(1)} %get-tuple-element.27), channel_id=1, source_target_pairs={{0,8},{4,12},{8,0},{12,4},{16,24},{20,28},{24,16},{28,20},{1,9},{5... | collective-permute-start | bytes 331784 | tf_op jit(solution)/shard_map/ppermute | solution.py:227
  6.0 1.5 %collective-permute-start.2 = (bf16[16,3456]{1,0:T(8,128)(2,1)S(1)}, bf16[16,3456]{1,0:T(8,128)(2,1)S(1)}, u32[]{:S(2)}, u32[]{:S(2)}) collective-permute-start(bf16[16,3456]{1,0:T(8,128)(2,1)S(1)} %get-tuple-element.28), channel_id=1, source_target_pairs={{0,16},{4,20},{8,24},{12,28},{16,0},{20,4},{24,8},{28,12},{1,17},{... | collective-permute-start | bytes 331784 | tf_op jit(solution)/shard_map/ppermute | solution.py:227
  7.5 1.9 %collective-permute-done.1.refs_1_.refs_5_ = bf16[16,3456]{1,0:T(8,128)(2,1)S(1)} collective-permute-done((bf16[16,3456]{1,0:T(8,128)(2,1)S(1)}, bf16[16,3456]{1,0:T(8,128)(2,1)S(1)}, u32[]{:S(2)}, u32[]{:S(2)}) %collective-permute-start.1) | collective-permute-done | bytes 110624 | tf_op jit(solution)/shard_map/ppermute | solution.py:227
  9.4 2.8 %collective-permute-done.2.refs_2_.refs_6_ = bf16[16,3456]{1,0:T(8,128)(2,1)S(1)} collective-permute-done((bf16[16,3456]{1,0:T(8,128)(2,1)S(1)}, bf16[16,3456]{1,0:T(8,128)(2,1)S(1)}, u32[]{:S(2)}, u32[]{:S(2)}) %collective-permute-start.2) | collective-permute-done | bytes 110624 | tf_op jit(solution)/shard_map/ppermute | solution.py:227
  12.2 1.0 %collective-permute-done.3.refs_3_.refs_7_ = bf16[16,3456]{1,0:T(8,128)(2,1)S(1)} collective-permute-done((bf16[16,3456]{1,0:T(8,128)(2,1)S(1)}, bf16[16,3456]{1,0:T(8,128)(2,1)S(1)}, u32[]{:S(2)}, u32[]{:S(2)}) %collective-permute-start.3) | collective-permute-done | bytes 110624 | tf_op jit(solution)/shard_map/ppermute | solution.py:227
  13.4 1.2 %shard_map.79 = (bf16[2,16,1152]{2,1,0:T(8,128)(2,1)S(1)}, bf16[2,16,1152]{2,1,0:T(8,128)(2,1)S(1)}, bf16[2,16,1152]{2,1,0:T(8,128)(2,1)S(1)}, bf16[2,16,1152]{2,1,0:T(8,128)(2,1)S(1)}) custom-call(bf16[512,1152]{1,0:T(8,128)(2,1)S(1)} %bitcast.1, bf16[16,3456]{1,0:T(8,128)(2,1)S(1)} %get-tuple-element.26.refs_0_.refs_4_, ...), custom_call_target="tpu_custom_call" | custom-call | tf_op jit(solution)/shard_map/pallas_call | solution.py:22
  14.6 1.3 %collective-permute-start.4 = (bf16[2,16,1152]{2,1,0:T(8,128)(2,1)S(1)}, bf16[2,16,1152]{2,1,0:T(8,128)(2,1)S(1)}, u32[]{:S(2)}, u32[]{:S(2)}) collective-permute-start(bf16[2,16,1152]{2,1,0:T(8,128)(2,1)S(1)} %get-tuple-element.31), channel_id=1, source_target_pairs={{0,8},{4,12},{8,0},{12,4},{16,24},{20,28},{24,16},{28,20},{1,9},{5... | collective-permute-start | bytes 221192 | tf_op jit(solution)/shard_map/ppermute | solution.py:227
  15.9 0.8 %collective-permute-start.5 = (bf16[2,16,1152]{2,1,0:T(8,128)(2,1)S(1)}, bf16[2,16,1152]{2,1,0:T(8,128)(2,1)S(1)}, u32[]{:S(2)}, u32[]{:S(2)}) collective-permute-start(bf16[2,16,1152]{2,1,0:T(8,128)(2,1)S(1)} %get-tuple-element.32), channel_id=1, source_target_pairs={{0,16},{4,20},{8,24},{12,28},{16,0},{20,4},{24,8},{28,12},{1,17},{... | collective-permute-start | bytes 221192 | tf_op jit(solution)/shard_map/ppermute | solution.py:227
  16.7 1.4 %collective-permute-start.6 = (bf16[2,16,1152]{2,1,0:T(8,128)(2,1)S(1)}, bf16[2,16,1152]{2,1,0:T(8,128)(2,1)S(1)}, u32[]{:S(2)}, u32[]{:S(2)}) collective-permute-start(bf16[2,16,1152]{2,1,0:T(8,128)(2,1)S(1)} %get-tuple-element.33), channel_id=1, source_target_pairs={{0,24},{4,28},{8,16},{12,20},{16,8},{20,12},{24,0},{28,4},{1,25},{... | collective-permute-start | bytes 221192 | tf_op jit(solution)/shard_map/ppermute | solution.py:227
  18.1 1.6 %collective-permute-start.11 = (bf16[8,1152]{1,0:T(8,128)(2,1)S(1)}, bf16[8,1152]{1,0:T(8,128)(2,1)S(1)}, u32[]{:S(2)}, u32[]{:S(2)}) collective-permute-start(bf16[8,1152]{1,0:T(8,128)(2,1)S(1)} %copy-done.2), channel_id=1, source_target_pairs={{0,1},{1,2},{2,3},{3,0},{4,5},{5,6},{6,7},{7,4},{8,9},{9,10},{10,1... | collective-permute-start | bytes 55304 | tf_op jit(solution)/shard_map/ppermute | solution.py:232
  19.7 2.6 %collective-permute-start.12 = (bf16[8,1152]{1,0:T(8,128)(2,1)S(1)}, bf16[8,1152]{1,0:T(8,128)(2,1)S(1)}, u32[]{:S(2)}, u32[]{:S(2)}) collective-permute-start(bf16[8,1152]{1,0:T(8,128)(2,1)S(1)} %copy-done.2), channel_id=1, source_target_pairs={{0,2},{1,3},{2,0},{3,1},{4,6},{5,7},{6,4},{7,5},{8,10},{9,11},{10,... | collective-permute-start | bytes 55304 | tf_op jit(solution)/shard_map/ppermute | solution.py:232
  22.3 1.7 %collective-permute-start.13 = (bf16[8,1152]{1,0:T(8,128)(2,1)S(1)}, bf16[8,1152]{1,0:T(8,128)(2,1)S(1)}, u32[]{:S(2)}, u32[]{:S(2)}) collective-permute-start(bf16[8,1152]{1,0:T(8,128)(2,1)S(1)} %copy-done.2), channel_id=1, source_target_pairs={{0,3},{1,0},{2,1},{3,2},{4,7},{5,4},{6,5},{7,6},{8,11},{9,8},{10,9... | collective-permute-start | bytes 55304 | tf_op jit(solution)/shard_map/ppermute | solution.py:232
  24.0 0.8 %shard_map.81 = (bf16[8,1152]{1,0:T(8,128)(2,1)S(1)}, bf16[8,1152]{1,0:T(8,128)(2,1)S(1)}, bf16[8,1152]{1,0:T(8,128)(2,1)S(1)}, bf16[8,1152]{1,0:T(8,128)(2,1)S(1)}) custom-call(bf16[2,16,1152]{2,1,0:T(8,128)(2,1)S(1)} %get-tuple-element.30.refs_0_, bf16[2,16,1152]{2,1,0:T(8,128)(2,1)S(1)} %collective-permute-done.4.refs_1_, ...), custom_call_target="tpu_custom_call" | custom-call | tf_op jit(solution)/shard_map/pallas_call | solution.py:22
  24.8 3.3 %collective-permute-start.10 = (bf16[8,1152]{1,0:T(8,128)(2,1)S(1)}, bf16[8,1152]{1,0:T(8,128)(2,1)S(1)}, u32[]{:S(2)}, u32[]{:S(2)}) collective-permute-start(bf16[8,1152]{1,0:T(8,128)(2,1)S(1)} %get-tuple-element.37), channel_id=1, source_target_pairs={{0,24},{4,28},{8,16},{12,20},{16,8},{20,12},{24,0},{28,4},{1,25},{... | collective-permute-start | bytes 55304 | tf_op jit(solution)/shard_map/ppermute | solution.py:227
  28.1 0.6 %collective-permute-start.9 = (bf16[8,1152]{1,0:T(8,128)(2,1)S(1)}, bf16[8,1152]{1,0:T(8,128)(2,1)S(1)}, u32[]{:S(2)}, u32[]{:S(2)}) collective-permute-start(bf16[8,1152]{1,0:T(8,128)(2,1)S(1)} %get-tuple-element.36), channel_id=1, source_target_pairs={{0,16},{4,20},{8,24},{12,28},{16,0},{20,4},{24,8},{28,12},{1,17},{... | collective-permute-start | bytes 55304 | tf_op jit(solution)/shard_map/ppermute | solution.py:227
  28.9 1.0 %collective-permute-done.10.refs_3_ = bf16[8,1152]{1,0:T(8,128)(2,1)S(1)} collective-permute-done((bf16[8,1152]{1,0:T(8,128)(2,1)S(1)}, bf16[8,1152]{1,0:T(8,128)(2,1)S(1)}, u32[]{:S(2)}, u32[]{:S(2)}) %collective-permute-start.10) | collective-permute-done | bytes 18464 | tf_op jit(solution)/shard_map/ppermute | solution.py:227
  29.8 2.0 %collective-permute-done.8.refs_1_ = bf16[8,1152]{1,0:T(8,128)(2,1)S(1)} collective-permute-done((bf16[8,1152]{1,0:T(8,128)(2,1)S(1)}, bf16[8,1152]{1,0:T(8,128)(2,1)S(1)}, u32[]{:S(2)}, u32[]{:S(2)}) %collective-permute-start.8) | collective-permute-done | bytes 18464 | tf_op jit(solution)/shard_map/ppermute | solution.py:227
  32.1 1.5 %collective-permute-start.15 = (bf16[8,1152]{1,0:T(8,128)(2,1)S(1)}, bf16[8,1152]{1,0:T(8,128)(2,1)S(1)}, u32[]{:S(2)}, u32[]{:S(2)}) collective-permute-start(bf16[8,1152]{1,0:T(8,128)(2,1)S(1)} %get-tuple-element.43.refs_0_), channel_id=1, source_target_pairs={{0,2},{1,3},{2,0},{3,1},{4,6},{5,7},{6,4},{7,5},{8,10},{9,11},{10,... | collective-permute-start | bytes 55304 | tf_op jit(solution)/shard_map/ppermute | solution.py:227
  33.6 2.8 %collective-permute-start.16 = (bf16[8,1152]{1,0:T(8,128)(2,1)S(1)}, bf16[8,1152]{1,0:T(8,128)(2,1)S(1)}, u32[]{:S(2)}, u32[]{:S(2)}) collective-permute-start(bf16[8,1152]{1,0:T(8,128)(2,1)S(1)} %get-tuple-element.43.refs_0_), channel_id=1, source_target_pairs={{0,3},{1,2},{2,1},{3,0},{4,7},{5,6},{6,5},{7,4},{8,11},{9,10},{10,... | collective-permute-start | bytes 55304 | tf_op jit(solution)/shard_map/ppermute | solution.py:227
  36.4 1.0 %shard_map.84 = f32[8,1152]{1,0:T(8,128)} custom-call(f32[8,1152]{1,0:T(8,128)S(1)} %get-tuple-element.39.unit_ref, f32[8,128]{1,0:T(8,128)S(1)} %get-tuple-element.40.inverse_ref, bf16[32,1152]{1,0:T(8,128)(2,1)S(1)} %get-tuple-element.41.refs_0_), custom_call_target="tpu_custom_call" | custom-call | tf_op jit(solution)/shard_map/pallas_call | solution.py:22
  37.4 1.8 %collective-permute-done.16.refs_3_ = bf16[8,1152]{1,0:T(8,128)(2,1)S(1)} collective-permute-done((bf16[8,1152]{1,0:T(8,128)(2,1)S(1)}, bf16[8,1152]{1,0:T(8,128)(2,1)S(1)}, u32[]{:S(2)}, u32[]{:S(2)}) %collective-permute-start.16) | collective-permute-done | bytes 18464 | tf_op jit(solution)/shard_map/ppermute | solution.py:227
  39.1 1.0 %shard_map.85 = f32[8,1152]{1,0:T(8,128)} custom-call(f32[8,1152]{1,0:T(8,128)S(1)} %get-tuple-element.42.unit_ref, f32[8,128]{1,0:T(8,128)S(1)} %get-tuple-element.38.refs_4_.inverse_ref, bf16[8,1152]{1,0:T(8,128)(2,1)S(1)} %get-tuple-element.43.refs_0_, bf16[8,1152]{1,0:T(8,128)(2,1)S(1)} %collective-permute-done.14.refs_1_, ...), custom_call_target="tpu_custom_call" | custom-call | tf_op jit(solution)/shard_map/pallas_call | solution.py:22
  (25 shorter events, 1.0 us)
Async XLA Ops:
  0.6 12.6 %copy-start = (bf16[144,1152]{1,0:T(8,128)(2,1)S(1)}, bf16[144,1152]{1,0:T(8,128)(2,1)}, u32[]{:S(2)}) copy-start(bf16[144,1152]{1,0:T(8,128)(2,1)} %refs_8_.1) | copy-start | bytes 995332
  0.6 2.0 %collective-permute-start = (bf16[144,1152]{1,0:T(8,128)(2,1)}, bf16[144,1152]{1,0:T(8,128)(2,1)S(1)}, u32[]{:S(2)}, u32[]{:S(2)}) collective-permute-start(bf16[144,1152]{1,0:T(8,128)(2,1)} %w_key_hbm.1), channel_id=1, source_target_pairs={{0,4},{4,0},{8,12},{12,8},{16,20},{20,16},{24,28},{28,24},{1,5},{5... | collective-permute-start | bytes 995336 | tf_op jit(solution)/shard_map/ppermute | solution.py:227
  2.6 10.8 %copy-start.1 = (bf16[8,64,1152]{2,1,0:T(8,128)(2,1)S(1)}, bf16[8,64,1152]{2,1,0:T(8,128)(2,1)}, u32[]{:S(2)}) copy-start(bf16[8,64,1152]{2,1,0:T(8,128)(2,1)} %param.6) | copy-start | bytes 3538948
  3.1 6.3 %collective-permute-start.1 = (bf16[16,3456]{1,0:T(8,128)(2,1)S(1)}, bf16[16,3456]{1,0:T(8,128)(2,1)S(1)}, u32[]{:S(2)}, u32[]{:S(2)}) collective-permute-start(bf16[16,3456]{1,0:T(8,128)(2,1)S(1)} %get-tuple-element.27), channel_id=1, source_target_pairs={{0,8},{4,12},{8,0},{12,4},{16,24},{20,28},{24,16},{28,20},{1,9},{5... | collective-permute-start | bytes 331784 | tf_op jit(solution)/shard_map/ppermute | solution.py:227
  6.0 6.2 %collective-permute-start.2 = (bf16[16,3456]{1,0:T(8,128)(2,1)S(1)}, bf16[16,3456]{1,0:T(8,128)(2,1)S(1)}, u32[]{:S(2)}, u32[]{:S(2)}) collective-permute-start(bf16[16,3456]{1,0:T(8,128)(2,1)S(1)} %get-tuple-element.28), channel_id=1, source_target_pairs={{0,16},{4,20},{8,24},{12,28},{16,0},{20,4},{24,8},{28,12},{1,17},{... | collective-permute-start | bytes 331784 | tf_op jit(solution)/shard_map/ppermute | solution.py:227
  7.5 5.7 %collective-permute-start.3 = (bf16[16,3456]{1,0:T(8,128)(2,1)S(1)}, bf16[16,3456]{1,0:T(8,128)(2,1)S(1)}, u32[]{:S(2)}, u32[]{:S(2)}) collective-permute-start(bf16[16,3456]{1,0:T(8,128)(2,1)S(1)} %get-tuple-element.29), channel_id=1, source_target_pairs={{0,24},{4,28},{8,16},{12,20},{16,8},{20,12},{24,0},{28,4},{1,25},{... | collective-permute-start | bytes 331784 | tf_op jit(solution)/shard_map/ppermute | solution.py:227
  13.3 4.9 %copy-start.2 = (bf16[8,1152]{1,0:T(8,128)(2,1)S(1)}, bf16[8,1152]{1,0:T(8,128)(2,1)}, u32[]{:S(2)}) copy-start(bf16[8,1152]{1,0:T(8,128)(2,1)} %refs_0_.1) | copy-start | bytes 55300
  13.3 10.7 %collective-permute-start.7 = (bf16[9,16,2592]{2,1,0:T(8,128)(2,1)S(1)}, bf16[9,16,2592]{2,1,0:T(8,128)(2,1)S(1)}, u32[]{:S(2)}, u32[]{:S(2)}) collective-permute-start(bf16[9,16,2592]{2,1,0:T(8,128)(2,1)S(1)} %shard_map.80), channel_id=1, source_target_pairs={{0,4},{4,0},{8,12},{12,8},{16,20},{20,16},{24,28},{28,24},{1,5},{5... | collective-permute-start | bytes 2239496 | tf_op jit(solution)/shard_map/ppermute | solution.py:227
  14.6 5.1 %collective-permute-start.4 = (bf16[2,16,1152]{2,1,0:T(8,128)(2,1)S(1)}, bf16[2,16,1152]{2,1,0:T(8,128)(2,1)S(1)}, u32[]{:S(2)}, u32[]{:S(2)}) collective-permute-start(bf16[2,16,1152]{2,1,0:T(8,128)(2,1)S(1)} %get-tuple-element.31), channel_id=1, source_target_pairs={{0,8},{4,12},{8,0},{12,4},{16,24},{20,28},{24,16},{28,20},{1,9},{5... | collective-permute-start | bytes 221192 | tf_op jit(solution)/shard_map/ppermute | solution.py:227
  15.9 6.4 %collective-permute-start.5 = (bf16[2,16,1152]{2,1,0:T(8,128)(2,1)S(1)}, bf16[2,16,1152]{2,1,0:T(8,128)(2,1)S(1)}, u32[]{:S(2)}, u32[]{:S(2)}) collective-permute-start(bf16[2,16,1152]{2,1,0:T(8,128)(2,1)S(1)} %get-tuple-element.32), channel_id=1, source_target_pairs={{0,16},{4,20},{8,24},{12,28},{16,0},{20,4},{24,8},{28,12},{1,17},{... | collective-permute-start | bytes 221192 | tf_op jit(solution)/shard_map/ppermute | solution.py:227
  16.7 7.3 %collective-permute-start.6 = (bf16[2,16,1152]{2,1,0:T(8,128)(2,1)S(1)}, bf16[2,16,1152]{2,1,0:T(8,128)(2,1)S(1)}, u32[]{:S(2)}, u32[]{:S(2)}) collective-permute-start(bf16[2,16,1152]{2,1,0:T(8,128)(2,1)S(1)} %get-tuple-element.33), channel_id=1, source_target_pairs={{0,24},{4,28},{8,16},{12,20},{16,8},{20,12},{24,0},{28,4},{1,25},{... | collective-permute-start | bytes 221192 | tf_op jit(solution)/shard_map/ppermute | solution.py:227
  18.1 10.0 %collective-permute-start.11 = (bf16[8,1152]{1,0:T(8,128)(2,1)S(1)}, bf16[8,1152]{1,0:T(8,128)(2,1)S(1)}, u32[]{:S(2)}, u32[]{:S(2)}) collective-permute-start(bf16[8,1152]{1,0:T(8,128)(2,1)S(1)} %copy-done.2), channel_id=1, source_target_pairs={{0,1},{1,2},{2,3},{3,0},{4,5},{5,6},{6,7},{7,4},{8,9},{9,10},{10,1... | collective-permute-start | bytes 55304 | tf_op jit(solution)/shard_map/ppermute | solution.py:232
  19.7 9.0 %collective-permute-start.12 = (bf16[8,1152]{1,0:T(8,128)(2,1)S(1)}, bf16[8,1152]{1,0:T(8,128)(2,1)S(1)}, u32[]{:S(2)}, u32[]{:S(2)}) collective-permute-start(bf16[8,1152]{1,0:T(8,128)(2,1)S(1)} %copy-done.2), channel_id=1, source_target_pairs={{0,2},{1,3},{2,0},{3,1},{4,6},{5,7},{6,4},{7,5},{8,10},{9,11},{10,... | collective-permute-start | bytes 55304 | tf_op jit(solution)/shard_map/ppermute | solution.py:232
  22.3 6.5 %collective-permute-start.13 = (bf16[8,1152]{1,0:T(8,128)(2,1)S(1)}, bf16[8,1152]{1,0:T(8,128)(2,1)S(1)}, u32[]{:S(2)}, u32[]{:S(2)}) collective-permute-start(bf16[8,1152]{1,0:T(8,128)(2,1)S(1)} %copy-done.2), channel_id=1, source_target_pairs={{0,3},{1,0},{2,1},{3,2},{4,7},{5,4},{6,5},{7,6},{8,11},{9,8},{10,9... | collective-permute-start | bytes 55304 | tf_op jit(solution)/shard_map/ppermute | solution.py:232
  24.8 5.0 %collective-permute-start.10 = (bf16[8,1152]{1,0:T(8,128)(2,1)S(1)}, bf16[8,1152]{1,0:T(8,128)(2,1)S(1)}, u32[]{:S(2)}, u32[]{:S(2)}) collective-permute-start(bf16[8,1152]{1,0:T(8,128)(2,1)S(1)} %get-tuple-element.37), channel_id=1, source_target_pairs={{0,24},{4,28},{8,16},{12,20},{16,8},{20,12},{24,0},{28,4},{1,25},{... | collective-permute-start | bytes 55304 | tf_op jit(solution)/shard_map/ppermute | solution.py:227
  28.1 3.8 %collective-permute-start.8 = (bf16[8,1152]{1,0:T(8,128)(2,1)S(1)}, bf16[8,1152]{1,0:T(8,128)(2,1)S(1)}, u32[]{:S(2)}, u32[]{:S(2)}) collective-permute-start(bf16[8,1152]{1,0:T(8,128)(2,1)S(1)} %get-tuple-element.35), channel_id=1, source_target_pairs={{0,8},{4,12},{8,0},{12,4},{16,24},{20,28},{24,16},{28,20},{1,9},{5... | collective-permute-start | bytes 55304 | tf_op jit(solution)/shard_map/ppermute | solution.py:227
  28.1 3.8 %collective-permute-start.9 = (bf16[8,1152]{1,0:T(8,128)(2,1)S(1)}, bf16[8,1152]{1,0:T(8,128)(2,1)S(1)}, u32[]{:S(2)}, u32[]{:S(2)}) collective-permute-start(bf16[8,1152]{1,0:T(8,128)(2,1)S(1)} %get-tuple-element.36), channel_id=1, source_target_pairs={{0,16},{4,20},{8,24},{12,28},{16,0},{20,4},{24,8},{28,12},{1,17},{... | collective-permute-start | bytes 55304 | tf_op jit(solution)/shard_map/ppermute | solution.py:227
  32.0 5.4 %collective-permute-start.14 = (bf16[8,1152]{1,0:T(8,128)(2,1)S(1)}, bf16[8,1152]{1,0:T(8,128)(2,1)S(1)}, u32[]{:S(2)}, u32[]{:S(2)}) collective-permute-start(bf16[8,1152]{1,0:T(8,128)(2,1)S(1)} %get-tuple-element.43.refs_0_), channel_id=1, source_target_pairs={{0,1},{1,0},{2,3},{3,2},{4,5},{5,4},{6,7},{7,6},{8,9},{9,8},{10,11... | collective-permute-start | bytes 55304 | tf_op jit(solution)/shard_map/ppermute | solution.py:227
  32.1 5.3 %collective-permute-start.15 = (bf16[8,1152]{1,0:T(8,128)(2,1)S(1)}, bf16[8,1152]{1,0:T(8,128)(2,1)S(1)}, u32[]{:S(2)}, u32[]{:S(2)}) collective-permute-start(bf16[8,1152]{1,0:T(8,128)(2,1)S(1)} %get-tuple-element.43.refs_0_), channel_id=1, source_target_pairs={{0,2},{1,3},{2,0},{3,1},{4,6},{5,7},{6,4},{7,5},{8,10},{9,11},{10,... | collective-permute-start | bytes 55304 | tf_op jit(solution)/shard_map/ppermute | solution.py:227
  33.6 5.6 %collective-permute-start.16 = (bf16[8,1152]{1,0:T(8,128)(2,1)S(1)}, bf16[8,1152]{1,0:T(8,128)(2,1)S(1)}, u32[]{:S(2)}, u32[]{:S(2)}) collective-permute-start(bf16[8,1152]{1,0:T(8,128)(2,1)S(1)} %get-tuple-element.43.refs_0_), channel_id=1, source_target_pairs={{0,3},{1,2},{2,1},{3,0},{4,7},{5,6},{6,5},{7,4},{8,11},{9,10},{10,... | collective-permute-start | bytes 55304 | tf_op jit(solution)/shard_map/ppermute | solution.py:227

commit v3 on v2

--- a/solution.py
+++ b/solution.py
@@ -59,6 +59,10 @@
     rest = values - high.astype(F32)
     middle = rest.astype(BF16)
     return high, middle, (rest - middle.astype(F32)).astype(BF16)
+
+
+def flips(chips):
+    return [0, *range(chips - 1, 0, -1)]
 
 
 def chip_and_core():
@@ -106,7 +110,7 @@
         for h in range(HEADS // rows)
     ]
     keys = jnp.concatenate(keys, axis=1)
-    for m, out_ref in enumerate(out_refs):
+    for m, out_ref in zip(flips(len(out_refs)), out_refs):
         out_ref[:, :packed] = blocks_ref[chip ^ m]
         out_ref[:, packed:] = keys
 
@@ -115,8 +119,8 @@
     w_out_ref, out_ref = refs[chips:]
     _, rows, length = out_ref.shape
     part, width = w_out_ref.shape
-    for m in range(chips):
-        out_ref[m] = refs[m][:, :length]
+    for i in range(chips):
+        out_ref[i] = refs[i][:, :length]
     fit = length // width
     for j in range(part // rows):
         first = j % fit * width
@@ -132,8 +136,8 @@
     wide = width // chips
     pieces = table.shape[0] // rows
     chip, _ = chip_and_core()
-    for m in range(chips):
-        placed[chip ^ m] = parts[m][:, length - pieces * wide :]
+    for m, part_ref in zip(flips(chips), parts):
+        placed[chip ^ m] = part_ref[:, length - pieces * wide :]
     for j in range(pieces):
         for q in range(chips):
             table[j * rows : (j + 1) * rows, q * wide : (q + 1) * wide] = placed[
@@ -148,50 +152,52 @@
     expo = jnp.exp(spread - jnp.max(spread, axis=2, keepdims=True))
     weights = expo / jnp.sum(expo, axis=2, keepdims=True)
     weights = weights.reshape(HEADS * images, x.shape[0])
-    high = weights.astype(BF16)
-    low = (weights - high.astype(F32)).astype(BF16)
-    mixed = nn(jnp.concatenate([high, low], axis=0), x)
-    mixed = (mixed[: HEADS * images] + mixed[HEADS * images :]).astype(BF16)
-    every[...] = mixed.reshape(every.shape)
-    for m, out_ref in enumerate(outs):
+    every[...] = nn(weights.astype(BF16), x).astype(BF16).reshape(every.shape)
+    for m, out_ref in zip(flips(chips), outs):
         out_ref[...] = every[chip ^ m]
 
 
-def project_kernel(images, chips, *refs):
-    mixed_refs, parts = refs[:chips], refs[chips : 2 * chips]
-    w_out_ref, other_ref = refs[2 * chips : 2 * chips + 2]
-    out_refs, w_value = refs[2 * chips + 2 : -1], refs[-1]
-    _, rows, width = mixed_refs[0].shape
-    part = w_out_ref.shape[0]
-    heads = rows // images
+def unpack_kernel(chips, *refs):
+    w_out_ref, other_ref, w_value_ref, outs_ref = refs[chips:]
+    part, width = w_out_ref.shape
+    rows = other_ref.shape[1]
     chip, core = chip_and_core()
-    for m in range(chips):
-        for c, source in enumerate((parts[m], other_ref.at[m])):
-            place = core if c == 0 else 1 - core
+    for i, m in enumerate(flips(chips)):
+        for c, source in enumerate((refs[i], other_ref.at[i])):
+            place = core if (c == 0) == (m == 0) else 1 - core
             for t in range(CORES):
                 for j in range(part // rows):
                     first = (j * CORES + t) * part
-                    w_value[t, chip ^ m, place, j * rows : (j + 1) * rows] = source[
+                    w_value_ref[t, chip ^ m, place, j * rows : (j + 1) * rows] = source[
                         :, first : first + part
                     ]
+    outs_ref[core] = w_out_ref[...]
     fit = other_ref.shape[2] // width
-    outs = [
-        other_ref[chips + j // fit, :, j % fit * width : (j % fit + 1) * width]
-        for j in range(part // rows)
-    ]
+    for j in range(part // rows):
+        first = j % fit * width
+        outs_ref[1 - core, j * rows : (j + 1) * rows] = other_ref[
+            chips + j // fit, :, first : first + width
+        ]
+
+
+def project_kernel(images, chips, *refs):
+    mixed_refs, (w_value_ref, outs_ref), out_refs = refs[:chips], refs[chips : chips + 2], refs[chips + 2 :]
+    _, rows, width = mixed_refs[0].shape
+    part = outs_ref.shape[1]
+    heads = rows // images
     head = lax.broadcasted_iota(jnp.int32, (chips, images, part), 2)
     embed = jnp.zeros((chips * images, width), F32)
-    for shard, rows_out in ((core, w_out_ref[...]), (1 - core, jnp.concatenate(outs, axis=0))):
-        mixed = jnp.concatenate([ref[shard] for ref in mixed_refs], axis=0)
-        columns = w_value[shard].reshape(width, part)
-        every = nn(mixed, columns).reshape(chips, heads, images, part)
+    for t in range(CORES):
+        mixed = jnp.concatenate([ref[t] for ref in mixed_refs], axis=0)
+        every = nn(mixed, w_value_ref[t].reshape(width, part))
+        every = every.reshape(chips, heads, images, part)
         pooled = every[:, 0]
         for h in range(1, heads):
             pooled = jnp.where(head >= h * (part // heads), every[:, h], pooled)
         pooled = pooled.reshape(chips * images, part).astype(BF16)
-        embed = embed + nn(pooled, rows_out)
-    for m, out_ref in enumerate(out_refs):
-        out_ref[...] = embed[m * images : (m + 1) * images].astype(BF16)
+        embed = embed + nn(pooled, outs_ref[t])
+    for i, out_ref in enumerate(out_refs):
+        out_ref[...] = embed[i * images : (i + 1) * images].astype(BF16)
 
 
 def unit_text_kernel(blocks, *refs):
@@ -235,7 +241,10 @@
 
 
 def exchange_chips(arrays, devices):
-    return [array if m == 0 else exchange(array, devices, m * CORES) for m, array in enumerate(arrays)]
+    return [
+        exchange(array, devices, m * CORES + 1) if m else array
+        for m, array in zip(flips(len(arrays)), arrays)
+    ]
 
 
 def local(patches, probe, w_key, w_value, w_out, texts):
@@ -278,13 +287,6 @@
         exchange(w_key, devices, 1),
     )
     parts = exchange_chips(parts, devices)
-    shard = call(
-        functools.partial(shard_kernel, chips),
-        struct((chips + pl.cdiv(part // rows, fit), rows, packed), BF16),
-        *parts,
-        w_out,
-    )
-    other = exchange(shard, devices, 1)
     mixed = call(
         functools.partial(attend_kernel, images, scaling, chips),
         [struct((CORES, rows, width), BF16)] * chips,
@@ -296,14 +298,28 @@
             pltpu.VMEM((chips, CORES, rows, width), BF16),
         ],
     )
+    shard = call(
+        functools.partial(shard_kernel, chips),
+        struct((chips + pl.cdiv(part // rows, fit), rows, packed), BF16),
+        *parts,
+        w_out,
+    )
+    w_values, w_outs = call(
+        functools.partial(unpack_kernel, chips),
+        (
+            struct((CORES, chips, CORES, part, part), BF16),
+            struct((CORES, part, width), BF16),
+        ),
+        *parts,
+        w_out,
+        exchange(shard, devices, 1),
+    )
     partial_embed = call(
         functools.partial(project_kernel, images, chips),
         [struct((images, width), BF16)] * chips,
         *exchange_chips(mixed, devices),
-        *parts,
-        w_out,
-        other,
-        scratch=[pltpu.VMEM((CORES, chips, CORES, part, part), BF16)],
+        w_values,
+        w_outs,
     )
     row, column = struct((images, width), F32), struct((images, 128), F32)
     words, unit_text, inverse_text = call(
@@ -317,9 +333,9 @@
         *exchange_chips(partial_embed, devices),
         inverse_text,
     )
-    all_images = [rounded] + [exchange(rounded, blocks, m, "blk") for m in range(1, blocks)]
+    all_images = [exchange(rounded, blocks, m, "blk") for m in range(blocks - 1, 0, -1)]
     grad_image = call(grad_kernel, row, unit, inverse, words)
-    grad_text = call(grad_kernel, row, unit_text, inverse_text, *all_images)
+    grad_text = call(grad_kernel, row, unit_text, inverse_text, rounded, *all_images)
     return grad_image, grad_text
 
 

time: 40.3 us -> 37.8 us (0.938)
  starting transfers between devices: 22.8 us -> 21.2 us
  waiting for transfers between devices: 10.5 us -> 9.75 us
    ppermute x14, starting transfers between devices: 16.9 us -> 15.5 us  [exchange(): return lax.ppermute(array, axis, [(i, i ^ flip) for i in range(devices)])]
    ppermute x14, waiting for transfers between devices: 10.5 us -> 9.74 us  [exchange(): return lax.ppermute(array, axis, [(i, i ^ flip) for i in range(devices)])]
    pallas_call x9 -> x10, Pallas kernels: 6.14 us -> 5.99 us  [call(): pl.pallas_call(body, out_shape=out, in_specs=[pl.BlockSpec(memory_space=s...]
  transfers between devices with their start and end apart: 17 -> 17, of which waited for: 6 -> 9; matrix products, arithmetic and copies ran while one was open for 0% -> 0% of each run, Pallas kernels for 11% -> 12%
where the time goes in v3:
time: 37.8 us; the launch traced here: 37.7 us
  starting transfers between devices  21.2 us (56%)
  waiting for transfers between devices  9.75 us (26%)
  Pallas kernels  5.99 us (16%)
  between operations  0.72 us (2%)
    ppermute x14, starting transfers between devices, exchange(): return lax.ppermute(array, axis, [(i, i ^ flip) for i in range(devices)])  15.5 us
    ppermute x14, waiting for transfers between devices, exchange(): return lax.ppermute(array, axis, [(i, i ^ flip) for i in range(devices)])  9.74 us
    pallas_call x10, Pallas kernels, call(): pl.pallas_call(body, out_shape=out, in_specs=[pl.BlockSpec(memory_space=s...  5.99 us
    ppermute x3, starting transfers between devices, all_blocks(): lax.ppermute(array, 'blk', [(i, (i + by) % blocks) for i in range(blocks)])  5.73 us
  transfers between devices with their start and end apart: 17, of which 9 were waited for; matrix products, arithmetic and copies ran while one was open for 0% of the time, Pallas kernels for 12%

profile of v3, /device:TPU:0, one launch (start us, length us, event | category | flops | bytes accessed | tf_op | source)
XLA Modules:
  0.0 37.7 jit_solution(6366914320585899631)
XLA Ops:
  0.6 0.5 %collective-permute-start = (bf16[144,1152]{1,0:T(8,128)(2,1)}, bf16[144,1152]{1,0:T(8,128)(2,1)S(1)}, u32[]{:S(2)}, u32[]{:S(2)}) collective-permute-start(bf16[144,1152]{1,0:T(8,128)(2,1)} %w_key_hbm.1), channel_id=1, source_target_pairs={{0,4},{4,0},{8,12},{12,8},{16,20},{20,16},{24,28},{28,24},{1,5},{5... | collective-permute-start | bytes 995336 | tf_op jit(solution)/shard_map/ppermute | solution.py:233
  1.2 1.4 %shard_map.77 = (f32[16,144]{1,0:T(8,128)S(1)}, bf16[16,1152]{1,0:T(8,128)(2,1)S(1)}, bf16[4,16,2592]{2,1,0:T(8,128)(2,1)S(1)}) custom-call(bf16[1152]{0:T(1024)(128)(2,1)} %probe_hbm.1, bf16[144,1152]{1,0:T(8,128)(2,1)} %w_key_hbm.1, bf16[144,1152]{1,0:T(8,128)(2,1)} %w_value_hbm.1), custom_call_target="tpu_custom_call" | custom-call | tf_op jit(solution)/shard_map/pallas_call | solution.py:22
  2.6 0.4 %shard_map.78 = (bf16[16,3456]{1,0:T(8,128)(2,1)S(1)}, bf16[16,3456]{1,0:T(8,128)(2,1)S(1)}, bf16[16,3456]{1,0:T(8,128)(2,1)S(1)}, bf16[16,3456]{1,0:T(8,128)(2,1)S(1)}) custom-call(f32[16,144]{1,0:T(8,128)S(1)} %get-tuple-element.25.keys_ref, bf16[16,1152]{1,0:T(8,128)(2,1)S(1)} %get-tuple-element.26.table_ref, ...), custom_call_target="tpu_custom_call" | custom-call | tf_op jit(solution)/shard_map/pallas_call | solution.py:22
  3.1 3.6 %collective-permute-start.1 = (bf16[16,3456]{1,0:T(8,128)(2,1)S(1)}, bf16[16,3456]{1,0:T(8,128)(2,1)S(1)}, u32[]{:S(2)}, u32[]{:S(2)}) collective-permute-start(bf16[16,3456]{1,0:T(8,128)(2,1)S(1)} %get-tuple-element.29), channel_id=1, source_target_pairs={{0,28},{4,24},{8,20},{12,16},{16,12},{20,8},{24,4},{28,0},{1,29},{... | collective-permute-start | bytes 331784 | tf_op jit(solution)/shard_map/ppermute | solution.py:233
  6.7 0.5 %collective-permute-start.2 = (bf16[16,3456]{1,0:T(8,128)(2,1)S(1)}, bf16[16,3456]{1,0:T(8,128)(2,1)S(1)}, u32[]{:S(2)}, u32[]{:S(2)}) collective-permute-start(bf16[16,3456]{1,0:T(8,128)(2,1)S(1)} %get-tuple-element.30), channel_id=1, source_target_pairs={{0,20},{4,16},{8,28},{12,24},{16,4},{20,0},{24,12},{28,8},{1,21},{... | collective-permute-start | bytes 331784 | tf_op jit(solution)/shard_map/ppermute | solution.py:233
  7.3 2.9 %collective-permute-done.1.refs_1_ = bf16[16,3456]{1,0:T(8,128)(2,1)S(1)} collective-permute-done((bf16[16,3456]{1,0:T(8,128)(2,1)S(1)}, bf16[16,3456]{1,0:T(8,128)(2,1)S(1)}, u32[]{:S(2)}, u32[]{:S(2)}) %collective-permute-start.1) | collective-permute-done | bytes 110624 | tf_op jit(solution)/shard_map/ppermute | solution.py:233
  10.2 2.4 %collective-permute-done.2.refs_2_ = bf16[16,3456]{1,0:T(8,128)(2,1)S(1)} collective-permute-done((bf16[16,3456]{1,0:T(8,128)(2,1)S(1)}, bf16[16,3456]{1,0:T(8,128)(2,1)S(1)}, u32[]{:S(2)}, u32[]{:S(2)}) %collective-permute-start.2) | collective-permute-done | bytes 110624 | tf_op jit(solution)/shard_map/ppermute | solution.py:233
  13.2 1.0 %shard_map.79 = (bf16[2,16,1152]{2,1,0:T(8,128)(2,1)S(1)}, bf16[2,16,1152]{2,1,0:T(8,128)(2,1)S(1)}, bf16[2,16,1152]{2,1,0:T(8,128)(2,1)S(1)}, bf16[2,16,1152]{2,1,0:T(8,128)(2,1)S(1)}) custom-call(bf16[512,1152]{1,0:T(8,128)(2,1)S(1)} %bitcast.1, bf16[16,3456]{1,0:T(8,128)(2,1)S(1)} %get-tuple-element.28.refs_0_, ...), custom_call_target="tpu_custom_call" | custom-call | tf_op jit(solution)/shard_map/pallas_call | solution.py:22
  14.2 1.6 %collective-permute-start.4 = (bf16[2,16,1152]{2,1,0:T(8,128)(2,1)S(1)}, bf16[2,16,1152]{2,1,0:T(8,128)(2,1)S(1)}, u32[]{:S(2)}, u32[]{:S(2)}) collective-permute-start(bf16[2,16,1152]{2,1,0:T(8,128)(2,1)S(1)} %get-tuple-element.33), channel_id=1, source_target_pairs={{0,28},{4,24},{8,20},{12,16},{16,12},{20,8},{24,4},{28,0},{1,29},{... | collective-permute-start | bytes 221192 | tf_op jit(solution)/shard_map/ppermute | solution.py:233
  15.8 1.4 %collective-permute-start.5 = (bf16[2,16,1152]{2,1,0:T(8,128)(2,1)S(1)}, bf16[2,16,1152]{2,1,0:T(8,128)(2,1)S(1)}, u32[]{:S(2)}, u32[]{:S(2)}) collective-permute-start(bf16[2,16,1152]{2,1,0:T(8,128)(2,1)S(1)} %get-tuple-element.34), channel_id=1, source_target_pairs={{0,20},{4,16},{8,28},{12,24},{16,4},{20,0},{24,12},{28,8},{1,21},{... | collective-permute-start | bytes 221192 | tf_op jit(solution)/shard_map/ppermute | solution.py:233
  17.5 1.8 %collective-permute-start.11 = (bf16[8,1152]{1,0:T(8,128)(2,1)S(1)}, bf16[8,1152]{1,0:T(8,128)(2,1)S(1)}, u32[]{:S(2)}, u32[]{:S(2)}) collective-permute-start(bf16[8,1152]{1,0:T(8,128)(2,1)S(1)} %copy-done.2), channel_id=1, source_target_pairs={{0,1},{1,2},{2,3},{3,0},{4,5},{5,6},{6,7},{7,4},{8,9},{9,10},{10,1... | collective-permute-start | bytes 55304 | tf_op jit(solution)/shard_map/ppermute | solution.py:238
  19.3 2.5 %collective-permute-start.12 = (bf16[8,1152]{1,0:T(8,128)(2,1)S(1)}, bf16[8,1152]{1,0:T(8,128)(2,1)S(1)}, u32[]{:S(2)}, u32[]{:S(2)}) collective-permute-start(bf16[8,1152]{1,0:T(8,128)(2,1)S(1)} %copy-done.2), channel_id=1, source_target_pairs={{0,2},{1,3},{2,0},{3,1},{4,6},{5,7},{6,4},{7,5},{8,10},{9,11},{10,... | collective-permute-start | bytes 55304 | tf_op jit(solution)/shard_map/ppermute | solution.py:238
  22.2 1.4 %collective-permute-start.13 = (bf16[8,1152]{1,0:T(8,128)(2,1)S(1)}, bf16[8,1152]{1,0:T(8,128)(2,1)S(1)}, u32[]{:S(2)}, u32[]{:S(2)}) collective-permute-start(bf16[8,1152]{1,0:T(8,128)(2,1)S(1)} %copy-done.2), channel_id=1, source_target_pairs={{0,3},{1,0},{2,1},{3,2},{4,7},{5,4},{6,5},{7,6},{8,11},{9,8},{10,9... | collective-permute-start | bytes 55304 | tf_op jit(solution)/shard_map/ppermute | solution.py:238
  23.6 0.5 %shard_map.82 = (bf16[8,1152]{1,0:T(8,128)(2,1)S(1)}, bf16[8,1152]{1,0:T(8,128)(2,1)S(1)}, bf16[8,1152]{1,0:T(8,128)(2,1)S(1)}, bf16[8,1152]{1,0:T(8,128)(2,1)S(1)}) custom-call(bf16[2,16,1152]{2,1,0:T(8,128)(2,1)S(1)} %get-tuple-element.32.refs_0_, bf16[2,16,1152]{2,1,0:T(8,128)(2,1)S(1)} %collective-permute-done.4.refs_1_, ...), custom_call_target="tpu_custom_call" | custom-call | tf_op jit(solution)/shard_map/pallas_call | solution.py:22
  24.1 0.7 %collective-permute-start.10 = (bf16[8,1152]{1,0:T(8,128)(2,1)S(1)}, bf16[8,1152]{1,0:T(8,128)(2,1)S(1)}, u32[]{:S(2)}, u32[]{:S(2)}) collective-permute-start(bf16[8,1152]{1,0:T(8,128)(2,1)S(1)} %get-tuple-element.41), channel_id=1, source_target_pairs={{0,12},{4,8},{8,4},{12,0},{16,28},{20,24},{24,20},{28,16},{1,13},{... | collective-permute-start | bytes 55304 | tf_op jit(solution)/shard_map/ppermute | solution.py:233
  24.9 2.0 %collective-permute-start.8 = (bf16[8,1152]{1,0:T(8,128)(2,1)S(1)}, bf16[8,1152]{1,0:T(8,128)(2,1)S(1)}, u32[]{:S(2)}, u32[]{:S(2)}) collective-permute-start(bf16[8,1152]{1,0:T(8,128)(2,1)S(1)} %get-tuple-element.39), channel_id=1, source_target_pairs={{0,28},{4,24},{8,20},{12,16},{16,12},{20,8},{24,4},{28,0},{1,29},{... | collective-permute-start | bytes 55304 | tf_op jit(solution)/shard_map/ppermute | solution.py:233
  27.5 1.5 %collective-permute-done.8.refs_1_ = bf16[8,1152]{1,0:T(8,128)(2,1)S(1)} collective-permute-done((bf16[8,1152]{1,0:T(8,128)(2,1)S(1)}, bf16[8,1152]{1,0:T(8,128)(2,1)S(1)}, u32[]{:S(2)}, u32[]{:S(2)}) %collective-permute-start.8) | collective-permute-done | bytes 18464 | tf_op jit(solution)/shard_map/ppermute | solution.py:233
  28.9 1.3 %collective-permute-done.9.refs_2_ = bf16[8,1152]{1,0:T(8,128)(2,1)S(1)} collective-permute-done((bf16[8,1152]{1,0:T(8,128)(2,1)S(1)}, bf16[8,1152]{1,0:T(8,128)(2,1)S(1)}, u32[]{:S(2)}, u32[]{:S(2)}) %collective-permute-start.9) | collective-permute-done | bytes 18464 | tf_op jit(solution)/shard_map/ppermute | solution.py:233
  30.4 1.5 %collective-permute-start.14 = (bf16[8,1152]{1,0:T(8,128)(2,1)S(1)}, bf16[8,1152]{1,0:T(8,128)(2,1)S(1)}, u32[]{:S(2)}, u32[]{:S(2)}) collective-permute-start(bf16[8,1152]{1,0:T(8,128)(2,1)S(1)} %get-tuple-element.47.refs_0_), channel_id=1, source_target_pairs={{0,3},{1,2},{2,1},{3,0},{4,7},{5,6},{6,5},{7,4},{8,11},{9,10},{10,... | collective-permute-start | bytes 55304 | tf_op jit(solution)/shard_map/ppermute | solution.py:233
  31.8 0.7 %collective-permute-start.15 = (bf16[8,1152]{1,0:T(8,128)(2,1)S(1)}, bf16[8,1152]{1,0:T(8,128)(2,1)S(1)}, u32[]{:S(2)}, u32[]{:S(2)}) collective-permute-start(bf16[8,1152]{1,0:T(8,128)(2,1)S(1)} %get-tuple-element.47.refs_0_), channel_id=1, source_target_pairs={{0,2},{1,3},{2,0},{3,1},{4,6},{5,7},{6,4},{7,5},{8,10},{9,11},{10,... | collective-permute-start | bytes 55304 | tf_op jit(solution)/shard_map/ppermute | solution.py:233
  32.5 2.2 %collective-permute-start.16 = (bf16[8,1152]{1,0:T(8,128)(2,1)S(1)}, bf16[8,1152]{1,0:T(8,128)(2,1)S(1)}, u32[]{:S(2)}, u32[]{:S(2)}) collective-permute-start(bf16[8,1152]{1,0:T(8,128)(2,1)S(1)} %get-tuple-element.47.refs_0_), channel_id=1, source_target_pairs={{0,1},{1,0},{2,3},{3,2},{4,5},{5,4},{6,7},{7,6},{8,9},{9,8},{10,11... | collective-permute-start | bytes 55304 | tf_op jit(solution)/shard_map/ppermute | solution.py:233
  34.8 1.0 %shard_map.85 = f32[8,1152]{1,0:T(8,128)} custom-call(f32[8,1152]{1,0:T(8,128)S(1)} %get-tuple-element.43.unit_ref, f32[8,128]{1,0:T(8,128)S(1)} %get-tuple-element.44.inverse_ref, bf16[32,1152]{1,0:T(8,128)(2,1)S(1)} %get-tuple-element.45.refs_0_), custom_call_target="tpu_custom_call" | custom-call | tf_op jit(solution)/shard_map/pallas_call | solution.py:22
  35.9 0.6 %collective-permute-done.15.refs_2_ = bf16[8,1152]{1,0:T(8,128)(2,1)S(1)} collective-permute-done((bf16[8,1152]{1,0:T(8,128)(2,1)S(1)}, bf16[8,1152]{1,0:T(8,128)(2,1)S(1)}, u32[]{:S(2)}, u32[]{:S(2)}) %collective-permute-start.15) | collective-permute-done | bytes 18464 | tf_op jit(solution)/shard_map/ppermute | solution.py:233
  36.7 1.0 %shard_map.86 = f32[8,1152]{1,0:T(8,128)} custom-call(f32[8,1152]{1,0:T(8,128)S(1)} %get-tuple-element.46.unit_ref, f32[8,128]{1,0:T(8,128)S(1)} %get-tuple-element.42.refs_4_.inverse_ref, bf16[8,1152]{1,0:T(8,128)(2,1)S(1)} %get-tuple-element.47.refs_0_, bf16[8,1152]{1,0:T(8,128)(2,1)S(1)} %collective-permute-done.14.refs_1_, ...), custom_call_target="tpu_custom_call" | custom-call | tf_op jit(solution)/shard_map/pallas_call | solution.py:22
  (26 shorter events, 2.4 us)
Async XLA Ops:
  0.6 12.3 %copy-start = (bf16[144,1152]{1,0:T(8,128)(2,1)S(1)}, bf16[144,1152]{1,0:T(8,128)(2,1)}, u32[]{:S(2)}) copy-start(bf16[144,1152]{1,0:T(8,128)(2,1)} %refs_4_.3) | copy-start | bytes 995332
  0.6 2.0 %collective-permute-start = (bf16[144,1152]{1,0:T(8,128)(2,1)}, bf16[144,1152]{1,0:T(8,128)(2,1)S(1)}, u32[]{:S(2)}, u32[]{:S(2)}) collective-permute-start(bf16[144,1152]{1,0:T(8,128)(2,1)} %w_key_hbm.1), channel_id=1, source_target_pairs={{0,4},{4,0},{8,12},{12,8},{16,20},{20,16},{24,28},{28,24},{1,5},{5... | collective-permute-start | bytes 995336 | tf_op jit(solution)/shard_map/ppermute | solution.py:233
  2.6 10.6 %copy-start.1 = (bf16[8,64,1152]{2,1,0:T(8,128)(2,1)S(1)}, bf16[8,64,1152]{2,1,0:T(8,128)(2,1)}, u32[]{:S(2)}) copy-start(bf16[8,64,1152]{2,1,0:T(8,128)(2,1)} %param.6) | copy-start | bytes 3538948
  3.1 7.1 %collective-permute-start.1 = (bf16[16,3456]{1,0:T(8,128)(2,1)S(1)}, bf16[16,3456]{1,0:T(8,128)(2,1)S(1)}, u32[]{:S(2)}, u32[]{:S(2)}) collective-permute-start(bf16[16,3456]{1,0:T(8,128)(2,1)S(1)} %get-tuple-element.29), channel_id=1, source_target_pairs={{0,28},{4,24},{8,20},{12,16},{16,12},{20,8},{24,4},{28,0},{1,29},{... | collective-permute-start | bytes 331784 | tf_op jit(solution)/shard_map/ppermute | solution.py:233
  6.7 5.9 %collective-permute-start.2 = (bf16[16,3456]{1,0:T(8,128)(2,1)S(1)}, bf16[16,3456]{1,0:T(8,128)(2,1)S(1)}, u32[]{:S(2)}, u32[]{:S(2)}) collective-permute-start(bf16[16,3456]{1,0:T(8,128)(2,1)S(1)} %get-tuple-element.30), channel_id=1, source_target_pairs={{0,20},{4,16},{8,28},{12,24},{16,4},{20,0},{24,12},{28,8},{1,21},{... | collective-permute-start | bytes 331784 | tf_op jit(solution)/shard_map/ppermute | solution.py:233
  7.2 5.7 %collective-permute-start.3 = (bf16[16,3456]{1,0:T(8,128)(2,1)S(1)}, bf16[16,3456]{1,0:T(8,128)(2,1)S(1)}, u32[]{:S(2)}, u32[]{:S(2)}) collective-permute-start(bf16[16,3456]{1,0:T(8,128)(2,1)S(1)} %get-tuple-element.31), channel_id=1, source_target_pairs={{0,12},{4,8},{8,4},{12,0},{16,28},{20,24},{24,20},{28,16},{1,13},{... | collective-permute-start | bytes 331784 | tf_op jit(solution)/shard_map/ppermute | solution.py:233
  13.0 4.5 %copy-start.2 = (bf16[8,1152]{1,0:T(8,128)(2,1)S(1)}, bf16[8,1152]{1,0:T(8,128)(2,1)}, u32[]{:S(2)}) copy-start(bf16[8,1152]{1,0:T(8,128)(2,1)} %refs_0_.1) | copy-start | bytes 55300
  13.0 6.3 %collective-permute-start.7 = (bf16[9,16,2592]{2,1,0:T(8,128)(2,1)S(1)}, bf16[9,16,2592]{2,1,0:T(8,128)(2,1)S(1)}, u32[]{:S(2)}, u32[]{:S(2)}) collective-permute-start(bf16[9,16,2592]{2,1,0:T(8,128)(2,1)S(1)} %shard_map.80), channel_id=1, source_target_pairs={{0,4},{4,0},{8,12},{12,8},{16,20},{20,16},{24,28},{28,24},{1,5},{5... | collective-permute-start | bytes 2239496 | tf_op jit(solution)/shard_map/ppermute | solution.py:233
  14.2 8.0 %collective-permute-start.4 = (bf16[2,16,1152]{2,1,0:T(8,128)(2,1)S(1)}, bf16[2,16,1152]{2,1,0:T(8,128)(2,1)S(1)}, u32[]{:S(2)}, u32[]{:S(2)}) collective-permute-start(bf16[2,16,1152]{2,1,0:T(8,128)(2,1)S(1)} %get-tuple-element.33), channel_id=1, source_target_pairs={{0,28},{4,24},{8,20},{12,16},{16,12},{20,8},{24,4},{28,0},{1,29},{... | collective-permute-start | bytes 221192 | tf_op jit(solution)/shard_map/ppermute | solution.py:233
  15.8 7.8 %collective-permute-start.5 = (bf16[2,16,1152]{2,1,0:T(8,128)(2,1)S(1)}, bf16[2,16,1152]{2,1,0:T(8,128)(2,1)S(1)}, u32[]{:S(2)}, u32[]{:S(2)}) collective-permute-start(bf16[2,16,1152]{2,1,0:T(8,128)(2,1)S(1)} %get-tuple-element.34), channel_id=1, source_target_pairs={{0,20},{4,16},{8,28},{12,24},{16,4},{20,0},{24,12},{28,8},{1,21},{... | collective-permute-start | bytes 221192 | tf_op jit(solution)/shard_map/ppermute | solution.py:233
  17.2 6.4 %collective-permute-start.6 = (bf16[2,16,1152]{2,1,0:T(8,128)(2,1)S(1)}, bf16[2,16,1152]{2,1,0:T(8,128)(2,1)S(1)}, u32[]{:S(2)}, u32[]{:S(2)}) collective-permute-start(bf16[2,16,1152]{2,1,0:T(8,128)(2,1)S(1)} %get-tuple-element.35), channel_id=1, source_target_pairs={{0,12},{4,8},{8,4},{12,0},{16,28},{20,24},{24,20},{28,16},{1,13},{... | collective-permute-start | bytes 221192 | tf_op jit(solution)/shard_map/ppermute | solution.py:233
  17.5 9.4 %collective-permute-start.11 = (bf16[8,1152]{1,0:T(8,128)(2,1)S(1)}, bf16[8,1152]{1,0:T(8,128)(2,1)S(1)}, u32[]{:S(2)}, u32[]{:S(2)}) collective-permute-start(bf16[8,1152]{1,0:T(8,128)(2,1)S(1)} %copy-done.2), channel_id=1, source_target_pairs={{0,1},{1,2},{2,3},{3,0},{4,5},{5,6},{6,7},{7,4},{8,9},{9,10},{10,1... | collective-permute-start | bytes 55304 | tf_op jit(solution)/shard_map/ppermute | solution.py:238
  19.3 7.7 %collective-permute-start.12 = (bf16[8,1152]{1,0:T(8,128)(2,1)S(1)}, bf16[8,1152]{1,0:T(8,128)(2,1)S(1)}, u32[]{:S(2)}, u32[]{:S(2)}) collective-permute-start(bf16[8,1152]{1,0:T(8,128)(2,1)S(1)} %copy-done.2), channel_id=1, source_target_pairs={{0,2},{1,3},{2,0},{3,1},{4,6},{5,7},{6,4},{7,5},{8,10},{9,11},{10,... | collective-permute-start | bytes 55304 | tf_op jit(solution)/shard_map/ppermute | solution.py:238
  22.2 4.8 %collective-permute-start.13 = (bf16[8,1152]{1,0:T(8,128)(2,1)S(1)}, bf16[8,1152]{1,0:T(8,128)(2,1)S(1)}, u32[]{:S(2)}, u32[]{:S(2)}) collective-permute-start(bf16[8,1152]{1,0:T(8,128)(2,1)S(1)} %copy-done.2), channel_id=1, source_target_pairs={{0,3},{1,0},{2,1},{3,2},{4,7},{5,4},{6,5},{7,6},{8,11},{9,8},{10,9... | collective-permute-start | bytes 55304 | tf_op jit(solution)/shard_map/ppermute | solution.py:238
  24.1 3.4 %collective-permute-start.10 = (bf16[8,1152]{1,0:T(8,128)(2,1)S(1)}, bf16[8,1152]{1,0:T(8,128)(2,1)S(1)}, u32[]{:S(2)}, u32[]{:S(2)}) collective-permute-start(bf16[8,1152]{1,0:T(8,128)(2,1)S(1)} %get-tuple-element.41), channel_id=1, source_target_pairs={{0,12},{4,8},{8,4},{12,0},{16,28},{20,24},{24,20},{28,16},{1,13},{... | collective-permute-start | bytes 55304 | tf_op jit(solution)/shard_map/ppermute | solution.py:233
  24.9 4.1 %collective-permute-start.8 = (bf16[8,1152]{1,0:T(8,128)(2,1)S(1)}, bf16[8,1152]{1,0:T(8,128)(2,1)S(1)}, u32[]{:S(2)}, u32[]{:S(2)}) collective-permute-start(bf16[8,1152]{1,0:T(8,128)(2,1)S(1)} %get-tuple-element.39), channel_id=1, source_target_pairs={{0,28},{4,24},{8,20},{12,16},{16,12},{20,8},{24,4},{28,0},{1,29},{... | collective-permute-start | bytes 55304 | tf_op jit(solution)/shard_map/ppermute | solution.py:233
  26.9 3.4 %collective-permute-start.9 = (bf16[8,1152]{1,0:T(8,128)(2,1)S(1)}, bf16[8,1152]{1,0:T(8,128)(2,1)S(1)}, u32[]{:S(2)}, u32[]{:S(2)}) collective-permute-start(bf16[8,1152]{1,0:T(8,128)(2,1)S(1)} %get-tuple-element.40), channel_id=1, source_target_pairs={{0,20},{4,16},{8,28},{12,24},{16,4},{20,0},{24,12},{28,8},{1,21},{... | collective-permute-start | bytes 55304 | tf_op jit(solution)/shard_map/ppermute | solution.py:233
  30.4 5.6 %collective-permute-start.14 = (bf16[8,1152]{1,0:T(8,128)(2,1)S(1)}, bf16[8,1152]{1,0:T(8,128)(2,1)S(1)}, u32[]{:S(2)}, u32[]{:S(2)}) collective-permute-start(bf16[8,1152]{1,0:T(8,128)(2,1)S(1)} %get-tuple-element.47.refs_0_), channel_id=1, source_target_pairs={{0,3},{1,2},{2,1},{3,0},{4,7},{5,6},{6,5},{7,4},{8,11},{9,10},{10,... | collective-permute-start | bytes 55304 | tf_op jit(solution)/shard_map/ppermute | solution.py:233
  31.8 4.7 %collective-permute-start.15 = (bf16[8,1152]{1,0:T(8,128)(2,1)S(1)}, bf16[8,1152]{1,0:T(8,128)(2,1)S(1)}, u32[]{:S(2)}, u32[]{:S(2)}) collective-permute-start(bf16[8,1152]{1,0:T(8,128)(2,1)S(1)} %get-tuple-element.47.refs_0_), channel_id=1, source_target_pairs={{0,2},{1,3},{2,0},{3,1},{4,6},{5,7},{6,4},{7,5},{8,10},{9,11},{10,... | collective-permute-start | bytes 55304 | tf_op jit(solution)/shard_map/ppermute | solution.py:233
  32.5 4.2 %collective-permute-start.16 = (bf16[8,1152]{1,0:T(8,128)(2,1)S(1)}, bf16[8,1152]{1,0:T(8,128)(2,1)S(1)}, u32[]{:S(2)}, u32[]{:S(2)}) collective-permute-start(bf16[8,1152]{1,0:T(8,128)(2,1)S(1)} %get-tuple-element.47.refs_0_), channel_id=1, source_target_pairs={{0,1},{1,0},{2,3},{3,2},{4,5},{5,4},{6,7},{7,6},{8,9},{9,8},{10,11... | collective-permute-start | bytes 55304 | tf_op jit(solution)/shard_map/ppermute | solution.py:233

commit v4 on v3

--- a/solution.py
+++ b/solution.py
@@ -59,10 +59,6 @@
     rest = values - high.astype(F32)
     middle = rest.astype(BF16)
     return high, middle, (rest - middle.astype(F32)).astype(BF16)
-
-
-def flips(chips):
-    return [0, *range(chips - 1, 0, -1)]
 
 
 def chip_and_core():
@@ -110,7 +106,7 @@
         for h in range(HEADS // rows)
     ]
     keys = jnp.concatenate(keys, axis=1)
-    for m, out_ref in zip(flips(len(out_refs)), out_refs):
+    for m, out_ref in enumerate(out_refs):
         out_ref[:, :packed] = blocks_ref[chip ^ m]
         out_ref[:, packed:] = keys
 
@@ -119,15 +115,19 @@
     w_out_ref, out_ref = refs[chips:]
     _, rows, length = out_ref.shape
     part, width = w_out_ref.shape
-    for i in range(chips):
-        out_ref[i] = refs[i][:, :length]
+    for m in range(chips):
+        out_ref[m] = refs[m][:, :length]
     fit = length // width
     for j in range(part // rows):
         first = j % fit * width
         out_ref[chips + j // fit, :, first : first + width] = w_out_ref[j * rows : (j + 1) * rows]
 
 
-def attend_kernel(images, scaling, chips, x_ref, *refs):
+def turn_kernel(x_ref, out_ref):
+    out_ref[...] = x_ref[...].T
+
+
+def attend_kernel(images, scaling, chips, x_ref, turned_ref, *refs):
     parts, outs, (placed, table, every) = refs[:chips], refs[chips:-3], refs[-3:]
     x = x_ref[...]
     width = x.shape[1]
@@ -136,14 +136,14 @@
     wide = width // chips
     pieces = table.shape[0] // rows
     chip, _ = chip_and_core()
-    for m, part_ref in zip(flips(chips), parts):
-        placed[chip ^ m] = part_ref[:, length - pieces * wide :]
+    for m in range(chips):
+        placed[chip ^ m] = parts[m][:, length - pieces * wide :]
     for j in range(pieces):
         for q in range(chips):
             table[j * rows : (j + 1) * rows, q * wide : (q + 1) * wide] = placed[
                 q, :, j * wide : (j + 1) * wide
             ]
-    parts = nt(table[...], x)
+    parts = nn(table[...], turned_ref[...])
     scores = (parts[:HEADS] + parts[HEADS : 2 * HEADS] + parts[2 * HEADS :]) * scaling
     image = lax.broadcasted_iota(jnp.int32, (images, x.shape[0]), 0)
     first = lax.broadcasted_iota(jnp.int32, (images, x.shape[0]), 1) - image * patches
@@ -153,7 +153,7 @@
     weights = expo / jnp.sum(expo, axis=2, keepdims=True)
     weights = weights.reshape(HEADS * images, x.shape[0])
     every[...] = nn(weights.astype(BF16), x).astype(BF16).reshape(every.shape)
-    for m, out_ref in zip(flips(chips), outs):
+    for m, out_ref in enumerate(outs):
         out_ref[...] = every[chip ^ m]
 
 
@@ -162,8 +162,8 @@
     part, width = w_out_ref.shape
     rows = other_ref.shape[1]
     chip, core = chip_and_core()
-    for i, m in enumerate(flips(chips)):
-        for c, source in enumerate((refs[i], other_ref.at[i])):
+    for m in range(chips):
+        for c, source in enumerate((refs[m], other_ref.at[m])):
             place = core if (c == 0) == (m == 0) else 1 - core
             for t in range(CORES):
                 for j in range(part // rows):
@@ -196,8 +196,8 @@
             pooled = jnp.where(head >= h * (part // heads), every[:, h], pooled)
         pooled = pooled.reshape(chips * images, part).astype(BF16)
         embed = embed + nn(pooled, outs_ref[t])
-    for i, out_ref in enumerate(out_refs):
-        out_ref[...] = embed[i * images : (i + 1) * images].astype(BF16)
+    for m, out_ref in enumerate(out_refs):
+        out_ref[...] = embed[m * images : (m + 1) * images].astype(BF16)
 
 
 def unit_text_kernel(blocks, *refs):
@@ -241,9 +241,8 @@
 
 
 def exchange_chips(arrays, devices):
-    return [
-        exchange(array, devices, m * CORES + 1) if m else array
-        for m, array in zip(flips(len(arrays)), arrays)
+    return [arrays[0]] + [
+        exchange(array, devices, m * CORES + 1) for m, array in enumerate(arrays) if m
     ]
 
 
@@ -291,6 +290,7 @@
         functools.partial(attend_kernel, images, scaling, chips),
         [struct((CORES, rows, width), BF16)] * chips,
         flat,
+        call(turn_kernel, struct(flat.shape[::-1], BF16), flat),
         *parts,
         scratch=[
             pltpu.VMEM((chips, rows, 3 * HEADS // rows * wide), BF16),

time: 37.8 us -> 37.8 us (level)
  starting transfers between devices: 21.2 us -> 20.7 us
    pallas_call x10 -> x11, Pallas kernels: 5.99 us -> 6.26 us  [call(): pl.pallas_call(body, out_shape=out, in_specs=[pl.BlockSpec(memory_space=s...]
where the time goes in v4:
time: 37.8 us; the launch traced here: 37.7 us
  starting transfers between devices  20.7 us (55%)
  waiting for transfers between devices  9.94 us (26%)
  Pallas kernels  6.26 us (17%)
  between operations  0.73 us (2%)
    ppermute x14, starting transfers between devices, exchange(): return lax.ppermute(array, axis, [(i, i ^ flip) for i in range(devices)])  15.2 us
    ppermute x14, waiting for transfers between devices, exchange(): return lax.ppermute(array, axis, [(i, i ^ flip) for i in range(devices)])  9.94 us
    pallas_call x11, Pallas kernels, call(): pl.pallas_call(body, out_shape=out, in_specs=[pl.BlockSpec(memory_space=s...  6.26 us
    ppermute x3, starting transfers between devices, all_blocks(): lax.ppermute(array, 'blk', [(i, (i + by) % blocks) for i in range(blocks)])  5.57 us
  transfers between devices with their start and end apart: 17, of which 9 were waited for; matrix products, arithmetic and copies ran while one was open for 0% of the time, Pallas kernels for 12%

profile of v4, /device:TPU:0, one launch (start us, length us, event | category | flops | bytes accessed | tf_op | source)
XLA Modules:
  0.0 37.7 jit_solution(15005031139235678100)
XLA Ops:
  0.6 0.5 %collective-permute-start = (bf16[144,1152]{1,0:T(8,128)(2,1)}, bf16[144,1152]{1,0:T(8,128)(2,1)S(1)}, u32[]{:S(2)}, u32[]{:S(2)}) collective-permute-start(bf16[144,1152]{1,0:T(8,128)(2,1)} %w_key_hbm.1), channel_id=1, source_target_pairs={{0,4},{4,0},{8,12},{12,8},{16,20},{20,16},{24,28},{28,24},{1,5},{5... | collective-permute-start | bytes 995336 | tf_op jit(solution)/shard_map/ppermute | solution.py:233
  1.2 1.4 %shard_map.78 = (f32[16,144]{1,0:T(8,128)S(1)}, bf16[16,1152]{1,0:T(8,128)(2,1)S(1)}, bf16[4,16,2592]{2,1,0:T(8,128)(2,1)S(1)}) custom-call(bf16[1152]{0:T(1024)(128)(2,1)} %probe_hbm.1, bf16[144,1152]{1,0:T(8,128)(2,1)} %w_key_hbm.1, bf16[144,1152]{1,0:T(8,128)(2,1)} %w_value_hbm.1), custom_call_target="tpu_custom_call" | custom-call | tf_op jit(solution)/shard_map/pallas_call | solution.py:22
  3.1 2.7 %collective-permute-start.1 = (bf16[16,3456]{1,0:T(8,128)(2,1)S(1)}, bf16[16,3456]{1,0:T(8,128)(2,1)S(1)}, u32[]{:S(2)}, u32[]{:S(2)}) collective-permute-start(bf16[16,3456]{1,0:T(8,128)(2,1)S(1)} %get-tuple-element.29), channel_id=1, source_target_pairs={{0,12},{4,8},{8,4},{12,0},{16,28},{20,24},{24,20},{28,16},{1,13},{... | collective-permute-start | bytes 331784 | tf_op jit(solution)/shard_map/ppermute | solution.py:233
  5.7 1.5 %collective-permute-start.2 = (bf16[16,3456]{1,0:T(8,128)(2,1)S(1)}, bf16[16,3456]{1,0:T(8,128)(2,1)S(1)}, u32[]{:S(2)}, u32[]{:S(2)}) collective-permute-start(bf16[16,3456]{1,0:T(8,128)(2,1)S(1)} %get-tuple-element.30), channel_id=1, source_target_pairs={{0,20},{4,16},{8,28},{12,24},{16,4},{20,0},{24,12},{28,8},{1,21},{... | collective-permute-start | bytes 331784 | tf_op jit(solution)/shard_map/ppermute | solution.py:233
  7.3 1.9 %collective-permute-done.1.refs_1_ = bf16[16,3456]{1,0:T(8,128)(2,1)S(1)} collective-permute-done((bf16[16,3456]{1,0:T(8,128)(2,1)S(1)}, bf16[16,3456]{1,0:T(8,128)(2,1)S(1)}, u32[]{:S(2)}, u32[]{:S(2)}) %collective-permute-start.1) | collective-permute-done | bytes 110624 | tf_op jit(solution)/shard_map/ppermute | solution.py:233
  9.2 3.3 %collective-permute-done.2.refs_2_ = bf16[16,3456]{1,0:T(8,128)(2,1)S(1)} collective-permute-done((bf16[16,3456]{1,0:T(8,128)(2,1)S(1)}, bf16[16,3456]{1,0:T(8,128)(2,1)S(1)}, u32[]{:S(2)}, u32[]{:S(2)}) %collective-permute-start.2) | collective-permute-done | bytes 110624 | tf_op jit(solution)/shard_map/ppermute | solution.py:233
  12.5 0.6 %collective-permute-done.3.refs_3_ = bf16[16,3456]{1,0:T(8,128)(2,1)S(1)} collective-permute-done((bf16[16,3456]{1,0:T(8,128)(2,1)S(1)}, bf16[16,3456]{1,0:T(8,128)(2,1)S(1)}, u32[]{:S(2)}, u32[]{:S(2)}) %collective-permute-start.3) | collective-permute-done | bytes 110624 | tf_op jit(solution)/shard_map/ppermute | solution.py:233
  13.8 0.9 %shard_map.80 = (bf16[2,16,1152]{2,1,0:T(8,128)(2,1)S(1)}, bf16[2,16,1152]{2,1,0:T(8,128)(2,1)S(1)}, bf16[2,16,1152]{2,1,0:T(8,128)(2,1)S(1)}, bf16[2,16,1152]{2,1,0:T(8,128)(2,1)S(1)}) custom-call(bf16[512,1152]{1,0:T(8,128)(2,1)S(1)} %bitcast.2, bf16[1152,512]{1,0:T(8,128)(2,1)S(1)} %shard_map.77.turned_ref, ...), custom_call_target="tpu_custom_call" | custom-call | tf_op jit(solution)/shard_map/pallas_call | solution.py:22
  14.8 1.2 %collective-permute-start.4 = (bf16[2,16,1152]{2,1,0:T(8,128)(2,1)S(1)}, bf16[2,16,1152]{2,1,0:T(8,128)(2,1)S(1)}, u32[]{:S(2)}, u32[]{:S(2)}) collective-permute-start(bf16[2,16,1152]{2,1,0:T(8,128)(2,1)S(1)} %get-tuple-element.33), channel_id=1, source_target_pairs={{0,12},{4,8},{8,4},{12,0},{16,28},{20,24},{24,20},{28,16},{1,13},{... | collective-permute-start | bytes 221192 | tf_op jit(solution)/shard_map/ppermute | solution.py:233
  16.0 0.6 %collective-permute-start.5 = (bf16[2,16,1152]{2,1,0:T(8,128)(2,1)S(1)}, bf16[2,16,1152]{2,1,0:T(8,128)(2,1)S(1)}, u32[]{:S(2)}, u32[]{:S(2)}) collective-permute-start(bf16[2,16,1152]{2,1,0:T(8,128)(2,1)S(1)} %get-tuple-element.34), channel_id=1, source_target_pairs={{0,20},{4,16},{8,28},{12,24},{16,4},{20,0},{24,12},{28,8},{1,21},{... | collective-permute-start | bytes 221192 | tf_op jit(solution)/shard_map/ppermute | solution.py:233
  16.6 1.4 %collective-permute-start.6 = (bf16[2,16,1152]{2,1,0:T(8,128)(2,1)S(1)}, bf16[2,16,1152]{2,1,0:T(8,128)(2,1)S(1)}, u32[]{:S(2)}, u32[]{:S(2)}) collective-permute-start(bf16[2,16,1152]{2,1,0:T(8,128)(2,1)S(1)} %get-tuple-element.35), channel_id=1, source_target_pairs={{0,28},{4,24},{8,20},{12,16},{16,12},{20,8},{24,4},{28,0},{1,29},{... | collective-permute-start | bytes 221192 | tf_op jit(solution)/shard_map/ppermute | solution.py:233
  18.0 1.6 %collective-permute-start.11 = (bf16[8,1152]{1,0:T(8,128)(2,1)S(1)}, bf16[8,1152]{1,0:T(8,128)(2,1)S(1)}, u32[]{:S(2)}, u32[]{:S(2)}) collective-permute-start(bf16[8,1152]{1,0:T(8,128)(2,1)S(1)} %copy-done.2), channel_id=1, source_target_pairs={{0,1},{1,2},{2,3},{3,0},{4,5},{5,6},{6,7},{7,4},{8,9},{9,10},{10,1... | collective-permute-start | bytes 55304 | tf_op jit(solution)/shard_map/ppermute | solution.py:238
  19.6 2.6 %collective-permute-start.12 = (bf16[8,1152]{1,0:T(8,128)(2,1)S(1)}, bf16[8,1152]{1,0:T(8,128)(2,1)S(1)}, u32[]{:S(2)}, u32[]{:S(2)}) collective-permute-start(bf16[8,1152]{1,0:T(8,128)(2,1)S(1)} %copy-done.2), channel_id=1, source_target_pairs={{0,2},{1,3},{2,0},{3,1},{4,6},{5,7},{6,4},{7,5},{8,10},{9,11},{10,... | collective-permute-start | bytes 55304 | tf_op jit(solution)/shard_map/ppermute | solution.py:238
  22.5 1.4 %collective-permute-start.13 = (bf16[8,1152]{1,0:T(8,128)(2,1)S(1)}, bf16[8,1152]{1,0:T(8,128)(2,1)S(1)}, u32[]{:S(2)}, u32[]{:S(2)}) collective-permute-start(bf16[8,1152]{1,0:T(8,128)(2,1)S(1)} %copy-done.2), channel_id=1, source_target_pairs={{0,3},{1,0},{2,1},{3,2},{4,7},{5,4},{6,5},{7,6},{8,11},{9,8},{10,9... | collective-permute-start | bytes 55304 | tf_op jit(solution)/shard_map/ppermute | solution.py:238
  24.0 0.5 %shard_map.83 = (bf16[8,1152]{1,0:T(8,128)(2,1)S(1)}, bf16[8,1152]{1,0:T(8,128)(2,1)S(1)}, bf16[8,1152]{1,0:T(8,128)(2,1)S(1)}, bf16[8,1152]{1,0:T(8,128)(2,1)S(1)}) custom-call(bf16[2,16,1152]{2,1,0:T(8,128)(2,1)S(1)} %get-tuple-element.32.refs_0_, bf16[2,16,1152]{2,1,0:T(8,128)(2,1)S(1)} %collective-permute-done.4.refs_1_, ...), custom_call_target="tpu_custom_call" | custom-call | tf_op jit(solution)/shard_map/pallas_call | solution.py:22
  24.7 1.4 %collective-permute-start.9 = (bf16[8,1152]{1,0:T(8,128)(2,1)S(1)}, bf16[8,1152]{1,0:T(8,128)(2,1)S(1)}, u32[]{:S(2)}, u32[]{:S(2)}) collective-permute-start(bf16[8,1152]{1,0:T(8,128)(2,1)S(1)} %get-tuple-element.40), channel_id=1, source_target_pairs={{0,20},{4,16},{8,28},{12,24},{16,4},{20,0},{24,12},{28,8},{1,21},{... | collective-permute-start | bytes 55304 | tf_op jit(solution)/shard_map/ppermute | solution.py:233
  26.1 1.0 %collective-permute-start.10 = (bf16[8,1152]{1,0:T(8,128)(2,1)S(1)}, bf16[8,1152]{1,0:T(8,128)(2,1)S(1)}, u32[]{:S(2)}, u32[]{:S(2)}) collective-permute-start(bf16[8,1152]{1,0:T(8,128)(2,1)S(1)} %get-tuple-element.41), channel_id=1, source_target_pairs={{0,28},{4,24},{8,20},{12,16},{16,12},{20,8},{24,4},{28,0},{1,29},{... | collective-permute-start | bytes 55304 | tf_op jit(solution)/shard_map/ppermute | solution.py:233
  27.9 2.4 %collective-permute-done.10.refs_3_ = bf16[8,1152]{1,0:T(8,128)(2,1)S(1)} collective-permute-done((bf16[8,1152]{1,0:T(8,128)(2,1)S(1)}, bf16[8,1152]{1,0:T(8,128)(2,1)S(1)}, u32[]{:S(2)}, u32[]{:S(2)}) %collective-permute-start.10) | collective-permute-done | bytes 18464 | tf_op jit(solution)/shard_map/ppermute | solution.py:233
  30.3 1.5 %collective-permute-start.14 = (bf16[8,1152]{1,0:T(8,128)(2,1)S(1)}, bf16[8,1152]{1,0:T(8,128)(2,1)S(1)}, u32[]{:S(2)}, u32[]{:S(2)}) collective-permute-start(bf16[8,1152]{1,0:T(8,128)(2,1)S(1)} %get-tuple-element.47.refs_0_), channel_id=1, source_target_pairs={{0,3},{1,2},{2,1},{3,0},{4,7},{5,6},{6,5},{7,4},{8,11},{9,10},{10,... | collective-permute-start | bytes 55304 | tf_op jit(solution)/shard_map/ppermute | solution.py:233
  31.8 0.7 %collective-permute-start.15 = (bf16[8,1152]{1,0:T(8,128)(2,1)S(1)}, bf16[8,1152]{1,0:T(8,128)(2,1)S(1)}, u32[]{:S(2)}, u32[]{:S(2)}) collective-permute-start(bf16[8,1152]{1,0:T(8,128)(2,1)S(1)} %get-tuple-element.47.refs_0_), channel_id=1, source_target_pairs={{0,2},{1,3},{2,0},{3,1},{4,6},{5,7},{6,4},{7,5},{8,10},{9,11},{10,... | collective-permute-start | bytes 55304 | tf_op jit(solution)/shard_map/ppermute | solution.py:233
  32.5 2.2 %collective-permute-start.16 = (bf16[8,1152]{1,0:T(8,128)(2,1)S(1)}, bf16[8,1152]{1,0:T(8,128)(2,1)S(1)}, u32[]{:S(2)}, u32[]{:S(2)}) collective-permute-start(bf16[8,1152]{1,0:T(8,128)(2,1)S(1)} %get-tuple-element.47.refs_0_), channel_id=1, source_target_pairs={{0,1},{1,0},{2,3},{3,2},{4,5},{5,4},{6,7},{7,6},{8,9},{9,8},{10,11... | collective-permute-start | bytes 55304 | tf_op jit(solution)/shard_map/ppermute | solution.py:233
  34.7 1.0 %shard_map.86 = f32[8,1152]{1,0:T(8,128)} custom-call(f32[8,1152]{1,0:T(8,128)S(1)} %get-tuple-element.43.unit_ref, f32[8,128]{1,0:T(8,128)S(1)} %get-tuple-element.44.inverse_ref, bf16[32,1152]{1,0:T(8,128)(2,1)S(1)} %get-tuple-element.45.refs_0_), custom_call_target="tpu_custom_call" | custom-call | tf_op jit(solution)/shard_map/pallas_call | solution.py:22
  35.9 0.6 %collective-permute-done.15.refs_2_ = bf16[8,1152]{1,0:T(8,128)(2,1)S(1)} collective-permute-done((bf16[8,1152]{1,0:T(8,128)(2,1)S(1)}, bf16[8,1152]{1,0:T(8,128)(2,1)S(1)}, u32[]{:S(2)}, u32[]{:S(2)}) %collective-permute-start.15) | collective-permute-done | bytes 18464 | tf_op jit(solution)/shard_map/ppermute | solution.py:233
  36.7 1.0 %shard_map.87 = f32[8,1152]{1,0:T(8,128)} custom-call(f32[8,1152]{1,0:T(8,128)S(1)} %get-tuple-element.46.unit_ref, f32[8,128]{1,0:T(8,128)S(1)} %get-tuple-element.42.refs_4_.inverse_ref, bf16[8,1152]{1,0:T(8,128)(2,1)S(1)} %get-tuple-element.47.refs_0_, bf16[8,1152]{1,0:T(8,128)(2,1)S(1)} %collective-permute-done.14.refs_1_, ...), custom_call_target="tpu_custom_call" | custom-call | tf_op jit(solution)/shard_map/pallas_call | solution.py:22
  (27 shorter events, 2.9 us)
Async XLA Ops:
  0.6 12.5 %copy-start.1 = (bf16[144,1152]{1,0:T(8,128)(2,1)S(1)}, bf16[144,1152]{1,0:T(8,128)(2,1)}, u32[]{:S(2)}) copy-start(bf16[144,1152]{1,0:T(8,128)(2,1)} %refs_4_.3) | copy-start | bytes 995332
  0.6 2.0 %collective-permute-start = (bf16[144,1152]{1,0:T(8,128)(2,1)}, bf16[144,1152]{1,0:T(8,128)(2,1)S(1)}, u32[]{:S(2)}, u32[]{:S(2)}) collective-permute-start(bf16[144,1152]{1,0:T(8,128)(2,1)} %w_key_hbm.1), channel_id=1, source_target_pairs={{0,4},{4,0},{8,12},{12,8},{16,20},{20,16},{24,28},{28,24},{1,5},{5... | collective-permute-start | bytes 995336 | tf_op jit(solution)/shard_map/ppermute | solution.py:233
  2.6 10.9 %copy-start = (bf16[8,64,1152]{2,1,0:T(8,128)(2,1)S(1)}, bf16[8,64,1152]{2,1,0:T(8,128)(2,1)}, u32[]{:S(2)}) copy-start(bf16[8,64,1152]{2,1,0:T(8,128)(2,1)} %param.6) | copy-start | bytes 3538948
  3.1 6.1 %collective-permute-start.1 = (bf16[16,3456]{1,0:T(8,128)(2,1)S(1)}, bf16[16,3456]{1,0:T(8,128)(2,1)S(1)}, u32[]{:S(2)}, u32[]{:S(2)}) collective-permute-start(bf16[16,3456]{1,0:T(8,128)(2,1)S(1)} %get-tuple-element.29), channel_id=1, source_target_pairs={{0,12},{4,8},{8,4},{12,0},{16,28},{20,24},{24,20},{28,16},{1,13},{... | collective-permute-start | bytes 331784 | tf_op jit(solution)/shard_map/ppermute | solution.py:233
  5.7 6.8 %collective-permute-start.2 = (bf16[16,3456]{1,0:T(8,128)(2,1)S(1)}, bf16[16,3456]{1,0:T(8,128)(2,1)S(1)}, u32[]{:S(2)}, u32[]{:S(2)}) collective-permute-start(bf16[16,3456]{1,0:T(8,128)(2,1)S(1)} %get-tuple-element.30), channel_id=1, source_target_pairs={{0,20},{4,16},{8,28},{12,24},{16,4},{20,0},{24,12},{28,8},{1,21},{... | collective-permute-start | bytes 331784 | tf_op jit(solution)/shard_map/ppermute | solution.py:233
  7.2 5.9 %collective-permute-start.3 = (bf16[16,3456]{1,0:T(8,128)(2,1)S(1)}, bf16[16,3456]{1,0:T(8,128)(2,1)S(1)}, u32[]{:S(2)}, u32[]{:S(2)}) collective-permute-start(bf16[16,3456]{1,0:T(8,128)(2,1)S(1)} %get-tuple-element.31), channel_id=1, source_target_pairs={{0,28},{4,24},{8,20},{12,16},{16,12},{20,8},{24,4},{28,0},{1,29},{... | collective-permute-start | bytes 331784 | tf_op jit(solution)/shard_map/ppermute | solution.py:233
  13.2 6.4 %collective-permute-start.7 = (bf16[9,16,2592]{2,1,0:T(8,128)(2,1)S(1)}, bf16[9,16,2592]{2,1,0:T(8,128)(2,1)S(1)}, u32[]{:S(2)}, u32[]{:S(2)}) collective-permute-start(bf16[9,16,2592]{2,1,0:T(8,128)(2,1)S(1)} %shard_map.81), channel_id=1, source_target_pairs={{0,4},{4,0},{8,12},{12,8},{16,20},{20,16},{24,28},{28,24},{1,5},{5... | collective-permute-start | bytes 2239496 | tf_op jit(solution)/shard_map/ppermute | solution.py:233
  13.8 4.2 %copy-start.2 = (bf16[8,1152]{1,0:T(8,128)(2,1)S(1)}, bf16[8,1152]{1,0:T(8,128)(2,1)}, u32[]{:S(2)}) copy-start(bf16[8,1152]{1,0:T(8,128)(2,1)} %refs_0_.1) | copy-start | bytes 55300
  14.8 7.8 %collective-permute-start.4 = (bf16[2,16,1152]{2,1,0:T(8,128)(2,1)S(1)}, bf16[2,16,1152]{2,1,0:T(8,128)(2,1)S(1)}, u32[]{:S(2)}, u32[]{:S(2)}) collective-permute-start(bf16[2,16,1152]{2,1,0:T(8,128)(2,1)S(1)} %get-tuple-element.33), channel_id=1, source_target_pairs={{0,12},{4,8},{8,4},{12,0},{16,28},{20,24},{24,20},{28,16},{1,13},{... | collective-permute-start | bytes 221192 | tf_op jit(solution)/shard_map/ppermute | solution.py:233
  16.0 7.9 %collective-permute-start.5 = (bf16[2,16,1152]{2,1,0:T(8,128)(2,1)S(1)}, bf16[2,16,1152]{2,1,0:T(8,128)(2,1)S(1)}, u32[]{:S(2)}, u32[]{:S(2)}) collective-permute-start(bf16[2,16,1152]{2,1,0:T(8,128)(2,1)S(1)} %get-tuple-element.34), channel_id=1, source_target_pairs={{0,20},{4,16},{8,28},{12,24},{16,4},{20,0},{24,12},{28,8},{1,21},{... | collective-permute-start | bytes 221192 | tf_op jit(solution)/shard_map/ppermute | solution.py:233
  16.6 7.3 %collective-permute-start.6 = (bf16[2,16,1152]{2,1,0:T(8,128)(2,1)S(1)}, bf16[2,16,1152]{2,1,0:T(8,128)(2,1)S(1)}, u32[]{:S(2)}, u32[]{:S(2)}) collective-permute-start(bf16[2,16,1152]{2,1,0:T(8,128)(2,1)S(1)} %get-tuple-element.35), channel_id=1, source_target_pairs={{0,28},{4,24},{8,20},{12,16},{16,12},{20,8},{24,4},{28,0},{1,29},{... | collective-permute-start | bytes 221192 | tf_op jit(solution)/shard_map/ppermute | solution.py:233
  18.0 8.1 %collective-permute-start.11 = (bf16[8,1152]{1,0:T(8,128)(2,1)S(1)}, bf16[8,1152]{1,0:T(8,128)(2,1)S(1)}, u32[]{:S(2)}, u32[]{:S(2)}) collective-permute-start(bf16[8,1152]{1,0:T(8,128)(2,1)S(1)} %copy-done.2), channel_id=1, source_target_pairs={{0,1},{1,2},{2,3},{3,0},{4,5},{5,6},{6,7},{7,4},{8,9},{9,10},{10,1... | collective-permute-start | bytes 55304 | tf_op jit(solution)/shard_map/ppermute | solution.py:238
  19.6 7.5 %collective-permute-start.12 = (bf16[8,1152]{1,0:T(8,128)(2,1)S(1)}, bf16[8,1152]{1,0:T(8,128)(2,1)S(1)}, u32[]{:S(2)}, u32[]{:S(2)}) collective-permute-start(bf16[8,1152]{1,0:T(8,128)(2,1)S(1)} %copy-done.2), channel_id=1, source_target_pairs={{0,2},{1,3},{2,0},{3,1},{4,6},{5,7},{6,4},{7,5},{8,10},{9,11},{10,... | collective-permute-start | bytes 55304 | tf_op jit(solution)/shard_map/ppermute | solution.py:238
  22.5 4.6 %collective-permute-start.13 = (bf16[8,1152]{1,0:T(8,128)(2,1)S(1)}, bf16[8,1152]{1,0:T(8,128)(2,1)S(1)}, u32[]{:S(2)}, u32[]{:S(2)}) collective-permute-start(bf16[8,1152]{1,0:T(8,128)(2,1)S(1)} %copy-done.2), channel_id=1, source_target_pairs={{0,3},{1,0},{2,1},{3,2},{4,7},{5,4},{6,5},{7,6},{8,11},{9,8},{10,9... | collective-permute-start | bytes 55304 | tf_op jit(solution)/shard_map/ppermute | solution.py:238
  24.5 3.3 %collective-permute-start.8 = (bf16[8,1152]{1,0:T(8,128)(2,1)S(1)}, bf16[8,1152]{1,0:T(8,128)(2,1)S(1)}, u32[]{:S(2)}, u32[]{:S(2)}) collective-permute-start(bf16[8,1152]{1,0:T(8,128)(2,1)S(1)} %get-tuple-element.39), channel_id=1, source_target_pairs={{0,12},{4,8},{8,4},{12,0},{16,28},{20,24},{24,20},{28,16},{1,13},{... | collective-permute-start | bytes 55304 | tf_op jit(solution)/shard_map/ppermute | solution.py:233
  24.7 3.2 %collective-permute-start.9 = (bf16[8,1152]{1,0:T(8,128)(2,1)S(1)}, bf16[8,1152]{1,0:T(8,128)(2,1)S(1)}, u32[]{:S(2)}, u32[]{:S(2)}) collective-permute-start(bf16[8,1152]{1,0:T(8,128)(2,1)S(1)} %get-tuple-element.40), channel_id=1, source_target_pairs={{0,20},{4,16},{8,28},{12,24},{16,4},{20,0},{24,12},{28,8},{1,21},{... | collective-permute-start | bytes 55304 | tf_op jit(solution)/shard_map/ppermute | solution.py:233
  26.1 4.1 %collective-permute-start.10 = (bf16[8,1152]{1,0:T(8,128)(2,1)S(1)}, bf16[8,1152]{1,0:T(8,128)(2,1)S(1)}, u32[]{:S(2)}, u32[]{:S(2)}) collective-permute-start(bf16[8,1152]{1,0:T(8,128)(2,1)S(1)} %get-tuple-element.41), channel_id=1, source_target_pairs={{0,28},{4,24},{8,20},{12,16},{16,12},{20,8},{24,4},{28,0},{1,29},{... | collective-permute-start | bytes 55304 | tf_op jit(solution)/shard_map/ppermute | solution.py:233
  30.3 5.6 %collective-permute-start.14 = (bf16[8,1152]{1,0:T(8,128)(2,1)S(1)}, bf16[8,1152]{1,0:T(8,128)(2,1)S(1)}, u32[]{:S(2)}, u32[]{:S(2)}) collective-permute-start(bf16[8,1152]{1,0:T(8,128)(2,1)S(1)} %get-tuple-element.47.refs_0_), channel_id=1, source_target_pairs={{0,3},{1,2},{2,1},{3,0},{4,7},{5,6},{6,5},{7,4},{8,11},{9,10},{10,... | collective-permute-start | bytes 55304 | tf_op jit(solution)/shard_map/ppermute | solution.py:233
  31.8 4.7 %collective-permute-start.15 = (bf16[8,1152]{1,0:T(8,128)(2,1)S(1)}, bf16[8,1152]{1,0:T(8,128)(2,1)S(1)}, u32[]{:S(2)}, u32[]{:S(2)}) collective-permute-start(bf16[8,1152]{1,0:T(8,128)(2,1)S(1)} %get-tuple-element.47.refs_0_), channel_id=1, source_target_pairs={{0,2},{1,3},{2,0},{3,1},{4,6},{5,7},{6,4},{7,5},{8,10},{9,11},{10,... | collective-permute-start | bytes 55304 | tf_op jit(solution)/shard_map/ppermute | solution.py:233
  32.5 4.2 %collective-permute-start.16 = (bf16[8,1152]{1,0:T(8,128)(2,1)S(1)}, bf16[8,1152]{1,0:T(8,128)(2,1)S(1)}, u32[]{:S(2)}, u32[]{:S(2)}) collective-permute-start(bf16[8,1152]{1,0:T(8,128)(2,1)S(1)} %get-tuple-element.47.refs_0_), channel_id=1, source_target_pairs={{0,1},{1,0},{2,3},{3,2},{4,5},{5,4},{6,7},{7,6},{8,9},{9,8},{10,11... | collective-permute-start | bytes 55304 | tf_op jit(solution)/shard_map/ppermute | solution.py:233

commit v5 on v4

--- a/solution.py
+++ b/solution.py
@@ -18,12 +18,13 @@
     return jax.ShapeDtypeStruct(shape, dtype)
 
 
-def call(body, out, *args, scratch=(), space=pltpu.VMEM):
+def call(body, out, *args, scratch=(), space=pltpu.VMEM, cost=None):
     return pl.pallas_call(
         body,
         out_shape=out,
         in_specs=[pl.BlockSpec(memory_space=space)] * len(args),
         scratch_shapes=scratch,
+        cost_estimate=cost and pl.CostEstimate(flops=cost, bytes_accessed=0, transcendentals=0),
         compiler_params=pltpu.CompilerParams(vmem_limit_bytes=24 * 2**20),
     )(*args)
 
@@ -66,11 +67,10 @@
     return place // CORES, lax.rem(place, CORES)
 
 
-def prepare_kernel(
-    probe_hbm, w_key_hbm, w_value_hbm, keys_ref, table_ref, blocks_ref, probe, w_key, w_value, sems
-):
+def prepare_kernel(chips, probe_hbm, w_key_hbm, w_value_hbm, *refs):
+    out_refs, (probe, w_key, w_value, blocks, sems) = refs[:chips], refs[chips:]
     part, width = w_key.shape
-    chips, rows, _ = blocks_ref.shape
+    _, rows, packed = blocks.shape
     copies = [
         pltpu.make_async_copy(source, target, sems.at[i])
         for i, (source, target) in enumerate(
@@ -84,35 +84,37 @@
     inside = (first >= 0) & (first < width // HEADS)
     copies[0].wait()
     table = jnp.where(inside, probe[...].astype(F32).reshape(1, width), 0.0).astype(BF16)
-    table_ref[...] = table
     copies[1].wait()
-    keys_ref[...] = nt(table, w_key[...])
+    keys = [
+        term[h * rows : (h + 1) * rows]
+        for term in split_terms(nt(table, w_key[...]))
+        for h in range(HEADS // rows)
+    ]
+    keys = jnp.concatenate(keys, axis=1)
     copies[2].wait()
     wide = width // chips
     for q in range(chips):
         columns = w_value[:, q * wide : (q + 1) * wide]
         pieces = [columns[j * rows : (j + 1) * rows] for j in range(part // rows)]
-        blocks_ref[q] = jnp.concatenate(pieces, axis=1)
-
-
-def keys_kernel(keys_ref, table_ref, blocks_ref, other_ref, *out_refs):
-    _, rows, packed = blocks_ref.shape
-    chip, core = chip_and_core()
-    own, other = keys_ref[...], nt(table_ref[...], other_ref[...])
-    keys = [jnp.where(core == 0, own, other), jnp.where(core == 0, other, own)]
-    keys = [
-        term[h * rows : (h + 1) * rows]
-        for term in split_terms(jnp.concatenate(keys, axis=1))
-        for h in range(HEADS // rows)
-    ]
-    keys = jnp.concatenate(keys, axis=1)
+        blocks[q] = jnp.concatenate(pieces, axis=1)
+    chip, _ = chip_and_core()
     for m, out_ref in enumerate(out_refs):
-        out_ref[:, :packed] = blocks_ref[chip ^ m]
+        out_ref[:, :packed] = blocks[chip ^ m]
         out_ref[:, packed:] = keys
 
 
+def pack_keys_kernel(chips, *refs):
+    length = refs[-1].shape[2]
+    for m in range(chips):
+        refs[-1][m] = refs[m][:, refs[m].shape[1] - length :]
+
+
+def turn_kernel(x_ref, _, out_ref):
+    out_ref[...] = x_ref[...].T
+
+
 def shard_kernel(chips, *refs):
-    w_out_ref, out_ref = refs[chips:]
+    w_out_ref, _, out_ref = refs[chips:]
     _, rows, length = out_ref.shape
     part, width = w_out_ref.shape
     for m in range(chips):
@@ -123,27 +125,24 @@
         out_ref[chips + j // fit, :, first : first + width] = w_out_ref[j * rows : (j + 1) * rows]
 
 
-def turn_kernel(x_ref, out_ref):
-    out_ref[...] = x_ref[...].T
-
-
-def attend_kernel(images, scaling, chips, x_ref, turned_ref, *refs):
-    parts, outs, (placed, table, every) = refs[:chips], refs[chips:-3], refs[-3:]
+def attend_kernel(images, scaling, chips, x_ref, own_ref, other_ref, *refs):
+    outs, (placed, table, every) = refs[:chips], refs[chips:]
     x = x_ref[...]
     width = x.shape[1]
     patches = x.shape[0] // images
-    rows, length = parts[0].shape
-    wide = width // chips
-    pieces = table.shape[0] // rows
-    chip, _ = chip_and_core()
+    _, rows, length = own_ref.shape
+    part = width // (chips * CORES)
+    chip, core = chip_and_core()
     for m in range(chips):
-        placed[chip ^ m] = parts[m][:, length - pieces * wide :]
-    for j in range(pieces):
-        for q in range(chips):
-            table[j * rows : (j + 1) * rows, q * wide : (q + 1) * wide] = placed[
-                q, :, j * wide : (j + 1) * wide
+        place = core if m == 0 else 1 - core
+        placed[chip ^ m, place] = own_ref[m]
+        placed[chip ^ m, 1 - place] = other_ref[m]
+    for j in range(length // part):
+        for k in range(chips * CORES):
+            table[j * rows : (j + 1) * rows, k * part : (k + 1) * part] = placed[
+                k // CORES, k % CORES, :, j * part : (j + 1) * part
             ]
-    parts = nn(table[...], turned_ref[...])
+    parts = nt(table[...], x)
     scores = (parts[:HEADS] + parts[HEADS : 2 * HEADS] + parts[2 * HEADS :]) * scaling
     image = lax.broadcasted_iota(jnp.int32, (images, x.shape[0]), 0)
     first = lax.broadcasted_iota(jnp.int32, (images, x.shape[0]), 1) - image * patches
@@ -261,48 +260,43 @@
     packed = part // rows * wide
     fit = packed // width
 
-    keys, table, columns = call(
-        prepare_kernel,
-        (
-            struct((HEADS, part), F32),
-            struct((HEADS, width), BF16),
-            struct((chips, rows, packed), BF16),
-        ),
+    length = 3 * HEADS // rows * part
+    parts = call(
+        functools.partial(prepare_kernel, chips),
+        [struct((rows, packed + length), BF16)] * chips,
         *[pltpu.with_memory_space_constraint(a, pltpu.HBM) for a in (probe, w_key, w_value)],
         scratch=[
             pltpu.VMEM(probe.shape, BF16),
             pltpu.VMEM(w_key.shape, BF16),
             pltpu.VMEM(w_value.shape, BF16),
+            pltpu.VMEM((chips, rows, packed), BF16),
             pltpu.SemaphoreType.DMA((3,)),
         ],
         space=pltpu.HBM,
     )
-    parts = call(
-        keys_kernel,
-        [struct((rows, packed + 3 * HEADS // rows * wide), BF16)] * chips,
-        keys,
-        table,
-        columns,
-        exchange(w_key, devices, 1),
-    )
     parts = exchange_chips(parts, devices)
-    mixed = call(
-        functools.partial(attend_kernel, images, scaling, chips),
-        [struct((CORES, rows, width), BF16)] * chips,
-        flat,
-        call(turn_kernel, struct(flat.shape[::-1], BF16), flat),
-        *parts,
-        scratch=[
-            pltpu.VMEM((chips, rows, 3 * HEADS // rows * wide), BF16),
-            pltpu.VMEM((3 * HEADS, width), BF16),
-            pltpu.VMEM((chips, CORES, rows, width), BF16),
-        ],
+    keys = call(
+        functools.partial(pack_keys_kernel, chips), struct((chips, rows, length), BF16), *parts
     )
     shard = call(
         functools.partial(shard_kernel, chips),
         struct((chips + pl.cdiv(part // rows, fit), rows, packed), BF16),
         *parts,
         w_out,
+        keys,
+    )
+    mixed = call(
+        functools.partial(attend_kernel, images, scaling, chips),
+        [struct((CORES, rows, width), BF16)] * chips,
+        flat,
+        keys,
+        exchange(keys, devices, 1),
+        cost=10000000000,
+        scratch=[
+            pltpu.VMEM((chips, CORES, rows, length), BF16),
+            pltpu.VMEM((3 * HEADS, width), BF16),
+            pltpu.VMEM((chips, CORES, rows, width), BF16),
+        ],
     )
     w_values, w_outs = call(
         functools.partial(unpack_kernel, chips),

time: 37.8 us -> 37.3 us (0.987)
  Pallas kernels: 6.26 us -> 5.77 us
  waiting for transfers between devices: 9.94 us -> 10.4 us
  starting transfers between devices: 20.7 us -> 20.3 us
    pallas_call x11 -> x10, Pallas kernels: 6.26 us -> 5.77 us  [call(): pl.pallas_call(body, out_shape=out, in_specs=[pl.BlockSpec(memory_space=s...]
    ppermute x14, starting transfers between devices: 15.2 us -> 14.7 us  [exchange(): return lax.ppermute(array, axis, [(i, i ^ flip) for i in range(devices)])]
    ppermute x14, waiting for transfers between devices: 9.94 us -> 10.4 us  [exchange(): return lax.ppermute(array, axis, [(i, i ^ flip) for i in range(devices)])]
  transfers between devices with their start and end apart: 17 -> 17, of which waited for: 9 -> 8; matrix products, arithmetic and copies ran while one was open for 0% -> 0% of each run, Pallas kernels for 12% -> 8%
where the time goes in v5:
time: 37.3 us; the launch traced here: 37.2 us
  starting transfers between devices  20.3 us (54%)
  waiting for transfers between devices  10.4 us (28%)
  Pallas kernels  5.77 us (15%)
  between operations  0.72 us (2%)
    ppermute x14, starting transfers between devices, exchange(): return lax.ppermute(array, axis, [(i, i ^ flip) for i in range(devices)])  14.7 us
    ppermute x14, waiting for transfers between devices, exchange(): return lax.ppermute(array, axis, [(i, i ^ flip) for i in range(devices)])  10.4 us
    pallas_call x10, Pallas kernels, call(): pl.pallas_call(body, out_shape=out, in_specs=[pl.BlockSpec(memory_space=s...  5.77 us
    ppermute x3, starting transfers between devices, all_blocks(): lax.ppermute(array, 'blk', [(i, (i + by) % blocks) for i in range(blocks)])  5.56 us
  transfers between devices with their start and end apart: 17, of which 8 were waited for; matrix products, arithmetic and copies ran while one was open for 0% of the time, Pallas kernels for 8%

profile of v5, /device:TPU:0, one launch (start us, length us, event | category | flops | bytes accessed | tf_op | source)
XLA Modules:
  0.0 37.2 jit_solution(8839187904065124072)
XLA Ops:
  0.6 1.6 %shard_map.77 = (bf16[16,3024]{1,0:T(8,128)(2,1)S(1)}, bf16[16,3024]{1,0:T(8,128)(2,1)S(1)}, bf16[16,3024]{1,0:T(8,128)(2,1)S(1)}, bf16[16,3024]{1,0:T(8,128)(2,1)S(1)}) custom-call(bf16[1152]{0:T(1024)(128)(2,1)} %probe_hbm.1, bf16[144,1152]{1,0:T(8,128)(2,1)} %w_key_hbm.1, bf16[144,1152]{1,0:T(8,128)(2,1)} %w_value_hbm.1), custom_call_target="tpu_custom_call" | custom-call | tf_op jit(solution)/shard_map/pallas_call | solution.py:22
  2.2 2.4 %collective-permute-start = (bf16[16,3024]{1,0:T(8,128)(2,1)S(1)}, bf16[16,3024]{1,0:T(8,128)(2,1)S(1)}, u32[]{:S(2)}, u32[]{:S(2)}) collective-permute-start(bf16[16,3024]{1,0:T(8,128)(2,1)S(1)} %get-tuple-element.23), channel_id=1, source_target_pairs={{0,12},{4,8},{8,4},{12,0},{16,28},{20,24},{24,20},{28,16},{1,13},{... | collective-permute-start | bytes 290312 | tf_op jit(solution)/shard_map/ppermute | solution.py:232
  4.7 1.8 %collective-permute-start.1 = (bf16[16,3024]{1,0:T(8,128)(2,1)S(1)}, bf16[16,3024]{1,0:T(8,128)(2,1)S(1)}, u32[]{:S(2)}, u32[]{:S(2)}) collective-permute-start(bf16[16,3024]{1,0:T(8,128)(2,1)S(1)} %get-tuple-element.24), channel_id=1, source_target_pairs={{0,20},{4,16},{8,28},{12,24},{16,4},{20,0},{24,12},{28,8},{1,21},{... | collective-permute-start | bytes 290312 | tf_op jit(solution)/shard_map/ppermute | solution.py:232
  6.5 1.4 %collective-permute-done.refs_1_ = bf16[16,3024]{1,0:T(8,128)(2,1)S(1)} collective-permute-done((bf16[16,3024]{1,0:T(8,128)(2,1)S(1)}, bf16[16,3024]{1,0:T(8,128)(2,1)S(1)}, u32[]{:S(2)}, u32[]{:S(2)}) %collective-permute-start) | collective-permute-done | bytes 96800 | tf_op jit(solution)/shard_map/ppermute | solution.py:232
  7.9 3.1 %collective-permute-done.1.refs_2_ = bf16[16,3024]{1,0:T(8,128)(2,1)S(1)} collective-permute-done((bf16[16,3024]{1,0:T(8,128)(2,1)S(1)}, bf16[16,3024]{1,0:T(8,128)(2,1)S(1)}, u32[]{:S(2)}, u32[]{:S(2)}) %collective-permute-start.1) | collective-permute-done | bytes 96800 | tf_op jit(solution)/shard_map/ppermute | solution.py:232
  10.9 1.5 %collective-permute-done.2.refs_3_ = bf16[16,3024]{1,0:T(8,128)(2,1)S(1)} collective-permute-done((bf16[16,3024]{1,0:T(8,128)(2,1)S(1)}, bf16[16,3024]{1,0:T(8,128)(2,1)S(1)}, u32[]{:S(2)}, u32[]{:S(2)}) %collective-permute-start.2) | collective-permute-done | bytes 96800 | tf_op jit(solution)/shard_map/ppermute | solution.py:232
  13.2 0.6 %collective-permute-done.3.other_ref = bf16[4,16,432]{2,1,0:T(8,128)(2,1)S(1)} collective-permute-done((bf16[4,16,432]{2,1,0:T(8,128)(2,1)S(1)}, bf16[4,16,432]{2,1,0:T(8,128)(2,1)S(1)}, u32[]{:S(2)}, u32[]{:S(2)}) %collective-permute-start.3) | collective-permute-done | bytes 55328 | tf_op jit(solution)/shard_map/ppermute | solution.py:232
  13.9 1.0 %shard_map.79 = (bf16[2,16,1152]{2,1,0:T(8,128)(2,1)S(1)}, bf16[2,16,1152]{2,1,0:T(8,128)(2,1)S(1)}, bf16[2,16,1152]{2,1,0:T(8,128)(2,1)S(1)}, bf16[2,16,1152]{2,1,0:T(8,128)(2,1)S(1)}) custom-call(bf16[512,1152]{1,0:T(8,128)(2,1)S(1)} %bitcast.1, bf16[4,16,432]{2,1,0:T(8,128)(2,1)S(1)} %shard_map.78.own_ref.refs_5_, ...), custom_call_target="tpu_custom_call" | custom-call | flops 10000000000 | tf_op jit(solution)/shard_map/pallas_call | solution.py:22
  14.9 0.8 %collective-permute-start.4 = (bf16[2,16,1152]{2,1,0:T(8,128)(2,1)S(1)}, bf16[2,16,1152]{2,1,0:T(8,128)(2,1)S(1)}, u32[]{:S(2)}, u32[]{:S(2)}) collective-permute-start(bf16[2,16,1152]{2,1,0:T(8,128)(2,1)S(1)} %get-tuple-element.27), channel_id=1, source_target_pairs={{0,12},{4,8},{8,4},{12,0},{16,28},{20,24},{24,20},{28,16},{1,13},{... | collective-permute-start | bytes 221192 | tf_op jit(solution)/shard_map/ppermute | solution.py:232
  15.6 0.6 %collective-permute-start.5 = (bf16[2,16,1152]{2,1,0:T(8,128)(2,1)S(1)}, bf16[2,16,1152]{2,1,0:T(8,128)(2,1)S(1)}, u32[]{:S(2)}, u32[]{:S(2)}) collective-permute-start(bf16[2,16,1152]{2,1,0:T(8,128)(2,1)S(1)} %get-tuple-element.28), channel_id=1, source_target_pairs={{0,20},{4,16},{8,28},{12,24},{16,4},{20,0},{24,12},{28,8},{1,21},{... | collective-permute-start | bytes 221192 | tf_op jit(solution)/shard_map/ppermute | solution.py:232
  16.2 1.7 %collective-permute-start.6 = (bf16[2,16,1152]{2,1,0:T(8,128)(2,1)S(1)}, bf16[2,16,1152]{2,1,0:T(8,128)(2,1)S(1)}, u32[]{:S(2)}, u32[]{:S(2)}) collective-permute-start(bf16[2,16,1152]{2,1,0:T(8,128)(2,1)S(1)} %get-tuple-element.29), channel_id=1, source_target_pairs={{0,28},{4,24},{8,20},{12,16},{16,12},{20,8},{24,4},{28,0},{1,29},{... | collective-permute-start | bytes 221192 | tf_op jit(solution)/shard_map/ppermute | solution.py:232
  17.9 1.6 %collective-permute-start.11 = (bf16[8,1152]{1,0:T(8,128)(2,1)S(1)}, bf16[8,1152]{1,0:T(8,128)(2,1)S(1)}, u32[]{:S(2)}, u32[]{:S(2)}) collective-permute-start(bf16[8,1152]{1,0:T(8,128)(2,1)S(1)} %copy-done.1), channel_id=1, source_target_pairs={{0,1},{1,2},{2,3},{3,0},{4,5},{5,6},{6,7},{7,4},{8,9},{9,10},{10,1... | collective-permute-start | bytes 55304 | tf_op jit(solution)/shard_map/ppermute | solution.py:237
  19.5 2.6 %collective-permute-start.12 = (bf16[8,1152]{1,0:T(8,128)(2,1)S(1)}, bf16[8,1152]{1,0:T(8,128)(2,1)S(1)}, u32[]{:S(2)}, u32[]{:S(2)}) collective-permute-start(bf16[8,1152]{1,0:T(8,128)(2,1)S(1)} %copy-done.1), channel_id=1, source_target_pairs={{0,2},{1,3},{2,0},{3,1},{4,6},{5,7},{6,4},{7,5},{8,10},{9,11},{10,... | collective-permute-start | bytes 55304 | tf_op jit(solution)/shard_map/ppermute | solution.py:237
  22.5 1.4 %collective-permute-start.13 = (bf16[8,1152]{1,0:T(8,128)(2,1)S(1)}, bf16[8,1152]{1,0:T(8,128)(2,1)S(1)}, u32[]{:S(2)}, u32[]{:S(2)}) collective-permute-start(bf16[8,1152]{1,0:T(8,128)(2,1)S(1)} %copy-done.1), channel_id=1, source_target_pairs={{0,3},{1,0},{2,1},{3,2},{4,7},{5,4},{6,5},{7,6},{8,11},{9,8},{10,9... | collective-permute-start | bytes 55304 | tf_op jit(solution)/shard_map/ppermute | solution.py:237
  23.9 0.5 %shard_map.82 = (bf16[8,1152]{1,0:T(8,128)(2,1)S(1)}, bf16[8,1152]{1,0:T(8,128)(2,1)S(1)}, bf16[8,1152]{1,0:T(8,128)(2,1)S(1)}, bf16[8,1152]{1,0:T(8,128)(2,1)S(1)}) custom-call(bf16[2,16,1152]{2,1,0:T(8,128)(2,1)S(1)} %get-tuple-element.26.refs_0_, bf16[2,16,1152]{2,1,0:T(8,128)(2,1)S(1)} %collective-permute-done.4.refs_1_, ...), custom_call_target="tpu_custom_call" | custom-call | tf_op jit(solution)/shard_map/pallas_call | solution.py:22
  24.5 1.7 %collective-permute-start.8 = (bf16[8,1152]{1,0:T(8,128)(2,1)S(1)}, bf16[8,1152]{1,0:T(8,128)(2,1)S(1)}, u32[]{:S(2)}, u32[]{:S(2)}) collective-permute-start(bf16[8,1152]{1,0:T(8,128)(2,1)S(1)} %get-tuple-element.33), channel_id=1, source_target_pairs={{0,12},{4,8},{8,4},{12,0},{16,28},{20,24},{24,20},{28,16},{1,13},{... | collective-permute-start | bytes 55304 | tf_op jit(solution)/shard_map/ppermute | solution.py:232
  26.2 0.5 %collective-permute-start.9 = (bf16[8,1152]{1,0:T(8,128)(2,1)S(1)}, bf16[8,1152]{1,0:T(8,128)(2,1)S(1)}, u32[]{:S(2)}, u32[]{:S(2)}) collective-permute-start(bf16[8,1152]{1,0:T(8,128)(2,1)S(1)} %get-tuple-element.34), channel_id=1, source_target_pairs={{0,20},{4,16},{8,28},{12,24},{16,4},{20,0},{24,12},{28,8},{1,21},{... | collective-permute-start | bytes 55304 | tf_op jit(solution)/shard_map/ppermute | solution.py:232
  26.9 1.6 %collective-permute-done.10.refs_3_ = bf16[8,1152]{1,0:T(8,128)(2,1)S(1)} collective-permute-done((bf16[8,1152]{1,0:T(8,128)(2,1)S(1)}, bf16[8,1152]{1,0:T(8,128)(2,1)S(1)}, u32[]{:S(2)}, u32[]{:S(2)}) %collective-permute-start.10) | collective-permute-done | bytes 18464 | tf_op jit(solution)/shard_map/ppermute | solution.py:232
  28.5 1.1 %collective-permute-done.9.refs_2_ = bf16[8,1152]{1,0:T(8,128)(2,1)S(1)} collective-permute-done((bf16[8,1152]{1,0:T(8,128)(2,1)S(1)}, bf16[8,1152]{1,0:T(8,128)(2,1)S(1)}, u32[]{:S(2)}, u32[]{:S(2)}) %collective-permute-start.9) | collective-permute-done | bytes 18464 | tf_op jit(solution)/shard_map/ppermute | solution.py:232
  29.7 1.8 %collective-permute-start.14 = (bf16[8,1152]{1,0:T(8,128)(2,1)S(1)}, bf16[8,1152]{1,0:T(8,128)(2,1)S(1)}, u32[]{:S(2)}, u32[]{:S(2)}) collective-permute-start(bf16[8,1152]{1,0:T(8,128)(2,1)S(1)} %get-tuple-element.41.refs_0_), channel_id=1, source_target_pairs={{0,3},{1,2},{2,1},{3,0},{4,7},{5,6},{6,5},{7,4},{8,11},{9,10},{10,... | collective-permute-start | bytes 55304 | tf_op jit(solution)/shard_map/ppermute | solution.py:232
  31.9 2.2 %collective-permute-start.16 = (bf16[8,1152]{1,0:T(8,128)(2,1)S(1)}, bf16[8,1152]{1,0:T(8,128)(2,1)S(1)}, u32[]{:S(2)}, u32[]{:S(2)}) collective-permute-start(bf16[8,1152]{1,0:T(8,128)(2,1)S(1)} %get-tuple-element.41.refs_0_), channel_id=1, source_target_pairs={{0,1},{1,0},{2,3},{3,2},{4,5},{5,4},{6,7},{7,6},{8,9},{9,8},{10,11... | collective-permute-start | bytes 55304 | tf_op jit(solution)/shard_map/ppermute | solution.py:232
  34.1 1.0 %shard_map.85 = f32[8,1152]{1,0:T(8,128)} custom-call(f32[8,1152]{1,0:T(8,128)S(1)} %get-tuple-element.37.unit_ref, f32[8,128]{1,0:T(8,128)S(1)} %get-tuple-element.38.inverse_ref, bf16[32,1152]{1,0:T(8,128)(2,1)S(1)} %get-tuple-element.39.refs_0_), custom_call_target="tpu_custom_call" | custom-call | tf_op jit(solution)/shard_map/pallas_call | solution.py:22
  35.3 0.9 %collective-permute-done.15.refs_2_ = bf16[8,1152]{1,0:T(8,128)(2,1)S(1)} collective-permute-done((bf16[8,1152]{1,0:T(8,128)(2,1)S(1)}, bf16[8,1152]{1,0:T(8,128)(2,1)S(1)}, u32[]{:S(2)}, u32[]{:S(2)}) %collective-permute-start.15) | collective-permute-done | bytes 18464 | tf_op jit(solution)/shard_map/ppermute | solution.py:232
  36.2 1.0 %shard_map.86 = f32[8,1152]{1,0:T(8,128)} custom-call(f32[8,1152]{1,0:T(8,128)S(1)} %get-tuple-element.40.unit_ref, f32[8,128]{1,0:T(8,128)S(1)} %get-tuple-element.36.refs_4_.inverse_ref, bf16[8,1152]{1,0:T(8,128)(2,1)S(1)} %get-tuple-element.41.refs_0_, bf16[8,1152]{1,0:T(8,128)(2,1)S(1)} %collective-permute-done.14.refs_1_, ...), custom_call_target="tpu_custom_call" | custom-call | tf_op jit(solution)/shard_map/pallas_call | solution.py:22
  (26 shorter events, 2.1 us)
Async XLA Ops:
  0.6 12.1 %copy-start = (bf16[144,1152]{1,0:T(8,128)(2,1)S(1)}, bf16[144,1152]{1,0:T(8,128)(2,1)}, u32[]{:S(2)}) copy-start(bf16[144,1152]{1,0:T(8,128)(2,1)} %refs_4_.3) | copy-start | bytes 995332
  2.2 11.6 %copy-start.2 = (bf16[8,64,1152]{2,1,0:T(8,128)(2,1)S(1)}, bf16[8,64,1152]{2,1,0:T(8,128)(2,1)}, u32[]{:S(2)}) copy-start(bf16[8,64,1152]{2,1,0:T(8,128)(2,1)} %param.6) | copy-start | bytes 3538948
  2.2 5.6 %collective-permute-start = (bf16[16,3024]{1,0:T(8,128)(2,1)S(1)}, bf16[16,3024]{1,0:T(8,128)(2,1)S(1)}, u32[]{:S(2)}, u32[]{:S(2)}) collective-permute-start(bf16[16,3024]{1,0:T(8,128)(2,1)S(1)} %get-tuple-element.23), channel_id=1, source_target_pairs={{0,12},{4,8},{8,4},{12,0},{16,28},{20,24},{24,20},{28,16},{1,13},{... | collective-permute-start | bytes 290312 | tf_op jit(solution)/shard_map/ppermute | solution.py:232
  4.7 6.3 %collective-permute-start.1 = (bf16[16,3024]{1,0:T(8,128)(2,1)S(1)}, bf16[16,3024]{1,0:T(8,128)(2,1)S(1)}, u32[]{:S(2)}, u32[]{:S(2)}) collective-permute-start(bf16[16,3024]{1,0:T(8,128)(2,1)S(1)} %get-tuple-element.24), channel_id=1, source_target_pairs={{0,20},{4,16},{8,28},{12,24},{16,4},{20,0},{24,12},{28,8},{1,21},{... | collective-permute-start | bytes 290312 | tf_op jit(solution)/shard_map/ppermute | solution.py:232
  6.5 6.0 %collective-permute-start.2 = (bf16[16,3024]{1,0:T(8,128)(2,1)S(1)}, bf16[16,3024]{1,0:T(8,128)(2,1)S(1)}, u32[]{:S(2)}, u32[]{:S(2)}) collective-permute-start(bf16[16,3024]{1,0:T(8,128)(2,1)S(1)} %get-tuple-element.25), channel_id=1, source_target_pairs={{0,28},{4,24},{8,20},{12,16},{16,12},{20,8},{24,4},{28,0},{1,29},{... | collective-permute-start | bytes 290312 | tf_op jit(solution)/shard_map/ppermute | solution.py:232
  12.5 1.3 %collective-permute-start.3 = (bf16[4,16,432]{2,1,0:T(8,128)(2,1)S(1)}, bf16[4,16,432]{2,1,0:T(8,128)(2,1)S(1)}, u32[]{:S(2)}, u32[]{:S(2)}) collective-permute-start(bf16[4,16,432]{2,1,0:T(8,128)(2,1)S(1)} %shard_map.78.own_ref.refs_5_), channel_id=1, source_target_pairs={{0,4},{4,0},{8,12},{12,8},{16,20},{20,16},{24,28},{28,24},{1,5},{5... | collective-permute-start | bytes 165896 | tf_op jit(solution)/shard_map/ppermute | solution.py:232
  12.8 6.7 %collective-permute-start.7 = (bf16[9,16,2592]{2,1,0:T(8,128)(2,1)S(1)}, bf16[9,16,2592]{2,1,0:T(8,128)(2,1)S(1)}, u32[]{:S(2)}, u32[]{:S(2)}) collective-permute-start(bf16[9,16,2592]{2,1,0:T(8,128)(2,1)S(1)} %shard_map.80), channel_id=1, source_target_pairs={{0,4},{4,0},{8,12},{12,8},{16,20},{20,16},{24,28},{28,24},{1,5},{5... | collective-permute-start | bytes 2239496 | tf_op jit(solution)/shard_map/ppermute | solution.py:232
  13.9 4.1 %copy-start.1 = (bf16[8,1152]{1,0:T(8,128)(2,1)S(1)}, bf16[8,1152]{1,0:T(8,128)(2,1)}, u32[]{:S(2)}) copy-start(bf16[8,1152]{1,0:T(8,128)(2,1)} %refs_0_.1) | copy-start | bytes 55300
  14.9 7.6 %collective-permute-start.4 = (bf16[2,16,1152]{2,1,0:T(8,128)(2,1)S(1)}, bf16[2,16,1152]{2,1,0:T(8,128)(2,1)S(1)}, u32[]{:S(2)}, u32[]{:S(2)}) collective-permute-start(bf16[2,16,1152]{2,1,0:T(8,128)(2,1)S(1)} %get-tuple-element.27), channel_id=1, source_target_pairs={{0,12},{4,8},{8,4},{12,0},{16,28},{20,24},{24,20},{28,16},{1,13},{... | collective-permute-start | bytes 221192 | tf_op jit(solution)/shard_map/ppermute | solution.py:232
  15.6 8.2 %collective-permute-start.5 = (bf16[2,16,1152]{2,1,0:T(8,128)(2,1)S(1)}, bf16[2,16,1152]{2,1,0:T(8,128)(2,1)S(1)}, u32[]{:S(2)}, u32[]{:S(2)}) collective-permute-start(bf16[2,16,1152]{2,1,0:T(8,128)(2,1)S(1)} %get-tuple-element.28), channel_id=1, source_target_pairs={{0,20},{4,16},{8,28},{12,24},{16,4},{20,0},{24,12},{28,8},{1,21},{... | collective-permute-start | bytes 221192 | tf_op jit(solution)/shard_map/ppermute | solution.py:232
  16.2 7.7 %collective-permute-start.6 = (bf16[2,16,1152]{2,1,0:T(8,128)(2,1)S(1)}, bf16[2,16,1152]{2,1,0:T(8,128)(2,1)S(1)}, u32[]{:S(2)}, u32[]{:S(2)}) collective-permute-start(bf16[2,16,1152]{2,1,0:T(8,128)(2,1)S(1)} %get-tuple-element.29), channel_id=1, source_target_pairs={{0,28},{4,24},{8,20},{12,16},{16,12},{20,8},{24,4},{28,0},{1,29},{... | collective-permute-start | bytes 221192 | tf_op jit(solution)/shard_map/ppermute | solution.py:232
  17.9 8.3 %collective-permute-start.11 = (bf16[8,1152]{1,0:T(8,128)(2,1)S(1)}, bf16[8,1152]{1,0:T(8,128)(2,1)S(1)}, u32[]{:S(2)}, u32[]{:S(2)}) collective-permute-start(bf16[8,1152]{1,0:T(8,128)(2,1)S(1)} %copy-done.1), channel_id=1, source_target_pairs={{0,1},{1,2},{2,3},{3,0},{4,5},{5,6},{6,7},{7,4},{8,9},{9,10},{10,1... | collective-permute-start | bytes 55304 | tf_op jit(solution)/shard_map/ppermute | solution.py:237
  19.5 7.3 %collective-permute-start.12 = (bf16[8,1152]{1,0:T(8,128)(2,1)S(1)}, bf16[8,1152]{1,0:T(8,128)(2,1)S(1)}, u32[]{:S(2)}, u32[]{:S(2)}) collective-permute-start(bf16[8,1152]{1,0:T(8,128)(2,1)S(1)} %copy-done.1), channel_id=1, source_target_pairs={{0,2},{1,3},{2,0},{3,1},{4,6},{5,7},{6,4},{7,5},{8,10},{9,11},{10,... | collective-permute-start | bytes 55304 | tf_op jit(solution)/shard_map/ppermute | solution.py:237
  22.5 4.3 %collective-permute-start.13 = (bf16[8,1152]{1,0:T(8,128)(2,1)S(1)}, bf16[8,1152]{1,0:T(8,128)(2,1)S(1)}, u32[]{:S(2)}, u32[]{:S(2)}) collective-permute-start(bf16[8,1152]{1,0:T(8,128)(2,1)S(1)} %copy-done.1), channel_id=1, source_target_pairs={{0,3},{1,0},{2,1},{3,2},{4,7},{5,4},{6,5},{7,6},{8,11},{9,8},{10,9... | collective-permute-start | bytes 55304 | tf_op jit(solution)/shard_map/ppermute | solution.py:237
  24.4 4.2 %collective-permute-start.10 = (bf16[8,1152]{1,0:T(8,128)(2,1)S(1)}, bf16[8,1152]{1,0:T(8,128)(2,1)S(1)}, u32[]{:S(2)}, u32[]{:S(2)}) collective-permute-start(bf16[8,1152]{1,0:T(8,128)(2,1)S(1)} %get-tuple-element.35), channel_id=1, source_target_pairs={{0,28},{4,24},{8,20},{12,16},{16,12},{20,8},{24,4},{28,0},{1,29},{... | collective-permute-start | bytes 55304 | tf_op jit(solution)/shard_map/ppermute | solution.py:232
  24.5 4.0 %collective-permute-start.8 = (bf16[8,1152]{1,0:T(8,128)(2,1)S(1)}, bf16[8,1152]{1,0:T(8,128)(2,1)S(1)}, u32[]{:S(2)}, u32[]{:S(2)}) collective-permute-start(bf16[8,1152]{1,0:T(8,128)(2,1)S(1)} %get-tuple-element.33), channel_id=1, source_target_pairs={{0,12},{4,8},{8,4},{12,0},{16,28},{20,24},{24,20},{28,16},{1,13},{... | collective-permute-start | bytes 55304 | tf_op jit(solution)/shard_map/ppermute | solution.py:232
  26.2 3.4 %collective-permute-start.9 = (bf16[8,1152]{1,0:T(8,128)(2,1)S(1)}, bf16[8,1152]{1,0:T(8,128)(2,1)S(1)}, u32[]{:S(2)}, u32[]{:S(2)}) collective-permute-start(bf16[8,1152]{1,0:T(8,128)(2,1)S(1)} %get-tuple-element.34), channel_id=1, source_target_pairs={{0,20},{4,16},{8,28},{12,24},{16,4},{20,0},{24,12},{28,8},{1,21},{... | collective-permute-start | bytes 55304 | tf_op jit(solution)/shard_map/ppermute | solution.py:232
  29.7 5.6 %collective-permute-start.14 = (bf16[8,1152]{1,0:T(8,128)(2,1)S(1)}, bf16[8,1152]{1,0:T(8,128)(2,1)S(1)}, u32[]{:S(2)}, u32[]{:S(2)}) collective-permute-start(bf16[8,1152]{1,0:T(8,128)(2,1)S(1)} %get-tuple-element.41.refs_0_), channel_id=1, source_target_pairs={{0,3},{1,2},{2,1},{3,0},{4,7},{5,6},{6,5},{7,4},{8,11},{9,10},{10,... | collective-permute-start | bytes 55304 | tf_op jit(solution)/shard_map/ppermute | solution.py:232
  31.5 4.7 %collective-permute-start.15 = (bf16[8,1152]{1,0:T(8,128)(2,1)S(1)}, bf16[8,1152]{1,0:T(8,128)(2,1)S(1)}, u32[]{:S(2)}, u32[]{:S(2)}) collective-permute-start(bf16[8,1152]{1,0:T(8,128)(2,1)S(1)} %get-tuple-element.41.refs_0_), channel_id=1, source_target_pairs={{0,2},{1,3},{2,0},{3,1},{4,6},{5,7},{6,4},{7,5},{8,10},{9,11},{10,... | collective-permute-start | bytes 55304 | tf_op jit(solution)/shard_map/ppermute | solution.py:232
  31.9 4.3 %collective-permute-start.16 = (bf16[8,1152]{1,0:T(8,128)(2,1)S(1)}, bf16[8,1152]{1,0:T(8,128)(2,1)S(1)}, u32[]{:S(2)}, u32[]{:S(2)}) collective-permute-start(bf16[8,1152]{1,0:T(8,128)(2,1)S(1)} %get-tuple-element.41.refs_0_), channel_id=1, source_target_pairs={{0,1},{1,0},{2,3},{3,2},{4,5},{5,4},{6,7},{7,6},{8,9},{9,8},{10,11... | collective-permute-start | bytes 55304 | tf_op jit(solution)/shard_map/ppermute | solution.py:232

commit v6 on v5

--- a/solution.py
+++ b/solution.py
@@ -60,6 +60,10 @@
     rest = values - high.astype(F32)
     middle = rest.astype(BF16)
     return high, middle, (rest - middle.astype(F32)).astype(BF16)
+
+
+def flips(chips):
+    return [0, *range(chips - 1, chips - 2, -1), *range(1, chips - 1)]
 
 
 def chip_and_core():
@@ -98,7 +102,7 @@
         pieces = [columns[j * rows : (j + 1) * rows] for j in range(part // rows)]
         blocks[q] = jnp.concatenate(pieces, axis=1)
     chip, _ = chip_and_core()
-    for m, out_ref in enumerate(out_refs):
+    for m, out_ref in zip(flips(chips), out_refs):
         out_ref[:, :packed] = blocks[chip ^ m]
         out_ref[:, packed:] = keys
 
@@ -133,10 +137,10 @@
     _, rows, length = own_ref.shape
     part = width // (chips * CORES)
     chip, core = chip_and_core()
-    for m in range(chips):
+    for i, m in enumerate(flips(chips)):
         place = core if m == 0 else 1 - core
-        placed[chip ^ m, place] = own_ref[m]
-        placed[chip ^ m, 1 - place] = other_ref[m]
+        placed[chip ^ m, place] = own_ref[i]
+        placed[chip ^ m, 1 - place] = other_ref[i]
     for j in range(length // part):
         for k in range(chips * CORES):
             table[j * rows : (j + 1) * rows, k * part : (k + 1) * part] = placed[
@@ -152,7 +156,7 @@
     weights = expo / jnp.sum(expo, axis=2, keepdims=True)
     weights = weights.reshape(HEADS * images, x.shape[0])
     every[...] = nn(weights.astype(BF16), x).astype(BF16).reshape(every.shape)
-    for m, out_ref in enumerate(outs):
+    for m, out_ref in zip(flips(chips), outs):
         out_ref[...] = every[chip ^ m]
 
 
@@ -161,8 +165,8 @@
     part, width = w_out_ref.shape
     rows = other_ref.shape[1]
     chip, core = chip_and_core()
-    for m in range(chips):
-        for c, source in enumerate((refs[m], other_ref.at[m])):
+    for i, m in enumerate(flips(chips)):
+        for c, source in enumerate((refs[i], other_ref.at[i])):
             place = core if (c == 0) == (m == 0) else 1 - core
             for t in range(CORES):
                 for j in range(part // rows):
@@ -240,8 +244,9 @@
 
 
 def exchange_chips(arrays, devices):
-    return [arrays[0]] + [
-        exchange(array, devices, m * CORES + 1) for m, array in enumerate(arrays) if m
+    return [
+        exchange(array, devices, m * CORES + 1) if m else array
+        for m, array in zip(flips(len(arrays)), arrays)
     ]
 
 

time: 37.3 us -> 37.4 us (level)
  starting transfers between devices: 20.3 us -> 20.8 us
  waiting for transfers between devices: 10.4 us -> 9.92 us
    ppermute x14, starting transfers between devices: 14.7 us -> 15.3 us  [exchange(): return lax.ppermute(array, axis, [(i, i ^ flip) for i in range(devices)])]
    ppermute x14, waiting for transfers between devices: 10.4 us -> 9.92 us  [exchange(): return lax.ppermute(array, axis, [(i, i ^ flip) for i in range(devices)])]
where the time goes in v6:
time: 37.4 us; the launch traced here: 37.3 us
  starting transfers between devices  20.8 us (56%)
  waiting for transfers between devices  9.92 us (27%)
  Pallas kernels  5.77 us (15%)
  between operations  0.72 us (2%)
    ppermute x14, starting transfers between devices, exchange(): return lax.ppermute(array, axis, [(i, i ^ flip) for i in range(devices)])  15.3 us
    ppermute x14, waiting for transfers between devices, exchange(): return lax.ppermute(array, axis, [(i, i ^ flip) for i in range(devices)])  9.92 us
    pallas_call x10, Pallas kernels, call(): pl.pallas_call(body, out_shape=out, in_specs=[pl.BlockSpec(memory_space=s...  5.77 us
    ppermute x3, starting transfers between devices, all_blocks(): lax.ppermute(array, 'blk', [(i, (i + by) % blocks) for i in range(blocks)])  5.53 us
  transfers between devices with their start and end apart: 17, of which 8 were waited for; matrix products, arithmetic and copies ran while one was open for 0% of the time, Pallas kernels for 8%

profile of v6, /device:TPU:0, one launch (start us, length us, event | category | flops | bytes accessed | tf_op | source)
XLA Modules:
  0.0 37.3 jit_solution(16567887102125655794)
XLA Ops:
  0.6 1.6 %shard_map.77 = (bf16[16,3024]{1,0:T(8,128)(2,1)S(1)}, bf16[16,3024]{1,0:T(8,128)(2,1)S(1)}, bf16[16,3024]{1,0:T(8,128)(2,1)S(1)}, bf16[16,3024]{1,0:T(8,128)(2,1)S(1)}) custom-call(bf16[1152]{0:T(1024)(128)(2,1)} %probe_hbm.1, bf16[144,1152]{1,0:T(8,128)(2,1)} %w_key_hbm.1, bf16[144,1152]{1,0:T(8,128)(2,1)} %w_value_hbm.1), custom_call_target="tpu_custom_call" | custom-call | tf_op jit(solution)/shard_map/pallas_call | solution.py:22
  2.2 3.4 %collective-permute-start = (bf16[16,3024]{1,0:T(8,128)(2,1)S(1)}, bf16[16,3024]{1,0:T(8,128)(2,1)S(1)}, u32[]{:S(2)}, u32[]{:S(2)}) collective-permute-start(bf16[16,3024]{1,0:T(8,128)(2,1)S(1)} %get-tuple-element.23), channel_id=1, source_target_pairs={{0,28},{4,24},{8,20},{12,16},{16,12},{20,8},{24,4},{28,0},{1,29},{... | collective-permute-start | bytes 290312 | tf_op jit(solution)/shard_map/ppermute | solution.py:236
  5.6 0.8 %collective-permute-start.1 = (bf16[16,3024]{1,0:T(8,128)(2,1)S(1)}, bf16[16,3024]{1,0:T(8,128)(2,1)S(1)}, u32[]{:S(2)}, u32[]{:S(2)}) collective-permute-start(bf16[16,3024]{1,0:T(8,128)(2,1)S(1)} %get-tuple-element.24), channel_id=1, source_target_pairs={{0,12},{4,8},{8,4},{12,0},{16,28},{20,24},{24,20},{28,16},{1,13},{... | collective-permute-start | bytes 290312 | tf_op jit(solution)/shard_map/ppermute | solution.py:236
  6.5 2.3 %collective-permute-done.refs_1_ = bf16[16,3024]{1,0:T(8,128)(2,1)S(1)} collective-permute-done((bf16[16,3024]{1,0:T(8,128)(2,1)S(1)}, bf16[16,3024]{1,0:T(8,128)(2,1)S(1)}, u32[]{:S(2)}, u32[]{:S(2)}) %collective-permute-start) | collective-permute-done | bytes 96800 | tf_op jit(solution)/shard_map/ppermute | solution.py:236
  8.8 3.1 %collective-permute-done.1.refs_2_ = bf16[16,3024]{1,0:T(8,128)(2,1)S(1)} collective-permute-done((bf16[16,3024]{1,0:T(8,128)(2,1)S(1)}, bf16[16,3024]{1,0:T(8,128)(2,1)S(1)}, u32[]{:S(2)}, u32[]{:S(2)}) %collective-permute-start.1) | collective-permute-done | bytes 96800 | tf_op jit(solution)/shard_map/ppermute | solution.py:236
  12.3 0.5 %collective-permute-start.7 = (bf16[9,16,2592]{2,1,0:T(8,128)(2,1)S(1)}, bf16[9,16,2592]{2,1,0:T(8,128)(2,1)S(1)}, u32[]{:S(2)}, u32[]{:S(2)}) collective-permute-start(bf16[9,16,2592]{2,1,0:T(8,128)(2,1)S(1)} %shard_map.80), channel_id=1, source_target_pairs={{0,4},{4,0},{8,12},{12,8},{16,20},{20,16},{24,28},{28,24},{1,5},{5... | collective-permute-start | bytes 2239496 | tf_op jit(solution)/shard_map/ppermute | solution.py:236
  12.7 0.6 %collective-permute-done.3.other_ref = bf16[4,16,432]{2,1,0:T(8,128)(2,1)S(1)} collective-permute-done((bf16[4,16,432]{2,1,0:T(8,128)(2,1)S(1)}, bf16[4,16,432]{2,1,0:T(8,128)(2,1)S(1)}, u32[]{:S(2)}, u32[]{:S(2)}) %collective-permute-start.3) | collective-permute-done | bytes 55328 | tf_op jit(solution)/shard_map/ppermute | solution.py:236
  13.3 1.0 %shard_map.79 = (bf16[2,16,1152]{2,1,0:T(8,128)(2,1)S(1)}, bf16[2,16,1152]{2,1,0:T(8,128)(2,1)S(1)}, bf16[2,16,1152]{2,1,0:T(8,128)(2,1)S(1)}, bf16[2,16,1152]{2,1,0:T(8,128)(2,1)S(1)}) custom-call(bf16[512,1152]{1,0:T(8,128)(2,1)S(1)} %bitcast.1, bf16[4,16,432]{2,1,0:T(8,128)(2,1)S(1)} %shard_map.78.own_ref.refs_5_, ...), custom_call_target="tpu_custom_call" | custom-call | flops 10000000000 | tf_op jit(solution)/shard_map/pallas_call | solution.py:22
  14.4 2.2 %collective-permute-start.4 = (bf16[2,16,1152]{2,1,0:T(8,128)(2,1)S(1)}, bf16[2,16,1152]{2,1,0:T(8,128)(2,1)S(1)}, u32[]{:S(2)}, u32[]{:S(2)}) collective-permute-start(bf16[2,16,1152]{2,1,0:T(8,128)(2,1)S(1)} %get-tuple-element.27), channel_id=1, source_target_pairs={{0,28},{4,24},{8,20},{12,16},{16,12},{20,8},{24,4},{28,0},{1,29},{... | collective-permute-start | bytes 221192 | tf_op jit(solution)/shard_map/ppermute | solution.py:236
  17.0 0.4 %collective-permute-start.6 = (bf16[2,16,1152]{2,1,0:T(8,128)(2,1)S(1)}, bf16[2,16,1152]{2,1,0:T(8,128)(2,1)S(1)}, u32[]{:S(2)}, u32[]{:S(2)}) collective-permute-start(bf16[2,16,1152]{2,1,0:T(8,128)(2,1)S(1)} %get-tuple-element.29), channel_id=1, source_target_pairs={{0,20},{4,16},{8,28},{12,24},{16,4},{20,0},{24,12},{28,8},{1,21},{... | collective-permute-start | bytes 221192 | tf_op jit(solution)/shard_map/ppermute | solution.py:236
  17.4 1.5 %collective-permute-start.11 = (bf16[8,1152]{1,0:T(8,128)(2,1)S(1)}, bf16[8,1152]{1,0:T(8,128)(2,1)S(1)}, u32[]{:S(2)}, u32[]{:S(2)}) collective-permute-start(bf16[8,1152]{1,0:T(8,128)(2,1)S(1)} %copy-done.1), channel_id=1, source_target_pairs={{0,1},{1,2},{2,3},{3,0},{4,5},{5,6},{6,7},{7,4},{8,9},{9,10},{10,1... | collective-permute-start | bytes 55304 | tf_op jit(solution)/shard_map/ppermute | solution.py:241
  19.0 2.6 %collective-permute-start.12 = (bf16[8,1152]{1,0:T(8,128)(2,1)S(1)}, bf16[8,1152]{1,0:T(8,128)(2,1)S(1)}, u32[]{:S(2)}, u32[]{:S(2)}) collective-permute-start(bf16[8,1152]{1,0:T(8,128)(2,1)S(1)} %copy-done.1), channel_id=1, source_target_pairs={{0,2},{1,3},{2,0},{3,1},{4,6},{5,7},{6,4},{7,5},{8,10},{9,11},{10,... | collective-permute-start | bytes 55304 | tf_op jit(solution)/shard_map/ppermute | solution.py:241
  21.9 1.4 %collective-permute-start.13 = (bf16[8,1152]{1,0:T(8,128)(2,1)S(1)}, bf16[8,1152]{1,0:T(8,128)(2,1)S(1)}, u32[]{:S(2)}, u32[]{:S(2)}) collective-permute-start(bf16[8,1152]{1,0:T(8,128)(2,1)S(1)} %copy-done.1), channel_id=1, source_target_pairs={{0,3},{1,0},{2,1},{3,2},{4,7},{5,4},{6,5},{7,6},{8,11},{9,8},{10,9... | collective-permute-start | bytes 55304 | tf_op jit(solution)/shard_map/ppermute | solution.py:241
  23.3 0.5 %shard_map.82 = (bf16[8,1152]{1,0:T(8,128)(2,1)S(1)}, bf16[8,1152]{1,0:T(8,128)(2,1)S(1)}, bf16[8,1152]{1,0:T(8,128)(2,1)S(1)}, bf16[8,1152]{1,0:T(8,128)(2,1)S(1)}) custom-call(bf16[2,16,1152]{2,1,0:T(8,128)(2,1)S(1)} %get-tuple-element.26.refs_0_, bf16[2,16,1152]{2,1,0:T(8,128)(2,1)S(1)} %collective-permute-done.4.refs_1_, ...), custom_call_target="tpu_custom_call" | custom-call | tf_op jit(solution)/shard_map/pallas_call | solution.py:22
  23.8 1.2 %collective-permute-start.10 = (bf16[8,1152]{1,0:T(8,128)(2,1)S(1)}, bf16[8,1152]{1,0:T(8,128)(2,1)S(1)}, u32[]{:S(2)}, u32[]{:S(2)}) collective-permute-start(bf16[8,1152]{1,0:T(8,128)(2,1)S(1)} %get-tuple-element.35), channel_id=1, source_target_pairs={{0,20},{4,16},{8,28},{12,24},{16,4},{20,0},{24,12},{28,8},{1,21},{... | collective-permute-start | bytes 55304 | tf_op jit(solution)/shard_map/ppermute | solution.py:236
  25.0 1.6 %collective-permute-start.8 = (bf16[8,1152]{1,0:T(8,128)(2,1)S(1)}, bf16[8,1152]{1,0:T(8,128)(2,1)S(1)}, u32[]{:S(2)}, u32[]{:S(2)}) collective-permute-start(bf16[8,1152]{1,0:T(8,128)(2,1)S(1)} %get-tuple-element.33), channel_id=1, source_target_pairs={{0,28},{4,24},{8,20},{12,16},{16,12},{20,8},{24,4},{28,0},{1,29},{... | collective-permute-start | bytes 55304 | tf_op jit(solution)/shard_map/ppermute | solution.py:236
  27.1 2.0 %collective-permute-done.8.refs_1_ = bf16[8,1152]{1,0:T(8,128)(2,1)S(1)} collective-permute-done((bf16[8,1152]{1,0:T(8,128)(2,1)S(1)}, bf16[8,1152]{1,0:T(8,128)(2,1)S(1)}, u32[]{:S(2)}, u32[]{:S(2)}) %collective-permute-start.8) | collective-permute-done | bytes 18464 | tf_op jit(solution)/shard_map/ppermute | solution.py:236
  29.1 0.7 %collective-permute-done.9.refs_2_ = bf16[8,1152]{1,0:T(8,128)(2,1)S(1)} collective-permute-done((bf16[8,1152]{1,0:T(8,128)(2,1)S(1)}, bf16[8,1152]{1,0:T(8,128)(2,1)S(1)}, u32[]{:S(2)}, u32[]{:S(2)}) %collective-permute-start.9) | collective-permute-done | bytes 18464 | tf_op jit(solution)/shard_map/ppermute | solution.py:236
  29.9 1.7 %collective-permute-start.14 = (bf16[8,1152]{1,0:T(8,128)(2,1)S(1)}, bf16[8,1152]{1,0:T(8,128)(2,1)S(1)}, u32[]{:S(2)}, u32[]{:S(2)}) collective-permute-start(bf16[8,1152]{1,0:T(8,128)(2,1)S(1)} %get-tuple-element.41.refs_0_), channel_id=1, source_target_pairs={{0,3},{1,2},{2,1},{3,0},{4,7},{5,6},{6,5},{7,4},{8,11},{9,10},{10,... | collective-permute-start | bytes 55304 | tf_op jit(solution)/shard_map/ppermute | solution.py:236
  31.6 0.5 %collective-permute-start.15 = (bf16[8,1152]{1,0:T(8,128)(2,1)S(1)}, bf16[8,1152]{1,0:T(8,128)(2,1)S(1)}, u32[]{:S(2)}, u32[]{:S(2)}) collective-permute-start(bf16[8,1152]{1,0:T(8,128)(2,1)S(1)} %get-tuple-element.41.refs_0_), channel_id=1, source_target_pairs={{0,2},{1,3},{2,0},{3,1},{4,6},{5,7},{6,4},{7,5},{8,10},{9,11},{10,... | collective-permute-start | bytes 55304 | tf_op jit(solution)/shard_map/ppermute | solution.py:236
  32.1 2.1 %collective-permute-start.16 = (bf16[8,1152]{1,0:T(8,128)(2,1)S(1)}, bf16[8,1152]{1,0:T(8,128)(2,1)S(1)}, u32[]{:S(2)}, u32[]{:S(2)}) collective-permute-start(bf16[8,1152]{1,0:T(8,128)(2,1)S(1)} %get-tuple-element.41.refs_0_), channel_id=1, source_target_pairs={{0,1},{1,0},{2,3},{3,2},{4,5},{5,4},{6,7},{7,6},{8,9},{9,8},{10,11... | collective-permute-start | bytes 55304 | tf_op jit(solution)/shard_map/ppermute | solution.py:236
  34.2 1.0 %shard_map.85 = f32[8,1152]{1,0:T(8,128)} custom-call(f32[8,1152]{1,0:T(8,128)S(1)} %get-tuple-element.37.unit_ref, f32[8,128]{1,0:T(8,128)S(1)} %get-tuple-element.38.inverse_ref, bf16[32,1152]{1,0:T(8,128)(2,1)S(1)} %get-tuple-element.39.refs_0_), custom_call_target="tpu_custom_call" | custom-call | tf_op jit(solution)/shard_map/pallas_call | solution.py:22
  35.4 0.8 %collective-permute-done.15.refs_2_ = bf16[8,1152]{1,0:T(8,128)(2,1)S(1)} collective-permute-done((bf16[8,1152]{1,0:T(8,128)(2,1)S(1)}, bf16[8,1152]{1,0:T(8,128)(2,1)S(1)}, u32[]{:S(2)}, u32[]{:S(2)}) %collective-permute-start.15) | collective-permute-done | bytes 18464 | tf_op jit(solution)/shard_map/ppermute | solution.py:236
  36.3 1.0 %shard_map.86 = f32[8,1152]{1,0:T(8,128)} custom-call(f32[8,1152]{1,0:T(8,128)S(1)} %get-tuple-element.40.unit_ref, f32[8,128]{1,0:T(8,128)S(1)} %get-tuple-element.36.refs_4_.inverse_ref, bf16[8,1152]{1,0:T(8,128)(2,1)S(1)} %get-tuple-element.41.refs_0_, bf16[8,1152]{1,0:T(8,128)(2,1)S(1)} %collective-permute-done.14.refs_1_, ...), custom_call_target="tpu_custom_call" | custom-call | tf_op jit(solution)/shard_map/pallas_call | solution.py:22
  (26 shorter events, 2.0 us)
Async XLA Ops:
  0.6 11.6 %copy-start = (bf16[144,1152]{1,0:T(8,128)(2,1)S(1)}, bf16[144,1152]{1,0:T(8,128)(2,1)}, u32[]{:S(2)}) copy-start(bf16[144,1152]{1,0:T(8,128)(2,1)} %refs_4_.3) | copy-start | bytes 995332
  2.2 11.1 %copy-start.2 = (bf16[8,64,1152]{2,1,0:T(8,128)(2,1)S(1)}, bf16[8,64,1152]{2,1,0:T(8,128)(2,1)}, u32[]{:S(2)}) copy-start(bf16[8,64,1152]{2,1,0:T(8,128)(2,1)} %param.6) | copy-start | bytes 3538948
  2.2 6.6 %collective-permute-start = (bf16[16,3024]{1,0:T(8,128)(2,1)S(1)}, bf16[16,3024]{1,0:T(8,128)(2,1)S(1)}, u32[]{:S(2)}, u32[]{:S(2)}) collective-permute-start(bf16[16,3024]{1,0:T(8,128)(2,1)S(1)} %get-tuple-element.23), channel_id=1, source_target_pairs={{0,28},{4,24},{8,20},{12,16},{16,12},{20,8},{24,4},{28,0},{1,29},{... | collective-permute-start | bytes 290312 | tf_op jit(solution)/shard_map/ppermute | solution.py:236
  5.6 6.3 %collective-permute-start.1 = (bf16[16,3024]{1,0:T(8,128)(2,1)S(1)}, bf16[16,3024]{1,0:T(8,128)(2,1)S(1)}, u32[]{:S(2)}, u32[]{:S(2)}) collective-permute-start(bf16[16,3024]{1,0:T(8,128)(2,1)S(1)} %get-tuple-element.24), channel_id=1, source_target_pairs={{0,12},{4,8},{8,4},{12,0},{16,28},{20,24},{24,20},{28,16},{1,13},{... | collective-permute-start | bytes 290312 | tf_op jit(solution)/shard_map/ppermute | solution.py:236
  6.4 5.5 %collective-permute-start.2 = (bf16[16,3024]{1,0:T(8,128)(2,1)S(1)}, bf16[16,3024]{1,0:T(8,128)(2,1)S(1)}, u32[]{:S(2)}, u32[]{:S(2)}) collective-permute-start(bf16[16,3024]{1,0:T(8,128)(2,1)S(1)} %get-tuple-element.25), channel_id=1, source_target_pairs={{0,20},{4,16},{8,28},{12,24},{16,4},{20,0},{24,12},{28,8},{1,21},{... | collective-permute-start | bytes 290312 | tf_op jit(solution)/shard_map/ppermute | solution.py:236
  12.0 1.3 %collective-permute-start.3 = (bf16[4,16,432]{2,1,0:T(8,128)(2,1)S(1)}, bf16[4,16,432]{2,1,0:T(8,128)(2,1)S(1)}, u32[]{:S(2)}, u32[]{:S(2)}) collective-permute-start(bf16[4,16,432]{2,1,0:T(8,128)(2,1)S(1)} %shard_map.78.own_ref.refs_5_), channel_id=1, source_target_pairs={{0,4},{4,0},{8,12},{12,8},{16,20},{20,16},{24,28},{28,24},{1,5},{5... | collective-permute-start | bytes 165896 | tf_op jit(solution)/shard_map/ppermute | solution.py:236
  12.3 6.7 %collective-permute-start.7 = (bf16[9,16,2592]{2,1,0:T(8,128)(2,1)S(1)}, bf16[9,16,2592]{2,1,0:T(8,128)(2,1)S(1)}, u32[]{:S(2)}, u32[]{:S(2)}) collective-permute-start(bf16[9,16,2592]{2,1,0:T(8,128)(2,1)S(1)} %shard_map.80), channel_id=1, source_target_pairs={{0,4},{4,0},{8,12},{12,8},{16,20},{20,16},{24,28},{28,24},{1,5},{5... | collective-permute-start | bytes 2239496 | tf_op jit(solution)/shard_map/ppermute | solution.py:236
  13.3 4.1 %copy-start.1 = (bf16[8,1152]{1,0:T(8,128)(2,1)S(1)}, bf16[8,1152]{1,0:T(8,128)(2,1)}, u32[]{:S(2)}) copy-start(bf16[8,1152]{1,0:T(8,128)(2,1)} %refs_0_.1) | copy-start | bytes 55300
  14.4 7.5 %collective-permute-start.4 = (bf16[2,16,1152]{2,1,0:T(8,128)(2,1)S(1)}, bf16[2,16,1152]{2,1,0:T(8,128)(2,1)S(1)}, u32[]{:S(2)}, u32[]{:S(2)}) collective-permute-start(bf16[2,16,1152]{2,1,0:T(8,128)(2,1)S(1)} %get-tuple-element.27), channel_id=1, source_target_pairs={{0,28},{4,24},{8,20},{12,16},{16,12},{20,8},{24,4},{28,0},{1,29},{... | collective-permute-start | bytes 221192 | tf_op jit(solution)/shard_map/ppermute | solution.py:236
  16.5 6.8 %collective-permute-start.5 = (bf16[2,16,1152]{2,1,0:T(8,128)(2,1)S(1)}, bf16[2,16,1152]{2,1,0:T(8,128)(2,1)S(1)}, u32[]{:S(2)}, u32[]{:S(2)}) collective-permute-start(bf16[2,16,1152]{2,1,0:T(8,128)(2,1)S(1)} %get-tuple-element.28), channel_id=1, source_target_pairs={{0,12},{4,8},{8,4},{12,0},{16,28},{20,24},{24,20},{28,16},{1,13},{... | collective-permute-start | bytes 221192 | tf_op jit(solution)/shard_map/ppermute | solution.py:236
  17.0 6.3 %collective-permute-start.6 = (bf16[2,16,1152]{2,1,0:T(8,128)(2,1)S(1)}, bf16[2,16,1152]{2,1,0:T(8,128)(2,1)S(1)}, u32[]{:S(2)}, u32[]{:S(2)}) collective-permute-start(bf16[2,16,1152]{2,1,0:T(8,128)(2,1)S(1)} %get-tuple-element.29), channel_id=1, source_target_pairs={{0,20},{4,16},{8,28},{12,24},{16,4},{20,0},{24,12},{28,8},{1,21},{... | collective-permute-start | bytes 221192 | tf_op jit(solution)/shard_map/ppermute | solution.py:236
  17.4 9.2 %collective-permute-start.11 = (bf16[8,1152]{1,0:T(8,128)(2,1)S(1)}, bf16[8,1152]{1,0:T(8,128)(2,1)S(1)}, u32[]{:S(2)}, u32[]{:S(2)}) collective-permute-start(bf16[8,1152]{1,0:T(8,128)(2,1)S(1)} %copy-done.1), channel_id=1, source_target_pairs={{0,1},{1,2},{2,3},{3,0},{4,5},{5,6},{6,7},{7,4},{8,9},{9,10},{10,1... | collective-permute-start | bytes 55304 | tf_op jit(solution)/shard_map/ppermute | solution.py:241
  19.0 7.8 %collective-permute-start.12 = (bf16[8,1152]{1,0:T(8,128)(2,1)S(1)}, bf16[8,1152]{1,0:T(8,128)(2,1)S(1)}, u32[]{:S(2)}, u32[]{:S(2)}) collective-permute-start(bf16[8,1152]{1,0:T(8,128)(2,1)S(1)} %copy-done.1), channel_id=1, source_target_pairs={{0,2},{1,3},{2,0},{3,1},{4,6},{5,7},{6,4},{7,5},{8,10},{9,11},{10,... | collective-permute-start | bytes 55304 | tf_op jit(solution)/shard_map/ppermute | solution.py:241
  21.9 4.9 %collective-permute-start.13 = (bf16[8,1152]{1,0:T(8,128)(2,1)S(1)}, bf16[8,1152]{1,0:T(8,128)(2,1)S(1)}, u32[]{:S(2)}, u32[]{:S(2)}) collective-permute-start(bf16[8,1152]{1,0:T(8,128)(2,1)S(1)} %copy-done.1), channel_id=1, source_target_pairs={{0,3},{1,0},{2,1},{3,2},{4,7},{5,4},{6,5},{7,6},{8,11},{9,8},{10,9... | collective-permute-start | bytes 55304 | tf_op jit(solution)/shard_map/ppermute | solution.py:241
  23.8 3.3 %collective-permute-start.10 = (bf16[8,1152]{1,0:T(8,128)(2,1)S(1)}, bf16[8,1152]{1,0:T(8,128)(2,1)S(1)}, u32[]{:S(2)}, u32[]{:S(2)}) collective-permute-start(bf16[8,1152]{1,0:T(8,128)(2,1)S(1)} %get-tuple-element.35), channel_id=1, source_target_pairs={{0,20},{4,16},{8,28},{12,24},{16,4},{20,0},{24,12},{28,8},{1,21},{... | collective-permute-start | bytes 55304 | tf_op jit(solution)/shard_map/ppermute | solution.py:236
  25.0 4.1 %collective-permute-start.8 = (bf16[8,1152]{1,0:T(8,128)(2,1)S(1)}, bf16[8,1152]{1,0:T(8,128)(2,1)S(1)}, u32[]{:S(2)}, u32[]{:S(2)}) collective-permute-start(bf16[8,1152]{1,0:T(8,128)(2,1)S(1)} %get-tuple-element.33), channel_id=1, source_target_pairs={{0,28},{4,24},{8,20},{12,16},{16,12},{20,8},{24,4},{28,0},{1,29},{... | collective-permute-start | bytes 55304 | tf_op jit(solution)/shard_map/ppermute | solution.py:236
  26.6 3.2 %collective-permute-start.9 = (bf16[8,1152]{1,0:T(8,128)(2,1)S(1)}, bf16[8,1152]{1,0:T(8,128)(2,1)S(1)}, u32[]{:S(2)}, u32[]{:S(2)}) collective-permute-start(bf16[8,1152]{1,0:T(8,128)(2,1)S(1)} %get-tuple-element.34), channel_id=1, source_target_pairs={{0,12},{4,8},{8,4},{12,0},{16,28},{20,24},{24,20},{28,16},{1,13},{... | collective-permute-start | bytes 55304 | tf_op jit(solution)/shard_map/ppermute | solution.py:236
  29.9 5.6 %collective-permute-start.14 = (bf16[8,1152]{1,0:T(8,128)(2,1)S(1)}, bf16[8,1152]{1,0:T(8,128)(2,1)S(1)}, u32[]{:S(2)}, u32[]{:S(2)}) collective-permute-start(bf16[8,1152]{1,0:T(8,128)(2,1)S(1)} %get-tuple-element.41.refs_0_), channel_id=1, source_target_pairs={{0,3},{1,2},{2,1},{3,0},{4,7},{5,6},{6,5},{7,4},{8,11},{9,10},{10,... | collective-permute-start | bytes 55304 | tf_op jit(solution)/shard_map/ppermute | solution.py:236
  31.6 4.7 %collective-permute-start.15 = (bf16[8,1152]{1,0:T(8,128)(2,1)S(1)}, bf16[8,1152]{1,0:T(8,128)(2,1)S(1)}, u32[]{:S(2)}, u32[]{:S(2)}) collective-permute-start(bf16[8,1152]{1,0:T(8,128)(2,1)S(1)} %get-tuple-element.41.refs_0_), channel_id=1, source_target_pairs={{0,2},{1,3},{2,0},{3,1},{4,6},{5,7},{6,4},{7,5},{8,10},{9,11},{10,... | collective-permute-start | bytes 55304 | tf_op jit(solution)/shard_map/ppermute | solution.py:236
  32.1 4.1 %collective-permute-start.16 = (bf16[8,1152]{1,0:T(8,128)(2,1)S(1)}, bf16[8,1152]{1,0:T(8,128)(2,1)S(1)}, u32[]{:S(2)}, u32[]{:S(2)}) collective-permute-start(bf16[8,1152]{1,0:T(8,128)(2,1)S(1)} %get-tuple-element.41.refs_0_), channel_id=1, source_target_pairs={{0,1},{1,0},{2,3},{3,2},{4,5},{5,4},{6,7},{7,6},{8,9},{9,8},{10,11... | collective-permute-start | bytes 55304 | tf_op jit(solution)/shard_map/ppermute | solution.py:236

commit v7 on v5

--- a/solution.py
+++ b/solution.py
@@ -60,6 +60,10 @@
     rest = values - high.astype(F32)
     middle = rest.astype(BF16)
     return high, middle, (rest - middle.astype(F32)).astype(BF16)
+
+
+def far_first(chips):
+    return [0, chips - 1, *range(1, chips - 1)]
 
 
 def chip_and_core():
@@ -152,7 +156,7 @@
     weights = expo / jnp.sum(expo, axis=2, keepdims=True)
     weights = weights.reshape(HEADS * images, x.shape[0])
     every[...] = nn(weights.astype(BF16), x).astype(BF16).reshape(every.shape)
-    for m, out_ref in enumerate(outs):
+    for m, out_ref in zip(far_first(chips), outs):
         out_ref[...] = every[chip ^ m]
 
 
@@ -239,9 +243,10 @@
     ]
 
 
-def exchange_chips(arrays, devices):
-    return [arrays[0]] + [
-        exchange(array, devices, m * CORES + 1) for m, array in enumerate(arrays) if m
+def exchange_chips(arrays, devices, order):
+    return [
+        exchange(array, devices, m * CORES + 1) if m else array
+        for m, array in zip(order, arrays)
     ]
 
 
@@ -274,9 +279,16 @@
         ],
         space=pltpu.HBM,
     )
-    parts = exchange_chips(parts, devices)
+    parts = exchange_chips(parts, devices, range(chips))
+    row, column = struct((images, width), F32), struct((images, 128), F32)
+    all_texts = all_blocks(texts, blocks)
+    words, unit_text, inverse_text = call(
+        functools.partial(unit_text_kernel, blocks),
+        (struct((blocks * images, width), BF16), row, column),
+        *all_texts,
+    )
     keys = call(
-        functools.partial(pack_keys_kernel, chips), struct((chips, rows, length), BF16), *parts
+        functools.partial(pack_keys_kernel, chips), struct((chips, rows, length), BF16), *parts, all_texts[1]
     )
     shard = call(
         functools.partial(shard_kernel, chips),
@@ -311,20 +323,14 @@
     partial_embed = call(
         functools.partial(project_kernel, images, chips),
         [struct((images, width), BF16)] * chips,
-        *exchange_chips(mixed, devices),
+        *exchange_chips(mixed, devices, far_first(chips)),
         w_values,
         w_outs,
-    )
-    row, column = struct((images, width), F32), struct((images, 128), F32)
-    words, unit_text, inverse_text = call(
-        functools.partial(unit_text_kernel, blocks),
-        (struct((blocks * images, width), BF16), row, column),
-        *all_blocks(texts, blocks),
     )
     unit, inverse, rounded = call(
         functools.partial(unit_image_kernel, chips),
         (row, column, struct((images, width), BF16)),
-        *exchange_chips(partial_embed, devices),
+        *exchange_chips(partial_embed, devices, far_first(chips)),
         inverse_text,
     )
     all_images = [exchange(rounded, blocks, m, "blk") for m in range(blocks - 1, 0, -1)]

time: 37.3 us -> 37.4 us (level)
  starting transfers between devices: 20.3 us -> 20.8 us
  waiting for transfers between devices: 10.4 us -> 9.98 us
    ppermute x14, waiting for transfers between devices: 10.4 us -> 5.78 us  [exchange(): return lax.ppermute(array, axis, [(i, i ^ flip) for i in range(devices)])]
    ppermute x3, waiting for transfers between devices: 0.01 us -> 4.2 us  [all_blocks(): lax.ppermute(array, 'blk', [(i, (i + by) % blocks) for i in range(blocks)])]
    ppermute x14, starting transfers between devices: 14.7 us -> 15.3 us  [exchange(): return lax.ppermute(array, axis, [(i, i ^ flip) for i in range(devices)])]
where the time goes in v7:
time: 37.4 us; the launch traced here: 37.3 us
  starting transfers between devices  20.8 us (56%)
  waiting for transfers between devices  9.98 us (27%)
  Pallas kernels  5.77 us (15%)
  between operations  0.73 us (2%)
    ppermute x14, starting transfers between devices, exchange(): return lax.ppermute(array, axis, [(i, i ^ flip) for i in range(devices)])  15.3 us
    ppermute x14, waiting for transfers between devices, exchange(): return lax.ppermute(array, axis, [(i, i ^ flip) for i in range(devices)])  5.78 us
    pallas_call x10, Pallas kernels, call(): pl.pallas_call(body, out_shape=out, in_specs=[pl.BlockSpec(memory_space=s...  5.77 us
    ppermute x3, starting transfers between devices, all_blocks(): lax.ppermute(array, 'blk', [(i, (i + by) % blocks) for i in range(blocks)])  5.51 us
    ppermute x3, waiting for transfers between devices, all_blocks(): lax.ppermute(array, 'blk', [(i, (i + by) % blocks) for i in range(blocks)])  4.2 us
  transfers between devices with their start and end apart: 17, of which 8 were waited for; matrix products, arithmetic and copies ran while one was open for 0% of the time, Pallas kernels for 8%

profile of v7, /device:TPU:0, one launch (start us, length us, event | category | flops | bytes accessed | tf_op | source)
XLA Modules:
  0.0 37.3 jit_solution(4827843030726078794)
XLA Ops:
  0.6 1.6 %shard_map.77 = (bf16[16,3024]{1,0:T(8,128)(2,1)S(1)}, bf16[16,3024]{1,0:T(8,128)(2,1)S(1)}, bf16[16,3024]{1,0:T(8,128)(2,1)S(1)}, bf16[16,3024]{1,0:T(8,128)(2,1)S(1)}) custom-call(bf16[1152]{0:T(1024)(128)(2,1)} %probe_hbm.1, bf16[144,1152]{1,0:T(8,128)(2,1)} %w_key_hbm.1, bf16[144,1152]{1,0:T(8,128)(2,1)} %w_value_hbm.1), custom_call_target="tpu_custom_call" | custom-call | tf_op jit(solution)/shard_map/pallas_call | solution.py:22
  2.2 2.4 %collective-permute-start = (bf16[16,3024]{1,0:T(8,128)(2,1)S(1)}, bf16[16,3024]{1,0:T(8,128)(2,1)S(1)}, u32[]{:S(2)}, u32[]{:S(2)}) collective-permute-start(bf16[16,3024]{1,0:T(8,128)(2,1)S(1)} %get-tuple-element.23), channel_id=1, source_target_pairs={{0,12},{4,8},{8,4},{12,0},{16,28},{20,24},{24,20},{28,16},{1,13},{... | collective-permute-start | bytes 290312 | tf_op jit(solution)/shard_map/ppermute | solution.py:236
  4.7 1.8 %collective-permute-start.1 = (bf16[16,3024]{1,0:T(8,128)(2,1)S(1)}, bf16[16,3024]{1,0:T(8,128)(2,1)S(1)}, u32[]{:S(2)}, u32[]{:S(2)}) collective-permute-start(bf16[16,3024]{1,0:T(8,128)(2,1)S(1)} %get-tuple-element.24), channel_id=1, source_target_pairs={{0,20},{4,16},{8,28},{12,24},{16,4},{20,0},{24,12},{28,8},{1,21},{... | collective-permute-start | bytes 290312 | tf_op jit(solution)/shard_map/ppermute | solution.py:236
  6.5 1.6 %collective-permute-start.3 = (bf16[8,1152]{1,0:T(8,128)(2,1)}, bf16[8,1152]{1,0:T(8,128)(2,1)S(1)}, u32[]{:S(2)}, u32[]{:S(2)}) collective-permute-start(bf16[8,1152]{1,0:T(8,128)(2,1)} %refs_0_.1), channel_id=1, source_target_pairs={{0,1},{1,2},{2,3},{3,0},{4,5},{5,6},{6,7},{7,4},{8,9},{9,10},{10,1... | collective-permute-start | bytes 55304 | tf_op jit(solution)/shard_map/ppermute | solution.py:241
  8.1 4.2 %collective-permute-done.3.refs_4_.refs_1_ = bf16[8,1152]{1,0:T(8,128)(2,1)S(1)} collective-permute-done((bf16[8,1152]{1,0:T(8,128)(2,1)}, bf16[8,1152]{1,0:T(8,128)(2,1)S(1)}, u32[]{:S(2)}, u32[]{:S(2)}) %collective-permute-start.3) | collective-permute-done | bytes 18464 | tf_op jit(solution)/shard_map/ppermute | solution.py:241
  12.8 0.5 %collective-permute-start.8 = (bf16[9,16,2592]{2,1,0:T(8,128)(2,1)S(1)}, bf16[9,16,2592]{2,1,0:T(8,128)(2,1)S(1)}, u32[]{:S(2)}, u32[]{:S(2)}) collective-permute-start(bf16[9,16,2592]{2,1,0:T(8,128)(2,1)S(1)} %shard_map.80), channel_id=1, source_target_pairs={{0,4},{4,0},{8,12},{12,8},{16,20},{20,16},{24,28},{28,24},{1,5},{5... | collective-permute-start | bytes 2239496 | tf_op jit(solution)/shard_map/ppermute | solution.py:236
  13.2 0.6 %collective-permute-done.4.other_ref = bf16[4,16,432]{2,1,0:T(8,128)(2,1)S(1)} collective-permute-done((bf16[4,16,432]{2,1,0:T(8,128)(2,1)S(1)}, bf16[4,16,432]{2,1,0:T(8,128)(2,1)S(1)}, u32[]{:S(2)}, u32[]{:S(2)}) %collective-permute-start.4) | collective-permute-done | bytes 55328 | tf_op jit(solution)/shard_map/ppermute | solution.py:236
  13.9 1.0 %shard_map.79 = (bf16[2,16,1152]{2,1,0:T(8,128)(2,1)S(1)}, bf16[2,16,1152]{2,1,0:T(8,128)(2,1)S(1)}, bf16[2,16,1152]{2,1,0:T(8,128)(2,1)S(1)}, bf16[2,16,1152]{2,1,0:T(8,128)(2,1)S(1)}) custom-call(bf16[512,1152]{1,0:T(8,128)(2,1)S(1)} %bitcast.1, bf16[4,16,432]{2,1,0:T(8,128)(2,1)S(1)} %shard_map.78.own_ref.refs_5_, ...), custom_call_target="tpu_custom_call" | custom-call | flops 10000000000 | tf_op jit(solution)/shard_map/pallas_call | solution.py:22
  14.9 2.0 %collective-permute-start.5 = (bf16[2,16,1152]{2,1,0:T(8,128)(2,1)S(1)}, bf16[2,16,1152]{2,1,0:T(8,128)(2,1)S(1)}, u32[]{:S(2)}, u32[]{:S(2)}) collective-permute-start(bf16[2,16,1152]{2,1,0:T(8,128)(2,1)S(1)} %get-tuple-element.27), channel_id=1, source_target_pairs={{0,28},{4,24},{8,20},{12,16},{16,12},{20,8},{24,4},{28,0},{1,29},{... | collective-permute-start | bytes 221192 | tf_op jit(solution)/shard_map/ppermute | solution.py:236
  16.9 0.6 %collective-permute-start.6 = (bf16[2,16,1152]{2,1,0:T(8,128)(2,1)S(1)}, bf16[2,16,1152]{2,1,0:T(8,128)(2,1)S(1)}, u32[]{:S(2)}, u32[]{:S(2)}) collective-permute-start(bf16[2,16,1152]{2,1,0:T(8,128)(2,1)S(1)} %get-tuple-element.28), channel_id=1, source_target_pairs={{0,12},{4,8},{8,4},{12,0},{16,28},{20,24},{24,20},{28,16},{1,13},{... | collective-permute-start | bytes 221192 | tf_op jit(solution)/shard_map/ppermute | solution.py:236
  17.5 0.5 %collective-permute-start.7 = (bf16[2,16,1152]{2,1,0:T(8,128)(2,1)S(1)}, bf16[2,16,1152]{2,1,0:T(8,128)(2,1)S(1)}, u32[]{:S(2)}, u32[]{:S(2)}) collective-permute-start(bf16[2,16,1152]{2,1,0:T(8,128)(2,1)S(1)} %get-tuple-element.29), channel_id=1, source_target_pairs={{0,20},{4,16},{8,28},{12,24},{16,4},{20,0},{24,12},{28,8},{1,21},{... | collective-permute-start | bytes 221192 | tf_op jit(solution)/shard_map/ppermute | solution.py:236
  17.9 2.6 %collective-permute-start.12 = (bf16[8,1152]{1,0:T(8,128)(2,1)S(1)}, bf16[8,1152]{1,0:T(8,128)(2,1)S(1)}, u32[]{:S(2)}, u32[]{:S(2)}) collective-permute-start(bf16[8,1152]{1,0:T(8,128)(2,1)S(1)} %copy-done.1), channel_id=1, source_target_pairs={{0,2},{1,3},{2,0},{3,1},{4,6},{5,7},{6,4},{7,5},{8,10},{9,11},{10,... | collective-permute-start | bytes 55304 | tf_op jit(solution)/shard_map/ppermute | solution.py:241
  20.5 1.4 %collective-permute-start.13 = (bf16[8,1152]{1,0:T(8,128)(2,1)S(1)}, bf16[8,1152]{1,0:T(8,128)(2,1)S(1)}, u32[]{:S(2)}, u32[]{:S(2)}) collective-permute-start(bf16[8,1152]{1,0:T(8,128)(2,1)S(1)} %copy-done.1), channel_id=1, source_target_pairs={{0,3},{1,0},{2,1},{3,2},{4,7},{5,4},{6,5},{7,6},{8,11},{9,8},{10,9... | collective-permute-start | bytes 55304 | tf_op jit(solution)/shard_map/ppermute | solution.py:241
  22.3 0.5 %shard_map.82 = (bf16[8,1152]{1,0:T(8,128)(2,1)S(1)}, bf16[8,1152]{1,0:T(8,128)(2,1)S(1)}, bf16[8,1152]{1,0:T(8,128)(2,1)S(1)}, bf16[8,1152]{1,0:T(8,128)(2,1)S(1)}) custom-call(bf16[2,16,1152]{2,1,0:T(8,128)(2,1)S(1)} %get-tuple-element.26.refs_0_, bf16[2,16,1152]{2,1,0:T(8,128)(2,1)S(1)} %collective-permute-done.5.refs_1_, ...), custom_call_target="tpu_custom_call" | custom-call | tf_op jit(solution)/shard_map/pallas_call | solution.py:22
  22.8 0.8 %collective-permute-start.10 = (bf16[8,1152]{1,0:T(8,128)(2,1)S(1)}, bf16[8,1152]{1,0:T(8,128)(2,1)S(1)}, u32[]{:S(2)}, u32[]{:S(2)}) collective-permute-start(bf16[8,1152]{1,0:T(8,128)(2,1)S(1)} %get-tuple-element.34), channel_id=1, source_target_pairs={{0,12},{4,8},{8,4},{12,0},{16,28},{20,24},{24,20},{28,16},{1,13},{... | collective-permute-start | bytes 55304 | tf_op jit(solution)/shard_map/ppermute | solution.py:236
  23.6 1.4 %collective-permute-start.11 = (bf16[8,1152]{1,0:T(8,128)(2,1)S(1)}, bf16[8,1152]{1,0:T(8,128)(2,1)S(1)}, u32[]{:S(2)}, u32[]{:S(2)}) collective-permute-start(bf16[8,1152]{1,0:T(8,128)(2,1)S(1)} %get-tuple-element.35), channel_id=1, source_target_pairs={{0,20},{4,16},{8,28},{12,24},{16,4},{20,0},{24,12},{28,8},{1,21},{... | collective-permute-start | bytes 55304 | tf_op jit(solution)/shard_map/ppermute | solution.py:236
  25.0 0.7 %collective-permute-start.9 = (bf16[8,1152]{1,0:T(8,128)(2,1)S(1)}, bf16[8,1152]{1,0:T(8,128)(2,1)S(1)}, u32[]{:S(2)}, u32[]{:S(2)}) collective-permute-start(bf16[8,1152]{1,0:T(8,128)(2,1)S(1)} %get-tuple-element.33), channel_id=1, source_target_pairs={{0,28},{4,24},{8,20},{12,16},{16,12},{20,8},{24,4},{28,0},{1,29},{... | collective-permute-start | bytes 55304 | tf_op jit(solution)/shard_map/ppermute | solution.py:236
  26.0 0.8 %collective-permute-done.11.refs_3_ = bf16[8,1152]{1,0:T(8,128)(2,1)S(1)} collective-permute-done((bf16[8,1152]{1,0:T(8,128)(2,1)S(1)}, bf16[8,1152]{1,0:T(8,128)(2,1)S(1)}, u32[]{:S(2)}, u32[]{:S(2)}) %collective-permute-start.11) | collective-permute-done | bytes 18464 | tf_op jit(solution)/shard_map/ppermute | solution.py:236
  26.8 2.3 %collective-permute-done.9.refs_1_ = bf16[8,1152]{1,0:T(8,128)(2,1)S(1)} collective-permute-done((bf16[8,1152]{1,0:T(8,128)(2,1)S(1)}, bf16[8,1152]{1,0:T(8,128)(2,1)S(1)}, u32[]{:S(2)}, u32[]{:S(2)}) %collective-permute-start.9) | collective-permute-done | bytes 18464 | tf_op jit(solution)/shard_map/ppermute | solution.py:236
  29.2 2.4 %collective-permute-start.14 = (bf16[8,1152]{1,0:T(8,128)(2,1)S(1)}, bf16[8,1152]{1,0:T(8,128)(2,1)S(1)}, u32[]{:S(2)}, u32[]{:S(2)}) collective-permute-start(bf16[8,1152]{1,0:T(8,128)(2,1)S(1)} %get-tuple-element.41.refs_0_), channel_id=1, source_target_pairs={{0,3},{1,2},{2,1},{3,0},{4,7},{5,6},{6,5},{7,4},{8,11},{9,10},{10,... | collective-permute-start | bytes 55304 | tf_op jit(solution)/shard_map/ppermute | solution.py:236
  31.6 2.0 %collective-permute-start.16 = (bf16[8,1152]{1,0:T(8,128)(2,1)S(1)}, bf16[8,1152]{1,0:T(8,128)(2,1)S(1)}, u32[]{:S(2)}, u32[]{:S(2)}) collective-permute-start(bf16[8,1152]{1,0:T(8,128)(2,1)S(1)} %get-tuple-element.41.refs_0_), channel_id=1, source_target_pairs={{0,1},{1,0},{2,3},{3,2},{4,5},{5,4},{6,7},{7,6},{8,9},{9,8},{10,11... | collective-permute-start | bytes 55304 | tf_op jit(solution)/shard_map/ppermute | solution.py:236
  33.6 1.0 %shard_map.85 = f32[8,1152]{1,0:T(8,128)} custom-call(f32[8,1152]{1,0:T(8,128)S(1)} %get-tuple-element.37.unit_ref, f32[8,128]{1,0:T(8,128)S(1)} %get-tuple-element.38.inverse_ref, bf16[32,1152]{1,0:T(8,128)(2,1)S(1)} %get-tuple-element.39.refs_0_), custom_call_target="tpu_custom_call" | custom-call | tf_op jit(solution)/shard_map/pallas_call | solution.py:22
  34.8 1.5 %collective-permute-done.15.refs_2_ = bf16[8,1152]{1,0:T(8,128)(2,1)S(1)} collective-permute-done((bf16[8,1152]{1,0:T(8,128)(2,1)S(1)}, bf16[8,1152]{1,0:T(8,128)(2,1)S(1)}, u32[]{:S(2)}, u32[]{:S(2)}) %collective-permute-start.15) | collective-permute-done | bytes 18464 | tf_op jit(solution)/shard_map/ppermute | solution.py:236
  36.3 1.0 %shard_map.86 = f32[8,1152]{1,0:T(8,128)} custom-call(f32[8,1152]{1,0:T(8,128)S(1)} %get-tuple-element.40.unit_ref, f32[8,128]{1,0:T(8,128)S(1)} %get-tuple-element.36.refs_4_.inverse_ref, bf16[8,1152]{1,0:T(8,128)(2,1)S(1)} %get-tuple-element.41.refs_0_, bf16[8,1152]{1,0:T(8,128)(2,1)S(1)} %collective-permute-done.14.refs_1_, ...), custom_call_target="tpu_custom_call" | custom-call | tf_op jit(solution)/shard_map/pallas_call | solution.py:22
  (26 shorter events, 1.5 us)
Async XLA Ops:
  0.6 12.1 %copy-start = (bf16[144,1152]{1,0:T(8,128)(2,1)S(1)}, bf16[144,1152]{1,0:T(8,128)(2,1)}, u32[]{:S(2)}) copy-start(bf16[144,1152]{1,0:T(8,128)(2,1)} %refs_4_.3) | copy-start | bytes 995332
  2.2 11.6 %copy-start.2 = (bf16[8,64,1152]{2,1,0:T(8,128)(2,1)S(1)}, bf16[8,64,1152]{2,1,0:T(8,128)(2,1)}, u32[]{:S(2)}) copy-start(bf16[8,64,1152]{2,1,0:T(8,128)(2,1)} %param.6) | copy-start | bytes 3538948
  2.2 10.0 %collective-permute-start = (bf16[16,3024]{1,0:T(8,128)(2,1)S(1)}, bf16[16,3024]{1,0:T(8,128)(2,1)S(1)}, u32[]{:S(2)}, u32[]{:S(2)}) collective-permute-start(bf16[16,3024]{1,0:T(8,128)(2,1)S(1)} %get-tuple-element.23), channel_id=1, source_target_pairs={{0,12},{4,8},{8,4},{12,0},{16,28},{20,24},{24,20},{28,16},{1,13},{... | collective-permute-start | bytes 290312 | tf_op jit(solution)/shard_map/ppermute | solution.py:236
  4.7 7.6 %collective-permute-start.1 = (bf16[16,3024]{1,0:T(8,128)(2,1)S(1)}, bf16[16,3024]{1,0:T(8,128)(2,1)S(1)}, u32[]{:S(2)}, u32[]{:S(2)}) collective-permute-start(bf16[16,3024]{1,0:T(8,128)(2,1)S(1)} %get-tuple-element.24), channel_id=1, source_target_pairs={{0,20},{4,16},{8,28},{12,24},{16,4},{20,0},{24,12},{28,8},{1,21},{... | collective-permute-start | bytes 290312 | tf_op jit(solution)/shard_map/ppermute | solution.py:236
  6.5 6.0 %collective-permute-start.2 = (bf16[16,3024]{1,0:T(8,128)(2,1)S(1)}, bf16[16,3024]{1,0:T(8,128)(2,1)S(1)}, u32[]{:S(2)}, u32[]{:S(2)}) collective-permute-start(bf16[16,3024]{1,0:T(8,128)(2,1)S(1)} %get-tuple-element.25), channel_id=1, source_target_pairs={{0,28},{4,24},{8,20},{12,16},{16,12},{20,8},{24,4},{28,0},{1,29},{... | collective-permute-start | bytes 290312 | tf_op jit(solution)/shard_map/ppermute | solution.py:236
  6.5 5.8 %collective-permute-start.3 = (bf16[8,1152]{1,0:T(8,128)(2,1)}, bf16[8,1152]{1,0:T(8,128)(2,1)S(1)}, u32[]{:S(2)}, u32[]{:S(2)}) collective-permute-start(bf16[8,1152]{1,0:T(8,128)(2,1)} %refs_0_.1), channel_id=1, source_target_pairs={{0,1},{1,2},{2,3},{3,0},{4,5},{5,6},{6,7},{7,4},{8,9},{9,10},{10,1... | collective-permute-start | bytes 55304 | tf_op jit(solution)/shard_map/ppermute | solution.py:241
  12.5 1.3 %collective-permute-start.4 = (bf16[4,16,432]{2,1,0:T(8,128)(2,1)S(1)}, bf16[4,16,432]{2,1,0:T(8,128)(2,1)S(1)}, u32[]{:S(2)}, u32[]{:S(2)}) collective-permute-start(bf16[4,16,432]{2,1,0:T(8,128)(2,1)S(1)} %shard_map.78.own_ref.refs_5_), channel_id=1, source_target_pairs={{0,4},{4,0},{8,12},{12,8},{16,20},{20,16},{24,28},{28,24},{1,5},{5... | collective-permute-start | bytes 165896 | tf_op jit(solution)/shard_map/ppermute | solution.py:236
  12.8 7.8 %collective-permute-start.8 = (bf16[9,16,2592]{2,1,0:T(8,128)(2,1)S(1)}, bf16[9,16,2592]{2,1,0:T(8,128)(2,1)S(1)}, u32[]{:S(2)}, u32[]{:S(2)}) collective-permute-start(bf16[9,16,2592]{2,1,0:T(8,128)(2,1)S(1)} %shard_map.80), channel_id=1, source_target_pairs={{0,4},{4,0},{8,12},{12,8},{16,20},{20,16},{24,28},{28,24},{1,5},{5... | collective-permute-start | bytes 2239496 | tf_op jit(solution)/shard_map/ppermute | solution.py:236
  13.9 4.1 %copy-start.1 = (bf16[8,1152]{1,0:T(8,128)(2,1)S(1)}, bf16[8,1152]{1,0:T(8,128)(2,1)}, u32[]{:S(2)}) copy-start(bf16[8,1152]{1,0:T(8,128)(2,1)} %refs_0_.1) | copy-start | bytes 55300
  14.9 7.3 %collective-permute-start.5 = (bf16[2,16,1152]{2,1,0:T(8,128)(2,1)S(1)}, bf16[2,16,1152]{2,1,0:T(8,128)(2,1)S(1)}, u32[]{:S(2)}, u32[]{:S(2)}) collective-permute-start(bf16[2,16,1152]{2,1,0:T(8,128)(2,1)S(1)} %get-tuple-element.27), channel_id=1, source_target_pairs={{0,28},{4,24},{8,20},{12,16},{16,12},{20,8},{24,4},{28,0},{1,29},{... | collective-permute-start | bytes 221192 | tf_op jit(solution)/shard_map/ppermute | solution.py:236
  16.9 5.3 %collective-permute-start.6 = (bf16[2,16,1152]{2,1,0:T(8,128)(2,1)S(1)}, bf16[2,16,1152]{2,1,0:T(8,128)(2,1)S(1)}, u32[]{:S(2)}, u32[]{:S(2)}) collective-permute-start(bf16[2,16,1152]{2,1,0:T(8,128)(2,1)S(1)} %get-tuple-element.28), channel_id=1, source_target_pairs={{0,12},{4,8},{8,4},{12,0},{16,28},{20,24},{24,20},{28,16},{1,13},{... | collective-permute-start | bytes 221192 | tf_op jit(solution)/shard_map/ppermute | solution.py:236
  17.5 4.8 %collective-permute-start.7 = (bf16[2,16,1152]{2,1,0:T(8,128)(2,1)S(1)}, bf16[2,16,1152]{2,1,0:T(8,128)(2,1)S(1)}, u32[]{:S(2)}, u32[]{:S(2)}) collective-permute-start(bf16[2,16,1152]{2,1,0:T(8,128)(2,1)S(1)} %get-tuple-element.29), channel_id=1, source_target_pairs={{0,20},{4,16},{8,28},{12,24},{16,4},{20,0},{24,12},{28,8},{1,21},{... | collective-permute-start | bytes 221192 | tf_op jit(solution)/shard_map/ppermute | solution.py:236
  17.9 7.8 %collective-permute-start.12 = (bf16[8,1152]{1,0:T(8,128)(2,1)S(1)}, bf16[8,1152]{1,0:T(8,128)(2,1)S(1)}, u32[]{:S(2)}, u32[]{:S(2)}) collective-permute-start(bf16[8,1152]{1,0:T(8,128)(2,1)S(1)} %copy-done.1), channel_id=1, source_target_pairs={{0,2},{1,3},{2,0},{3,1},{4,6},{5,7},{6,4},{7,5},{8,10},{9,11},{10,... | collective-permute-start | bytes 55304 | tf_op jit(solution)/shard_map/ppermute | solution.py:241
  20.5 5.2 %collective-permute-start.13 = (bf16[8,1152]{1,0:T(8,128)(2,1)S(1)}, bf16[8,1152]{1,0:T(8,128)(2,1)S(1)}, u32[]{:S(2)}, u32[]{:S(2)}) collective-permute-start(bf16[8,1152]{1,0:T(8,128)(2,1)S(1)} %copy-done.1), channel_id=1, source_target_pairs={{0,3},{1,0},{2,1},{3,2},{4,7},{5,4},{6,5},{7,6},{8,11},{9,8},{10,9... | collective-permute-start | bytes 55304 | tf_op jit(solution)/shard_map/ppermute | solution.py:241
  22.8 3.3 %collective-permute-start.10 = (bf16[8,1152]{1,0:T(8,128)(2,1)S(1)}, bf16[8,1152]{1,0:T(8,128)(2,1)S(1)}, u32[]{:S(2)}, u32[]{:S(2)}) collective-permute-start(bf16[8,1152]{1,0:T(8,128)(2,1)S(1)} %get-tuple-element.34), channel_id=1, source_target_pairs={{0,12},{4,8},{8,4},{12,0},{16,28},{20,24},{24,20},{28,16},{1,13},{... | collective-permute-start | bytes 55304 | tf_op jit(solution)/shard_map/ppermute | solution.py:236
  23.6 3.2 %collective-permute-start.11 = (bf16[8,1152]{1,0:T(8,128)(2,1)S(1)}, bf16[8,1152]{1,0:T(8,128)(2,1)S(1)}, u32[]{:S(2)}, u32[]{:S(2)}) collective-permute-start(bf16[8,1152]{1,0:T(8,128)(2,1)S(1)} %get-tuple-element.35), channel_id=1, source_target_pairs={{0,20},{4,16},{8,28},{12,24},{16,4},{20,0},{24,12},{28,8},{1,21},{... | collective-permute-start | bytes 55304 | tf_op jit(solution)/shard_map/ppermute | solution.py:236
  25.0 4.1 %collective-permute-start.9 = (bf16[8,1152]{1,0:T(8,128)(2,1)S(1)}, bf16[8,1152]{1,0:T(8,128)(2,1)S(1)}, u32[]{:S(2)}, u32[]{:S(2)}) collective-permute-start(bf16[8,1152]{1,0:T(8,128)(2,1)S(1)} %get-tuple-element.33), channel_id=1, source_target_pairs={{0,28},{4,24},{8,20},{12,16},{16,12},{20,8},{24,4},{28,0},{1,29},{... | collective-permute-start | bytes 55304 | tf_op jit(solution)/shard_map/ppermute | solution.py:236
  29.2 5.6 %collective-permute-start.14 = (bf16[8,1152]{1,0:T(8,128)(2,1)S(1)}, bf16[8,1152]{1,0:T(8,128)(2,1)S(1)}, u32[]{:S(2)}, u32[]{:S(2)}) collective-permute-start(bf16[8,1152]{1,0:T(8,128)(2,1)S(1)} %get-tuple-element.41.refs_0_), channel_id=1, source_target_pairs={{0,3},{1,2},{2,1},{3,0},{4,7},{5,6},{6,5},{7,4},{8,11},{9,10},{10,... | collective-permute-start | bytes 55304 | tf_op jit(solution)/shard_map/ppermute | solution.py:236
  31.6 4.7 %collective-permute-start.15 = (bf16[8,1152]{1,0:T(8,128)(2,1)S(1)}, bf16[8,1152]{1,0:T(8,128)(2,1)S(1)}, u32[]{:S(2)}, u32[]{:S(2)}) collective-permute-start(bf16[8,1152]{1,0:T(8,128)(2,1)S(1)} %get-tuple-element.41.refs_0_), channel_id=1, source_target_pairs={{0,2},{1,3},{2,0},{3,1},{4,6},{5,7},{6,4},{7,5},{8,10},{9,11},{10,... | collective-permute-start | bytes 55304 | tf_op jit(solution)/shard_map/ppermute | solution.py:236
  31.6 4.7 %collective-permute-start.16 = (bf16[8,1152]{1,0:T(8,128)(2,1)S(1)}, bf16[8,1152]{1,0:T(8,128)(2,1)S(1)}, u32[]{:S(2)}, u32[]{:S(2)}) collective-permute-start(bf16[8,1152]{1,0:T(8,128)(2,1)S(1)} %get-tuple-element.41.refs_0_), channel_id=1, source_target_pairs={{0,1},{1,0},{2,3},{3,2},{4,5},{5,4},{6,7},{7,6},{8,9},{9,8},{10,11... | collective-permute-start | bytes 55304 | tf_op jit(solution)/shard_map/ppermute | solution.py:236

commit v8 on v7

--- a/solution.py
+++ b/solution.py
@@ -155,9 +155,11 @@
     expo = jnp.exp(spread - jnp.max(spread, axis=2, keepdims=True))
     weights = expo / jnp.sum(expo, axis=2, keepdims=True)
     weights = weights.reshape(HEADS * images, x.shape[0])
-    every[...] = nn(weights.astype(BF16), x).astype(BF16).reshape(every.shape)
-    for m, out_ref in zip(far_first(chips), outs):
-        out_ref[...] = every[chip ^ m]
+    every[...] = weights.astype(BF16).reshape(every.shape)
+    ordered = jnp.concatenate([every[chip ^ m] for m in far_first(chips)], axis=0)
+    mixed = nn(ordered, x).astype(BF16).reshape(chips, *outs[0].shape)
+    for i, out_ref in enumerate(outs):
+        out_ref[...] = mixed[i]
 
 
 def unpack_kernel(chips, *refs):
@@ -280,15 +282,8 @@
         space=pltpu.HBM,
     )
     parts = exchange_chips(parts, devices, range(chips))
-    row, column = struct((images, width), F32), struct((images, 128), F32)
-    all_texts = all_blocks(texts, blocks)
-    words, unit_text, inverse_text = call(
-        functools.partial(unit_text_kernel, blocks),
-        (struct((blocks * images, width), BF16), row, column),
-        *all_texts,
-    )
     keys = call(
-        functools.partial(pack_keys_kernel, chips), struct((chips, rows, length), BF16), *parts, all_texts[1]
+        functools.partial(pack_keys_kernel, chips), struct((chips, rows, length), BF16), *parts
     )
     shard = call(
         functools.partial(shard_kernel, chips),
@@ -307,7 +302,7 @@
         scratch=[
             pltpu.VMEM((chips, CORES, rows, length), BF16),
             pltpu.VMEM((3 * HEADS, width), BF16),
-            pltpu.VMEM((chips, CORES, rows, width), BF16),
+            pltpu.VMEM((chips, CORES * rows, flat.shape[0]), BF16),
         ],
     )
     w_values, w_outs = call(
@@ -327,6 +322,12 @@
         w_values,
         w_outs,
     )
+    row, column = struct((images, width), F32), struct((images, 128), F32)
+    words, unit_text, inverse_text = call(
+        functools.partial(unit_text_kernel, blocks),
+        (struct((blocks * images, width), BF16), row, column),
+        *all_blocks(texts, blocks),
+    )
     unit, inverse, rounded = call(
         functools.partial(unit_image_kernel, chips),
         (row, column, struct((images, width), BF16)),

time: 37.4 us -> 37.4 us (level)
    ppermute x3, waiting for transfers between devices: 4.2 us -> 0.01 us  [all_blocks(): lax.ppermute(array, 'blk', [(i, (i + by) % blocks) for i in range(blocks)])]
    ppermute x14, waiting for transfers between devices: 5.78 us -> 9.89 us  [exchange(): return lax.ppermute(array, axis, [(i, i ^ flip) for i in range(devices)])]
  transfers between devices with their start and end apart: 17 -> 17, of which waited for: 8 -> 9; matrix products, arithmetic and copies ran while one was open for 0% -> 0% of each run, Pallas kernels for 8% -> 8%
where the time goes in v8:
time: 37.4 us; the launch traced here: 37.2 us
  starting transfers between devices  20.8 us (56%)
  waiting for transfers between devices  9.9 us (26%)
  Pallas kernels  5.78 us (15%)
  between operations  0.72 us (2%)
    ppermute x14, starting transfers between devices, exchange(): return lax.ppermute(array, axis, [(i, i ^ flip) for i in range(devices)])  15.3 us
    ppermute x14, waiting for transfers between devices, exchange(): return lax.ppermute(array, axis, [(i, i ^ flip) for i in range(devices)])  9.89 us
    pallas_call x10, Pallas kernels, call(): pl.pallas_call(body, out_shape=out, in_specs=[pl.BlockSpec(memory_space=s...  5.78 us
    ppermute x3, starting transfers between devices, all_blocks(): lax.ppermute(array, 'blk', [(i, (i + by) % blocks) for i in range(blocks)])  5.57 us
  transfers between devices with their start and end apart: 17, of which 9 were waited for; matrix products, arithmetic and copies ran while one was open for 0% of the time, Pallas kernels for 8%

profile of v8, /device:TPU:0, one launch (start us, length us, event | category | flops | bytes accessed | tf_op | source)
XLA Modules:
  0.0 37.2 jit_solution(11879732836562367047)
XLA Ops:
  0.6 1.6 %shard_map.77 = (bf16[16,3024]{1,0:T(8,128)(2,1)S(1)}, bf16[16,3024]{1,0:T(8,128)(2,1)S(1)}, bf16[16,3024]{1,0:T(8,128)(2,1)S(1)}, bf16[16,3024]{1,0:T(8,128)(2,1)S(1)}) custom-call(bf16[1152]{0:T(1024)(128)(2,1)} %probe_hbm.1, bf16[144,1152]{1,0:T(8,128)(2,1)} %w_key_hbm.1, bf16[144,1152]{1,0:T(8,128)(2,1)} %w_value_hbm.1), custom_call_target="tpu_custom_call" | custom-call | tf_op jit(solution)/shard_map/pallas_call | solution.py:22
  2.2 2.4 %collective-permute-start = (bf16[16,3024]{1,0:T(8,128)(2,1)S(1)}, bf16[16,3024]{1,0:T(8,128)(2,1)S(1)}, u32[]{:S(2)}, u32[]{:S(2)}) collective-permute-start(bf16[16,3024]{1,0:T(8,128)(2,1)S(1)} %get-tuple-element.23), channel_id=1, source_target_pairs={{0,12},{4,8},{8,4},{12,0},{16,28},{20,24},{24,20},{28,16},{1,13},{... | collective-permute-start | bytes 290312 | tf_op jit(solution)/shard_map/ppermute | solution.py:238
  4.7 1.8 %collective-permute-start.1 = (bf16[16,3024]{1,0:T(8,128)(2,1)S(1)}, bf16[16,3024]{1,0:T(8,128)(2,1)S(1)}, u32[]{:S(2)}, u32[]{:S(2)}) collective-permute-start(bf16[16,3024]{1,0:T(8,128)(2,1)S(1)} %get-tuple-element.24), channel_id=1, source_target_pairs={{0,20},{4,16},{8,28},{12,24},{16,4},{20,0},{24,12},{28,8},{1,21},{... | collective-permute-start | bytes 290312 | tf_op jit(solution)/shard_map/ppermute | solution.py:238
  6.5 1.4 %collective-permute-done.refs_1_ = bf16[16,3024]{1,0:T(8,128)(2,1)S(1)} collective-permute-done((bf16[16,3024]{1,0:T(8,128)(2,1)S(1)}, bf16[16,3024]{1,0:T(8,128)(2,1)S(1)}, u32[]{:S(2)}, u32[]{:S(2)}) %collective-permute-start) | collective-permute-done | bytes 96800 | tf_op jit(solution)/shard_map/ppermute | solution.py:238
  7.9 3.1 %collective-permute-done.1.refs_2_ = bf16[16,3024]{1,0:T(8,128)(2,1)S(1)} collective-permute-done((bf16[16,3024]{1,0:T(8,128)(2,1)S(1)}, bf16[16,3024]{1,0:T(8,128)(2,1)S(1)}, u32[]{:S(2)}, u32[]{:S(2)}) %collective-permute-start.1) | collective-permute-done | bytes 96800 | tf_op jit(solution)/shard_map/ppermute | solution.py:238
  10.9 1.5 %collective-permute-done.2.refs_3_ = bf16[16,3024]{1,0:T(8,128)(2,1)S(1)} collective-permute-done((bf16[16,3024]{1,0:T(8,128)(2,1)S(1)}, bf16[16,3024]{1,0:T(8,128)(2,1)S(1)}, u32[]{:S(2)}, u32[]{:S(2)}) %collective-permute-start.2) | collective-permute-done | bytes 96800 | tf_op jit(solution)/shard_map/ppermute | solution.py:238
  13.2 0.6 %collective-permute-done.3.other_ref = bf16[4,16,432]{2,1,0:T(8,128)(2,1)S(1)} collective-permute-done((bf16[4,16,432]{2,1,0:T(8,128)(2,1)S(1)}, bf16[4,16,432]{2,1,0:T(8,128)(2,1)S(1)}, u32[]{:S(2)}, u32[]{:S(2)}) %collective-permute-start.3) | collective-permute-done | bytes 55328 | tf_op jit(solution)/shard_map/ppermute | solution.py:238
  13.9 1.0 %shard_map.79 = (bf16[2,16,1152]{2,1,0:T(8,128)(2,1)S(1)}, bf16[2,16,1152]{2,1,0:T(8,128)(2,1)S(1)}, bf16[2,16,1152]{2,1,0:T(8,128)(2,1)S(1)}, bf16[2,16,1152]{2,1,0:T(8,128)(2,1)S(1)}) custom-call(bf16[512,1152]{1,0:T(8,128)(2,1)S(1)} %bitcast.1, bf16[4,16,432]{2,1,0:T(8,128)(2,1)S(1)} %shard_map.78.own_ref.refs_5_, ...), custom_call_target="tpu_custom_call" | custom-call | flops 10000000000 | tf_op jit(solution)/shard_map/pallas_call | solution.py:22
  14.9 0.8 %collective-permute-start.4 = (bf16[2,16,1152]{2,1,0:T(8,128)(2,1)S(1)}, bf16[2,16,1152]{2,1,0:T(8,128)(2,1)S(1)}, u32[]{:S(2)}, u32[]{:S(2)}) collective-permute-start(bf16[2,16,1152]{2,1,0:T(8,128)(2,1)S(1)} %get-tuple-element.27), channel_id=1, source_target_pairs={{0,28},{4,24},{8,20},{12,16},{16,12},{20,8},{24,4},{28,0},{1,29},{... | collective-permute-start | bytes 221192 | tf_op jit(solution)/shard_map/ppermute | solution.py:238
  15.7 1.0 %collective-permute-start.5 = (bf16[2,16,1152]{2,1,0:T(8,128)(2,1)S(1)}, bf16[2,16,1152]{2,1,0:T(8,128)(2,1)S(1)}, u32[]{:S(2)}, u32[]{:S(2)}) collective-permute-start(bf16[2,16,1152]{2,1,0:T(8,128)(2,1)S(1)} %get-tuple-element.28), channel_id=1, source_target_pairs={{0,12},{4,8},{8,4},{12,0},{16,28},{20,24},{24,20},{28,16},{1,13},{... | collective-permute-start | bytes 221192 | tf_op jit(solution)/shard_map/ppermute | solution.py:238
  16.7 1.2 %collective-permute-start.6 = (bf16[2,16,1152]{2,1,0:T(8,128)(2,1)S(1)}, bf16[2,16,1152]{2,1,0:T(8,128)(2,1)S(1)}, u32[]{:S(2)}, u32[]{:S(2)}) collective-permute-start(bf16[2,16,1152]{2,1,0:T(8,128)(2,1)S(1)} %get-tuple-element.29), channel_id=1, source_target_pairs={{0,20},{4,16},{8,28},{12,24},{16,4},{20,0},{24,12},{28,8},{1,21},{... | collective-permute-start | bytes 221192 | tf_op jit(solution)/shard_map/ppermute | solution.py:238
  17.9 1.6 %collective-permute-start.11 = (bf16[8,1152]{1,0:T(8,128)(2,1)S(1)}, bf16[8,1152]{1,0:T(8,128)(2,1)S(1)}, u32[]{:S(2)}, u32[]{:S(2)}) collective-permute-start(bf16[8,1152]{1,0:T(8,128)(2,1)S(1)} %copy-done.1), channel_id=1, source_target_pairs={{0,1},{1,2},{2,3},{3,0},{4,5},{5,6},{6,7},{7,4},{8,9},{9,10},{10,1... | collective-permute-start | bytes 55304 | tf_op jit(solution)/shard_map/ppermute | solution.py:243
  19.5 2.6 %collective-permute-start.12 = (bf16[8,1152]{1,0:T(8,128)(2,1)S(1)}, bf16[8,1152]{1,0:T(8,128)(2,1)S(1)}, u32[]{:S(2)}, u32[]{:S(2)}) collective-permute-start(bf16[8,1152]{1,0:T(8,128)(2,1)S(1)} %copy-done.1), channel_id=1, source_target_pairs={{0,2},{1,3},{2,0},{3,1},{4,6},{5,7},{6,4},{7,5},{8,10},{9,11},{10,... | collective-permute-start | bytes 55304 | tf_op jit(solution)/shard_map/ppermute | solution.py:243
  22.5 1.4 %collective-permute-start.13 = (bf16[8,1152]{1,0:T(8,128)(2,1)S(1)}, bf16[8,1152]{1,0:T(8,128)(2,1)S(1)}, u32[]{:S(2)}, u32[]{:S(2)}) collective-permute-start(bf16[8,1152]{1,0:T(8,128)(2,1)S(1)} %copy-done.1), channel_id=1, source_target_pairs={{0,3},{1,0},{2,1},{3,2},{4,7},{5,4},{6,5},{7,6},{8,11},{9,8},{10,9... | collective-permute-start | bytes 55304 | tf_op jit(solution)/shard_map/ppermute | solution.py:243
  23.9 0.5 %shard_map.82 = (bf16[8,1152]{1,0:T(8,128)(2,1)S(1)}, bf16[8,1152]{1,0:T(8,128)(2,1)S(1)}, bf16[8,1152]{1,0:T(8,128)(2,1)S(1)}, bf16[8,1152]{1,0:T(8,128)(2,1)S(1)}) custom-call(bf16[2,16,1152]{2,1,0:T(8,128)(2,1)S(1)} %get-tuple-element.26.refs_0_, bf16[2,16,1152]{2,1,0:T(8,128)(2,1)S(1)} %collective-permute-done.4.refs_1_, ...), custom_call_target="tpu_custom_call" | custom-call | tf_op jit(solution)/shard_map/pallas_call | solution.py:22
  24.6 1.9 %collective-permute-start.8 = (bf16[8,1152]{1,0:T(8,128)(2,1)S(1)}, bf16[8,1152]{1,0:T(8,128)(2,1)S(1)}, u32[]{:S(2)}, u32[]{:S(2)}) collective-permute-start(bf16[8,1152]{1,0:T(8,128)(2,1)S(1)} %get-tuple-element.33), channel_id=1, source_target_pairs={{0,28},{4,24},{8,20},{12,16},{16,12},{20,8},{24,4},{28,0},{1,29},{... | collective-permute-start | bytes 55304 | tf_op jit(solution)/shard_map/ppermute | solution.py:238
  26.6 0.8 %collective-permute-start.9 = (bf16[8,1152]{1,0:T(8,128)(2,1)S(1)}, bf16[8,1152]{1,0:T(8,128)(2,1)S(1)}, u32[]{:S(2)}, u32[]{:S(2)}) collective-permute-start(bf16[8,1152]{1,0:T(8,128)(2,1)S(1)} %get-tuple-element.34), channel_id=1, source_target_pairs={{0,12},{4,8},{8,4},{12,0},{16,28},{20,24},{24,20},{28,16},{1,13},{... | collective-permute-start | bytes 55304 | tf_op jit(solution)/shard_map/ppermute | solution.py:238
  27.7 1.1 %collective-permute-done.8.refs_1_ = bf16[8,1152]{1,0:T(8,128)(2,1)S(1)} collective-permute-done((bf16[8,1152]{1,0:T(8,128)(2,1)S(1)}, bf16[8,1152]{1,0:T(8,128)(2,1)S(1)}, u32[]{:S(2)}, u32[]{:S(2)}) %collective-permute-start.8) | collective-permute-done | bytes 18464 | tf_op jit(solution)/shard_map/ppermute | solution.py:238
  28.7 1.0 %collective-permute-done.9.refs_2_ = bf16[8,1152]{1,0:T(8,128)(2,1)S(1)} collective-permute-done((bf16[8,1152]{1,0:T(8,128)(2,1)S(1)}, bf16[8,1152]{1,0:T(8,128)(2,1)S(1)}, u32[]{:S(2)}, u32[]{:S(2)}) %collective-permute-start.9) | collective-permute-done | bytes 18464 | tf_op jit(solution)/shard_map/ppermute | solution.py:238
  29.9 1.7 %collective-permute-start.14 = (bf16[8,1152]{1,0:T(8,128)(2,1)S(1)}, bf16[8,1152]{1,0:T(8,128)(2,1)S(1)}, u32[]{:S(2)}, u32[]{:S(2)}) collective-permute-start(bf16[8,1152]{1,0:T(8,128)(2,1)S(1)} %get-tuple-element.41.refs_0_), channel_id=1, source_target_pairs={{0,3},{1,2},{2,1},{3,0},{4,7},{5,6},{6,5},{7,4},{8,11},{9,10},{10,... | collective-permute-start | bytes 55304 | tf_op jit(solution)/shard_map/ppermute | solution.py:238
  32.1 2.2 %collective-permute-start.16 = (bf16[8,1152]{1,0:T(8,128)(2,1)S(1)}, bf16[8,1152]{1,0:T(8,128)(2,1)S(1)}, u32[]{:S(2)}, u32[]{:S(2)}) collective-permute-start(bf16[8,1152]{1,0:T(8,128)(2,1)S(1)} %get-tuple-element.41.refs_0_), channel_id=1, source_target_pairs={{0,1},{1,0},{2,3},{3,2},{4,5},{5,4},{6,7},{7,6},{8,9},{9,8},{10,11... | collective-permute-start | bytes 55304 | tf_op jit(solution)/shard_map/ppermute | solution.py:238
  34.3 1.0 %shard_map.85 = f32[8,1152]{1,0:T(8,128)} custom-call(f32[8,1152]{1,0:T(8,128)S(1)} %get-tuple-element.37.unit_ref, f32[8,128]{1,0:T(8,128)S(1)} %get-tuple-element.38.inverse_ref, bf16[32,1152]{1,0:T(8,128)(2,1)S(1)} %get-tuple-element.39.refs_0_), custom_call_target="tpu_custom_call" | custom-call | tf_op jit(solution)/shard_map/pallas_call | solution.py:22
  35.4 0.8 %collective-permute-done.15.refs_2_ = bf16[8,1152]{1,0:T(8,128)(2,1)S(1)} collective-permute-done((bf16[8,1152]{1,0:T(8,128)(2,1)S(1)}, bf16[8,1152]{1,0:T(8,128)(2,1)S(1)}, u32[]{:S(2)}, u32[]{:S(2)}) %collective-permute-start.15) | collective-permute-done | bytes 18464 | tf_op jit(solution)/shard_map/ppermute | solution.py:238
  36.2 1.0 %shard_map.86 = f32[8,1152]{1,0:T(8,128)} custom-call(f32[8,1152]{1,0:T(8,128)S(1)} %get-tuple-element.40.unit_ref, f32[8,128]{1,0:T(8,128)S(1)} %get-tuple-element.36.refs_4_.inverse_ref, bf16[8,1152]{1,0:T(8,128)(2,1)S(1)} %get-tuple-element.41.refs_0_, bf16[8,1152]{1,0:T(8,128)(2,1)S(1)} %collective-permute-done.14.refs_1_, ...), custom_call_target="tpu_custom_call" | custom-call | tf_op jit(solution)/shard_map/pallas_call | solution.py:22
  (26 shorter events, 2.5 us)
Async XLA Ops:
  0.6 12.1 %copy-start = (bf16[144,1152]{1,0:T(8,128)(2,1)S(1)}, bf16[144,1152]{1,0:T(8,128)(2,1)}, u32[]{:S(2)}) copy-start(bf16[144,1152]{1,0:T(8,128)(2,1)} %refs_4_.3) | copy-start | bytes 995332
  2.2 11.6 %copy-start.2 = (bf16[8,64,1152]{2,1,0:T(8,128)(2,1)S(1)}, bf16[8,64,1152]{2,1,0:T(8,128)(2,1)}, u32[]{:S(2)}) copy-start(bf16[8,64,1152]{2,1,0:T(8,128)(2,1)} %param.6) | copy-start | bytes 3538948
  2.2 5.6 %collective-permute-start = (bf16[16,3024]{1,0:T(8,128)(2,1)S(1)}, bf16[16,3024]{1,0:T(8,128)(2,1)S(1)}, u32[]{:S(2)}, u32[]{:S(2)}) collective-permute-start(bf16[16,3024]{1,0:T(8,128)(2,1)S(1)} %get-tuple-element.23), channel_id=1, source_target_pairs={{0,12},{4,8},{8,4},{12,0},{16,28},{20,24},{24,20},{28,16},{1,13},{... | collective-permute-start | bytes 290312 | tf_op jit(solution)/shard_map/ppermute | solution.py:238
  4.7 6.3 %collective-permute-start.1 = (bf16[16,3024]{1,0:T(8,128)(2,1)S(1)}, bf16[16,3024]{1,0:T(8,128)(2,1)S(1)}, u32[]{:S(2)}, u32[]{:S(2)}) collective-permute-start(bf16[16,3024]{1,0:T(8,128)(2,1)S(1)} %get-tuple-element.24), channel_id=1, source_target_pairs={{0,20},{4,16},{8,28},{12,24},{16,4},{20,0},{24,12},{28,8},{1,21},{... | collective-permute-start | bytes 290312 | tf_op jit(solution)/shard_map/ppermute | solution.py:238
  6.5 6.0 %collective-permute-start.2 = (bf16[16,3024]{1,0:T(8,128)(2,1)S(1)}, bf16[16,3024]{1,0:T(8,128)(2,1)S(1)}, u32[]{:S(2)}, u32[]{:S(2)}) collective-permute-start(bf16[16,3024]{1,0:T(8,128)(2,1)S(1)} %get-tuple-element.25), channel_id=1, source_target_pairs={{0,28},{4,24},{8,20},{12,16},{16,12},{20,8},{24,4},{28,0},{1,29},{... | collective-permute-start | bytes 290312 | tf_op jit(solution)/shard_map/ppermute | solution.py:238
  12.5 1.3 %collective-permute-start.3 = (bf16[4,16,432]{2,1,0:T(8,128)(2,1)S(1)}, bf16[4,16,432]{2,1,0:T(8,128)(2,1)S(1)}, u32[]{:S(2)}, u32[]{:S(2)}) collective-permute-start(bf16[4,16,432]{2,1,0:T(8,128)(2,1)S(1)} %shard_map.78.own_ref.refs_5_), channel_id=1, source_target_pairs={{0,4},{4,0},{8,12},{12,8},{16,20},{20,16},{24,28},{28,24},{1,5},{5... | collective-permute-start | bytes 165896 | tf_op jit(solution)/shard_map/ppermute | solution.py:238
  12.8 6.8 %collective-permute-start.7 = (bf16[9,16,2592]{2,1,0:T(8,128)(2,1)S(1)}, bf16[9,16,2592]{2,1,0:T(8,128)(2,1)S(1)}, u32[]{:S(2)}, u32[]{:S(2)}) collective-permute-start(bf16[9,16,2592]{2,1,0:T(8,128)(2,1)S(1)} %shard_map.80), channel_id=1, source_target_pairs={{0,4},{4,0},{8,12},{12,8},{16,20},{20,16},{24,28},{28,24},{1,5},{5... | collective-permute-start | bytes 2239496 | tf_op jit(solution)/shard_map/ppermute | solution.py:238
  13.9 4.1 %copy-start.1 = (bf16[8,1152]{1,0:T(8,128)(2,1)S(1)}, bf16[8,1152]{1,0:T(8,128)(2,1)}, u32[]{:S(2)}) copy-start(bf16[8,1152]{1,0:T(8,128)(2,1)} %refs_0_.1) | copy-start | bytes 55300
  14.9 7.6 %collective-permute-start.4 = (bf16[2,16,1152]{2,1,0:T(8,128)(2,1)S(1)}, bf16[2,16,1152]{2,1,0:T(8,128)(2,1)S(1)}, u32[]{:S(2)}, u32[]{:S(2)}) collective-permute-start(bf16[2,16,1152]{2,1,0:T(8,128)(2,1)S(1)} %get-tuple-element.27), channel_id=1, source_target_pairs={{0,28},{4,24},{8,20},{12,16},{16,12},{20,8},{24,4},{28,0},{1,29},{... | collective-permute-start | bytes 221192 | tf_op jit(solution)/shard_map/ppermute | solution.py:238
  15.7 8.2 %collective-permute-start.5 = (bf16[2,16,1152]{2,1,0:T(8,128)(2,1)S(1)}, bf16[2,16,1152]{2,1,0:T(8,128)(2,1)S(1)}, u32[]{:S(2)}, u32[]{:S(2)}) collective-permute-start(bf16[2,16,1152]{2,1,0:T(8,128)(2,1)S(1)} %get-tuple-element.28), channel_id=1, source_target_pairs={{0,12},{4,8},{8,4},{12,0},{16,28},{20,24},{24,20},{28,16},{1,13},{... | collective-permute-start | bytes 221192 | tf_op jit(solution)/shard_map/ppermute | solution.py:238
  16.7 7.2 %collective-permute-start.6 = (bf16[2,16,1152]{2,1,0:T(8,128)(2,1)S(1)}, bf16[2,16,1152]{2,1,0:T(8,128)(2,1)S(1)}, u32[]{:S(2)}, u32[]{:S(2)}) collective-permute-start(bf16[2,16,1152]{2,1,0:T(8,128)(2,1)S(1)} %get-tuple-element.29), channel_id=1, source_target_pairs={{0,20},{4,16},{8,28},{12,24},{16,4},{20,0},{24,12},{28,8},{1,21},{... | collective-permute-start | bytes 221192 | tf_op jit(solution)/shard_map/ppermute | solution.py:238
  17.9 8.6 %collective-permute-start.11 = (bf16[8,1152]{1,0:T(8,128)(2,1)S(1)}, bf16[8,1152]{1,0:T(8,128)(2,1)S(1)}, u32[]{:S(2)}, u32[]{:S(2)}) collective-permute-start(bf16[8,1152]{1,0:T(8,128)(2,1)S(1)} %copy-done.1), channel_id=1, source_target_pairs={{0,1},{1,2},{2,3},{3,0},{4,5},{5,6},{6,7},{7,4},{8,9},{9,10},{10,1... | collective-permute-start | bytes 55304 | tf_op jit(solution)/shard_map/ppermute | solution.py:243
  19.5 7.8 %collective-permute-start.12 = (bf16[8,1152]{1,0:T(8,128)(2,1)S(1)}, bf16[8,1152]{1,0:T(8,128)(2,1)S(1)}, u32[]{:S(2)}, u32[]{:S(2)}) collective-permute-start(bf16[8,1152]{1,0:T(8,128)(2,1)S(1)} %copy-done.1), channel_id=1, source_target_pairs={{0,2},{1,3},{2,0},{3,1},{4,6},{5,7},{6,4},{7,5},{8,10},{9,11},{10,... | collective-permute-start | bytes 55304 | tf_op jit(solution)/shard_map/ppermute | solution.py:243
  22.5 4.9 %collective-permute-start.13 = (bf16[8,1152]{1,0:T(8,128)(2,1)S(1)}, bf16[8,1152]{1,0:T(8,128)(2,1)S(1)}, u32[]{:S(2)}, u32[]{:S(2)}) collective-permute-start(bf16[8,1152]{1,0:T(8,128)(2,1)S(1)} %copy-done.1), channel_id=1, source_target_pairs={{0,3},{1,0},{2,1},{3,2},{4,7},{5,4},{6,5},{7,6},{8,11},{9,8},{10,9... | collective-permute-start | bytes 55304 | tf_op jit(solution)/shard_map/ppermute | solution.py:243
  24.4 3.3 %collective-permute-start.10 = (bf16[8,1152]{1,0:T(8,128)(2,1)S(1)}, bf16[8,1152]{1,0:T(8,128)(2,1)S(1)}, u32[]{:S(2)}, u32[]{:S(2)}) collective-permute-start(bf16[8,1152]{1,0:T(8,128)(2,1)S(1)} %get-tuple-element.35), channel_id=1, source_target_pairs={{0,20},{4,16},{8,28},{12,24},{16,4},{20,0},{24,12},{28,8},{1,21},{... | collective-permute-start | bytes 55304 | tf_op jit(solution)/shard_map/ppermute | solution.py:238
  24.6 4.1 %collective-permute-start.8 = (bf16[8,1152]{1,0:T(8,128)(2,1)S(1)}, bf16[8,1152]{1,0:T(8,128)(2,1)S(1)}, u32[]{:S(2)}, u32[]{:S(2)}) collective-permute-start(bf16[8,1152]{1,0:T(8,128)(2,1)S(1)} %get-tuple-element.33), channel_id=1, source_target_pairs={{0,28},{4,24},{8,20},{12,16},{16,12},{20,8},{24,4},{28,0},{1,29},{... | collective-permute-start | bytes 55304 | tf_op jit(solution)/shard_map/ppermute | solution.py:238
  26.6 3.2 %collective-permute-start.9 = (bf16[8,1152]{1,0:T(8,128)(2,1)S(1)}, bf16[8,1152]{1,0:T(8,128)(2,1)S(1)}, u32[]{:S(2)}, u32[]{:S(2)}) collective-permute-start(bf16[8,1152]{1,0:T(8,128)(2,1)S(1)} %get-tuple-element.34), channel_id=1, source_target_pairs={{0,12},{4,8},{8,4},{12,0},{16,28},{20,24},{24,20},{28,16},{1,13},{... | collective-permute-start | bytes 55304 | tf_op jit(solution)/shard_map/ppermute | solution.py:238
  29.9 5.6 %collective-permute-start.14 = (bf16[8,1152]{1,0:T(8,128)(2,1)S(1)}, bf16[8,1152]{1,0:T(8,128)(2,1)S(1)}, u32[]{:S(2)}, u32[]{:S(2)}) collective-permute-start(bf16[8,1152]{1,0:T(8,128)(2,1)S(1)} %get-tuple-element.41.refs_0_), channel_id=1, source_target_pairs={{0,3},{1,2},{2,1},{3,0},{4,7},{5,6},{6,5},{7,4},{8,11},{9,10},{10,... | collective-permute-start | bytes 55304 | tf_op jit(solution)/shard_map/ppermute | solution.py:238
  31.6 4.7 %collective-permute-start.15 = (bf16[8,1152]{1,0:T(8,128)(2,1)S(1)}, bf16[8,1152]{1,0:T(8,128)(2,1)S(1)}, u32[]{:S(2)}, u32[]{:S(2)}) collective-permute-start(bf16[8,1152]{1,0:T(8,128)(2,1)S(1)} %get-tuple-element.41.refs_0_), channel_id=1, source_target_pairs={{0,2},{1,3},{2,0},{3,1},{4,6},{5,7},{6,4},{7,5},{8,10},{9,11},{10,... | collective-permute-start | bytes 55304 | tf_op jit(solution)/shard_map/ppermute | solution.py:238
  32.1 4.2 %collective-permute-start.16 = (bf16[8,1152]{1,0:T(8,128)(2,1)S(1)}, bf16[8,1152]{1,0:T(8,128)(2,1)S(1)}, u32[]{:S(2)}, u32[]{:S(2)}) collective-permute-start(bf16[8,1152]{1,0:T(8,128)(2,1)S(1)} %get-tuple-element.41.refs_0_), channel_id=1, source_target_pairs={{0,1},{1,0},{2,3},{3,2},{4,5},{5,4},{6,7},{7,6},{8,9},{9,8},{10,11... | collective-permute-start | bytes 55304 | tf_op jit(solution)/shard_map/ppermute | solution.py:238

commit v9 on v7

--- a/solution.py
+++ b/solution.py
@@ -62,8 +62,8 @@
     return high, middle, (rest - middle.astype(F32)).astype(BF16)
 
 
-def far_first(chips):
-    return [0, chips - 1, *range(1, chips - 1)]
+def near_first(chips):
+    return list(range(chips))
 
 
 def chip_and_core():
@@ -156,7 +156,7 @@
     weights = expo / jnp.sum(expo, axis=2, keepdims=True)
     weights = weights.reshape(HEADS * images, x.shape[0])
     every[...] = nn(weights.astype(BF16), x).astype(BF16).reshape(every.shape)
-    for m, out_ref in zip(far_first(chips), outs):
+    for m, out_ref in zip(near_first(chips), outs):
         out_ref[...] = every[chip ^ m]
 
 
@@ -323,14 +323,14 @@
     partial_embed = call(
         functools.partial(project_kernel, images, chips),
         [struct((images, width), BF16)] * chips,
-        *exchange_chips(mixed, devices, far_first(chips)),
+        *exchange_chips(mixed, devices, near_first(chips)),
         w_values,
         w_outs,
     )
     unit, inverse, rounded = call(
         functools.partial(unit_image_kernel, chips),
         (row, column, struct((images, width), BF16)),
-        *exchange_chips(partial_embed, devices, far_first(chips)),
+        *exchange_chips(partial_embed, devices, near_first(chips)),
         inverse_text,
     )
     all_images = [exchange(rounded, blocks, m, "blk") for m in range(blocks - 1, 0, -1)]

time: 37.4 us -> 37 us (0.989)
  waiting for transfers between devices: 9.98 us -> 9.45 us
    ppermute x14, waiting for transfers between devices: 5.78 us -> 5.25 us  [exchange(): return lax.ppermute(array, axis, [(i, i ^ flip) for i in range(devices)])]
  transfers between devices with their start and end apart: 17 -> 17, of which waited for: 8 -> 9; matrix products, arithmetic and copies ran while one was open for 0% -> 0% of each run, Pallas kernels for 8% -> 8%
where the time goes in v9:
time: 37 us; the launch traced here: 36.9 us
  starting transfers between devices  20.9 us (56%)
  waiting for transfers between devices  9.45 us (26%)
  Pallas kernels  5.77 us (16%)
  between operations  0.73 us (2%)
    ppermute x14, starting transfers between devices, exchange(): return lax.ppermute(array, axis, [(i, i ^ flip) for i in range(devices)])  15.4 us
    pallas_call x10, Pallas kernels, call(): pl.pallas_call(body, out_shape=out, in_specs=[pl.BlockSpec(memory_space=s...  5.77 us
    ppermute x3, starting transfers between devices, all_blocks(): lax.ppermute(array, 'blk', [(i, (i + by) % blocks) for i in range(blocks)])  5.51 us
    ppermute x14, waiting for transfers between devices, exchange(): return lax.ppermute(array, axis, [(i, i ^ flip) for i in range(devices)])  5.25 us
    ppermute x3, waiting for transfers between devices, all_blocks(): lax.ppermute(array, 'blk', [(i, (i + by) % blocks) for i in range(blocks)])  4.2 us
  transfers between devices with their start and end apart: 17, of which 9 were waited for; matrix products, arithmetic and copies ran while one was open for 0% of the time, Pallas kernels for 8%

profile of v9, /device:TPU:0, one launch (start us, length us, event | category | flops | bytes accessed | tf_op | source)
XLA Modules:
  0.0 36.9 jit_solution(10592025915594090529)
XLA Ops:
  0.6 1.6 %shard_map.77 = (bf16[16,3024]{1,0:T(8,128)(2,1)S(1)}, bf16[16,3024]{1,0:T(8,128)(2,1)S(1)}, bf16[16,3024]{1,0:T(8,128)(2,1)S(1)}, bf16[16,3024]{1,0:T(8,128)(2,1)S(1)}) custom-call(bf16[1152]{0:T(1024)(128)(2,1)} %probe_hbm.1, bf16[144,1152]{1,0:T(8,128)(2,1)} %w_key_hbm.1, bf16[144,1152]{1,0:T(8,128)(2,1)} %w_value_hbm.1), custom_call_target="tpu_custom_call" | custom-call | tf_op jit(solution)/shard_map/pallas_call | solution.py:22
  2.2 2.4 %collective-permute-start = (bf16[16,3024]{1,0:T(8,128)(2,1)S(1)}, bf16[16,3024]{1,0:T(8,128)(2,1)S(1)}, u32[]{:S(2)}, u32[]{:S(2)}) collective-permute-start(bf16[16,3024]{1,0:T(8,128)(2,1)S(1)} %get-tuple-element.23), channel_id=1, source_target_pairs={{0,12},{4,8},{8,4},{12,0},{16,28},{20,24},{24,20},{28,16},{1,13},{... | collective-permute-start | bytes 290312 | tf_op jit(solution)/shard_map/ppermute | solution.py:236
  4.7 1.8 %collective-permute-start.1 = (bf16[16,3024]{1,0:T(8,128)(2,1)S(1)}, bf16[16,3024]{1,0:T(8,128)(2,1)S(1)}, u32[]{:S(2)}, u32[]{:S(2)}) collective-permute-start(bf16[16,3024]{1,0:T(8,128)(2,1)S(1)} %get-tuple-element.24), channel_id=1, source_target_pairs={{0,20},{4,16},{8,28},{12,24},{16,4},{20,0},{24,12},{28,8},{1,21},{... | collective-permute-start | bytes 290312 | tf_op jit(solution)/shard_map/ppermute | solution.py:236
  6.5 1.6 %collective-permute-start.3 = (bf16[8,1152]{1,0:T(8,128)(2,1)}, bf16[8,1152]{1,0:T(8,128)(2,1)S(1)}, u32[]{:S(2)}, u32[]{:S(2)}) collective-permute-start(bf16[8,1152]{1,0:T(8,128)(2,1)} %refs_0_.1), channel_id=1, source_target_pairs={{0,1},{1,2},{2,3},{3,0},{4,5},{5,6},{6,7},{7,4},{8,9},{9,10},{10,1... | collective-permute-start | bytes 55304 | tf_op jit(solution)/shard_map/ppermute | solution.py:241
  8.1 4.2 %collective-permute-done.3.refs_4_.refs_1_ = bf16[8,1152]{1,0:T(8,128)(2,1)S(1)} collective-permute-done((bf16[8,1152]{1,0:T(8,128)(2,1)}, bf16[8,1152]{1,0:T(8,128)(2,1)S(1)}, u32[]{:S(2)}, u32[]{:S(2)}) %collective-permute-start.3) | collective-permute-done | bytes 18464 | tf_op jit(solution)/shard_map/ppermute | solution.py:241
  12.8 0.5 %collective-permute-start.8 = (bf16[9,16,2592]{2,1,0:T(8,128)(2,1)S(1)}, bf16[9,16,2592]{2,1,0:T(8,128)(2,1)S(1)}, u32[]{:S(2)}, u32[]{:S(2)}) collective-permute-start(bf16[9,16,2592]{2,1,0:T(8,128)(2,1)S(1)} %shard_map.80), channel_id=1, source_target_pairs={{0,4},{4,0},{8,12},{12,8},{16,20},{20,16},{24,28},{28,24},{1,5},{5... | collective-permute-start | bytes 2239496 | tf_op jit(solution)/shard_map/ppermute | solution.py:236
  13.2 0.6 %collective-permute-done.4.other_ref = bf16[4,16,432]{2,1,0:T(8,128)(2,1)S(1)} collective-permute-done((bf16[4,16,432]{2,1,0:T(8,128)(2,1)S(1)}, bf16[4,16,432]{2,1,0:T(8,128)(2,1)S(1)}, u32[]{:S(2)}, u32[]{:S(2)}) %collective-permute-start.4) | collective-permute-done | bytes 55328 | tf_op jit(solution)/shard_map/ppermute | solution.py:236
  13.9 1.0 %shard_map.79 = (bf16[2,16,1152]{2,1,0:T(8,128)(2,1)S(1)}, bf16[2,16,1152]{2,1,0:T(8,128)(2,1)S(1)}, bf16[2,16,1152]{2,1,0:T(8,128)(2,1)S(1)}, bf16[2,16,1152]{2,1,0:T(8,128)(2,1)S(1)}) custom-call(bf16[512,1152]{1,0:T(8,128)(2,1)S(1)} %bitcast.1, bf16[4,16,432]{2,1,0:T(8,128)(2,1)S(1)} %shard_map.78.own_ref.refs_5_, ...), custom_call_target="tpu_custom_call" | custom-call | flops 10000000000 | tf_op jit(solution)/shard_map/pallas_call | solution.py:22
  14.9 1.1 %collective-permute-start.5 = (bf16[2,16,1152]{2,1,0:T(8,128)(2,1)S(1)}, bf16[2,16,1152]{2,1,0:T(8,128)(2,1)S(1)}, u32[]{:S(2)}, u32[]{:S(2)}) collective-permute-start(bf16[2,16,1152]{2,1,0:T(8,128)(2,1)S(1)} %get-tuple-element.27), channel_id=1, source_target_pairs={{0,12},{4,8},{8,4},{12,0},{16,28},{20,24},{24,20},{28,16},{1,13},{... | collective-permute-start | bytes 221192 | tf_op jit(solution)/shard_map/ppermute | solution.py:236
  16.0 1.4 %collective-permute-start.6 = (bf16[2,16,1152]{2,1,0:T(8,128)(2,1)S(1)}, bf16[2,16,1152]{2,1,0:T(8,128)(2,1)S(1)}, u32[]{:S(2)}, u32[]{:S(2)}) collective-permute-start(bf16[2,16,1152]{2,1,0:T(8,128)(2,1)S(1)} %get-tuple-element.28), channel_id=1, source_target_pairs={{0,20},{4,16},{8,28},{12,24},{16,4},{20,0},{24,12},{28,8},{1,21},{... | collective-permute-start | bytes 221192 | tf_op jit(solution)/shard_map/ppermute | solution.py:236
  17.4 0.5 %collective-permute-start.7 = (bf16[2,16,1152]{2,1,0:T(8,128)(2,1)S(1)}, bf16[2,16,1152]{2,1,0:T(8,128)(2,1)S(1)}, u32[]{:S(2)}, u32[]{:S(2)}) collective-permute-start(bf16[2,16,1152]{2,1,0:T(8,128)(2,1)S(1)} %get-tuple-element.29), channel_id=1, source_target_pairs={{0,28},{4,24},{8,20},{12,16},{16,12},{20,8},{24,4},{28,0},{1,29},{... | collective-permute-start | bytes 221192 | tf_op jit(solution)/shard_map/ppermute | solution.py:236
  17.9 2.6 %collective-permute-start.12 = (bf16[8,1152]{1,0:T(8,128)(2,1)S(1)}, bf16[8,1152]{1,0:T(8,128)(2,1)S(1)}, u32[]{:S(2)}, u32[]{:S(2)}) collective-permute-start(bf16[8,1152]{1,0:T(8,128)(2,1)S(1)} %copy-done.1), channel_id=1, source_target_pairs={{0,2},{1,3},{2,0},{3,1},{4,6},{5,7},{6,4},{7,5},{8,10},{9,11},{10,... | collective-permute-start | bytes 55304 | tf_op jit(solution)/shard_map/ppermute | solution.py:241
  20.5 1.4 %collective-permute-start.13 = (bf16[8,1152]{1,0:T(8,128)(2,1)S(1)}, bf16[8,1152]{1,0:T(8,128)(2,1)S(1)}, u32[]{:S(2)}, u32[]{:S(2)}) collective-permute-start(bf16[8,1152]{1,0:T(8,128)(2,1)S(1)} %copy-done.1), channel_id=1, source_target_pairs={{0,3},{1,0},{2,1},{3,2},{4,7},{5,4},{6,5},{7,6},{8,11},{9,8},{10,9... | collective-permute-start | bytes 55304 | tf_op jit(solution)/shard_map/ppermute | solution.py:241
  21.9 0.3 shard_map.81
  22.5 0.5 %shard_map.82 = (bf16[8,1152]{1,0:T(8,128)(2,1)S(1)}, bf16[8,1152]{1,0:T(8,128)(2,1)S(1)}, bf16[8,1152]{1,0:T(8,128)(2,1)S(1)}, bf16[8,1152]{1,0:T(8,128)(2,1)S(1)}) custom-call(bf16[2,16,1152]{2,1,0:T(8,128)(2,1)S(1)} %get-tuple-element.26.refs_0_, bf16[2,16,1152]{2,1,0:T(8,128)(2,1)S(1)} %collective-permute-done.5.refs_1_, ...), custom_call_target="tpu_custom_call" | custom-call | tf_op jit(solution)/shard_map/pallas_call | solution.py:22
  23.1 0.9 %collective-permute-start.10 = (bf16[8,1152]{1,0:T(8,128)(2,1)S(1)}, bf16[8,1152]{1,0:T(8,128)(2,1)S(1)}, u32[]{:S(2)}, u32[]{:S(2)}) collective-permute-start(bf16[8,1152]{1,0:T(8,128)(2,1)S(1)} %get-tuple-element.34), channel_id=1, source_target_pairs={{0,20},{4,16},{8,28},{12,24},{16,4},{20,0},{24,12},{28,8},{1,21},{... | collective-permute-start | bytes 55304 | tf_op jit(solution)/shard_map/ppermute | solution.py:236
  23.9 1.0 %collective-permute-start.11 = (bf16[8,1152]{1,0:T(8,128)(2,1)S(1)}, bf16[8,1152]{1,0:T(8,128)(2,1)S(1)}, u32[]{:S(2)}, u32[]{:S(2)}) collective-permute-start(bf16[8,1152]{1,0:T(8,128)(2,1)S(1)} %get-tuple-element.35), channel_id=1, source_target_pairs={{0,28},{4,24},{8,20},{12,16},{16,12},{20,8},{24,4},{28,0},{1,29},{... | collective-permute-start | bytes 55304 | tf_op jit(solution)/shard_map/ppermute | solution.py:236
  25.0 1.2 %collective-permute-start.9 = (bf16[8,1152]{1,0:T(8,128)(2,1)S(1)}, bf16[8,1152]{1,0:T(8,128)(2,1)S(1)}, u32[]{:S(2)}, u32[]{:S(2)}) collective-permute-start(bf16[8,1152]{1,0:T(8,128)(2,1)S(1)} %get-tuple-element.33), channel_id=1, source_target_pairs={{0,12},{4,8},{8,4},{12,0},{16,28},{20,24},{24,20},{28,16},{1,13},{... | collective-permute-start | bytes 55304 | tf_op jit(solution)/shard_map/ppermute | solution.py:236
  26.3 1.7 %collective-permute-done.11.refs_3_ = bf16[8,1152]{1,0:T(8,128)(2,1)S(1)} collective-permute-done((bf16[8,1152]{1,0:T(8,128)(2,1)S(1)}, bf16[8,1152]{1,0:T(8,128)(2,1)S(1)}, u32[]{:S(2)}, u32[]{:S(2)}) %collective-permute-start.11) | collective-permute-done | bytes 18464 | tf_op jit(solution)/shard_map/ppermute | solution.py:236
  28.4 2.8 %collective-permute-start.14 = (bf16[8,1152]{1,0:T(8,128)(2,1)S(1)}, bf16[8,1152]{1,0:T(8,128)(2,1)S(1)}, u32[]{:S(2)}, u32[]{:S(2)}) collective-permute-start(bf16[8,1152]{1,0:T(8,128)(2,1)S(1)} %get-tuple-element.41.refs_0_), channel_id=1, source_target_pairs={{0,3},{1,2},{2,1},{3,0},{4,7},{5,6},{6,5},{7,4},{8,11},{9,10},{10,... | collective-permute-start | bytes 55304 | tf_op jit(solution)/shard_map/ppermute | solution.py:236
  31.2 1.6 %collective-permute-start.16 = (bf16[8,1152]{1,0:T(8,128)(2,1)S(1)}, bf16[8,1152]{1,0:T(8,128)(2,1)S(1)}, u32[]{:S(2)}, u32[]{:S(2)}) collective-permute-start(bf16[8,1152]{1,0:T(8,128)(2,1)S(1)} %get-tuple-element.41.refs_0_), channel_id=1, source_target_pairs={{0,1},{1,0},{2,3},{3,2},{4,5},{5,4},{6,7},{7,6},{8,9},{9,8},{10,11... | collective-permute-start | bytes 55304 | tf_op jit(solution)/shard_map/ppermute | solution.py:236
  32.8 1.0 %shard_map.85 = f32[8,1152]{1,0:T(8,128)} custom-call(f32[8,1152]{1,0:T(8,128)S(1)} %get-tuple-element.37.unit_ref, f32[8,128]{1,0:T(8,128)S(1)} %get-tuple-element.38.inverse_ref, bf16[32,1152]{1,0:T(8,128)(2,1)S(1)} %get-tuple-element.39.refs_0_), custom_call_target="tpu_custom_call" | custom-call | tf_op jit(solution)/shard_map/pallas_call | solution.py:22
  34.1 1.8 %collective-permute-done.15.refs_2_ = bf16[8,1152]{1,0:T(8,128)(2,1)S(1)} collective-permute-done((bf16[8,1152]{1,0:T(8,128)(2,1)S(1)}, bf16[8,1152]{1,0:T(8,128)(2,1)S(1)}, u32[]{:S(2)}, u32[]{:S(2)}) %collective-permute-start.15) | collective-permute-done | bytes 18464 | tf_op jit(solution)/shard_map/ppermute | solution.py:236
  35.9 1.0 %shard_map.86 = f32[8,1152]{1,0:T(8,128)} custom-call(f32[8,1152]{1,0:T(8,128)S(1)} %get-tuple-element.40.unit_ref, f32[8,128]{1,0:T(8,128)S(1)} %get-tuple-element.36.refs_4_.inverse_ref, bf16[8,1152]{1,0:T(8,128)(2,1)S(1)} %get-tuple-element.41.refs_0_, bf16[8,1152]{1,0:T(8,128)(2,1)S(1)} %collective-permute-done.14.refs_1_, ...), custom_call_target="tpu_custom_call" | custom-call | tf_op jit(solution)/shard_map/pallas_call | solution.py:22
  (26 shorter events, 1.7 us)
Async XLA Ops:
  0.6 12.1 %copy-start = (bf16[144,1152]{1,0:T(8,128)(2,1)S(1)}, bf16[144,1152]{1,0:T(8,128)(2,1)}, u32[]{:S(2)}) copy-start(bf16[144,1152]{1,0:T(8,128)(2,1)} %refs_4_.3) | copy-start | bytes 995332
  2.2 11.6 %copy-start.2 = (bf16[8,64,1152]{2,1,0:T(8,128)(2,1)S(1)}, bf16[8,64,1152]{2,1,0:T(8,128)(2,1)}, u32[]{:S(2)}) copy-start(bf16[8,64,1152]{2,1,0:T(8,128)(2,1)} %param.6) | copy-start | bytes 3538948
  2.2 10.0 %collective-permute-start = (bf16[16,3024]{1,0:T(8,128)(2,1)S(1)}, bf16[16,3024]{1,0:T(8,128)(2,1)S(1)}, u32[]{:S(2)}, u32[]{:S(2)}) collective-permute-start(bf16[16,3024]{1,0:T(8,128)(2,1)S(1)} %get-tuple-element.23), channel_id=1, source_target_pairs={{0,12},{4,8},{8,4},{12,0},{16,28},{20,24},{24,20},{28,16},{1,13},{... | collective-permute-start | bytes 290312 | tf_op jit(solution)/shard_map/ppermute | solution.py:236
  4.7 7.6 %collective-permute-start.1 = (bf16[16,3024]{1,0:T(8,128)(2,1)S(1)}, bf16[16,3024]{1,0:T(8,128)(2,1)S(1)}, u32[]{:S(2)}, u32[]{:S(2)}) collective-permute-start(bf16[16,3024]{1,0:T(8,128)(2,1)S(1)} %get-tuple-element.24), channel_id=1, source_target_pairs={{0,20},{4,16},{8,28},{12,24},{16,4},{20,0},{24,12},{28,8},{1,21},{... | collective-permute-start | bytes 290312 | tf_op jit(solution)/shard_map/ppermute | solution.py:236
  6.5 6.0 %collective-permute-start.2 = (bf16[16,3024]{1,0:T(8,128)(2,1)S(1)}, bf16[16,3024]{1,0:T(8,128)(2,1)S(1)}, u32[]{:S(2)}, u32[]{:S(2)}) collective-permute-start(bf16[16,3024]{1,0:T(8,128)(2,1)S(1)} %get-tuple-element.25), channel_id=1, source_target_pairs={{0,28},{4,24},{8,20},{12,16},{16,12},{20,8},{24,4},{28,0},{1,29},{... | collective-permute-start | bytes 290312 | tf_op jit(solution)/shard_map/ppermute | solution.py:236
  6.5 5.8 %collective-permute-start.3 = (bf16[8,1152]{1,0:T(8,128)(2,1)}, bf16[8,1152]{1,0:T(8,128)(2,1)S(1)}, u32[]{:S(2)}, u32[]{:S(2)}) collective-permute-start(bf16[8,1152]{1,0:T(8,128)(2,1)} %refs_0_.1), channel_id=1, source_target_pairs={{0,1},{1,2},{2,3},{3,0},{4,5},{5,6},{6,7},{7,4},{8,9},{9,10},{10,1... | collective-permute-start | bytes 55304 | tf_op jit(solution)/shard_map/ppermute | solution.py:241
  12.5 1.3 %collective-permute-start.4 = (bf16[4,16,432]{2,1,0:T(8,128)(2,1)S(1)}, bf16[4,16,432]{2,1,0:T(8,128)(2,1)S(1)}, u32[]{:S(2)}, u32[]{:S(2)}) collective-permute-start(bf16[4,16,432]{2,1,0:T(8,128)(2,1)S(1)} %shard_map.78.own_ref.refs_5_), channel_id=1, source_target_pairs={{0,4},{4,0},{8,12},{12,8},{16,20},{20,16},{24,28},{28,24},{1,5},{5... | collective-permute-start | bytes 165896 | tf_op jit(solution)/shard_map/ppermute | solution.py:236
  12.8 7.8 %collective-permute-start.8 = (bf16[9,16,2592]{2,1,0:T(8,128)(2,1)S(1)}, bf16[9,16,2592]{2,1,0:T(8,128)(2,1)S(1)}, u32[]{:S(2)}, u32[]{:S(2)}) collective-permute-start(bf16[9,16,2592]{2,1,0:T(8,128)(2,1)S(1)} %shard_map.80), channel_id=1, source_target_pairs={{0,4},{4,0},{8,12},{12,8},{16,20},{20,16},{24,28},{28,24},{1,5},{5... | collective-permute-start | bytes 2239496 | tf_op jit(solution)/shard_map/ppermute | solution.py:236
  13.9 4.1 %copy-start.1 = (bf16[8,1152]{1,0:T(8,128)(2,1)S(1)}, bf16[8,1152]{1,0:T(8,128)(2,1)}, u32[]{:S(2)}) copy-start(bf16[8,1152]{1,0:T(8,128)(2,1)} %refs_0_.1) | copy-start | bytes 55300
  14.9 7.3 %collective-permute-start.5 = (bf16[2,16,1152]{2,1,0:T(8,128)(2,1)S(1)}, bf16[2,16,1152]{2,1,0:T(8,128)(2,1)S(1)}, u32[]{:S(2)}, u32[]{:S(2)}) collective-permute-start(bf16[2,16,1152]{2,1,0:T(8,128)(2,1)S(1)} %get-tuple-element.27), channel_id=1, source_target_pairs={{0,12},{4,8},{8,4},{12,0},{16,28},{20,24},{24,20},{28,16},{1,13},{... | collective-permute-start | bytes 221192 | tf_op jit(solution)/shard_map/ppermute | solution.py:236
  16.0 6.2 %collective-permute-start.6 = (bf16[2,16,1152]{2,1,0:T(8,128)(2,1)S(1)}, bf16[2,16,1152]{2,1,0:T(8,128)(2,1)S(1)}, u32[]{:S(2)}, u32[]{:S(2)}) collective-permute-start(bf16[2,16,1152]{2,1,0:T(8,128)(2,1)S(1)} %get-tuple-element.28), channel_id=1, source_target_pairs={{0,20},{4,16},{8,28},{12,24},{16,4},{20,0},{24,12},{28,8},{1,21},{... | collective-permute-start | bytes 221192 | tf_op jit(solution)/shard_map/ppermute | solution.py:236
  17.4 5.1 %collective-permute-start.7 = (bf16[2,16,1152]{2,1,0:T(8,128)(2,1)S(1)}, bf16[2,16,1152]{2,1,0:T(8,128)(2,1)S(1)}, u32[]{:S(2)}, u32[]{:S(2)}) collective-permute-start(bf16[2,16,1152]{2,1,0:T(8,128)(2,1)S(1)} %get-tuple-element.29), channel_id=1, source_target_pairs={{0,28},{4,24},{8,20},{12,16},{16,12},{20,8},{24,4},{28,0},{1,29},{... | collective-permute-start | bytes 221192 | tf_op jit(solution)/shard_map/ppermute | solution.py:236
  17.9 8.2 %collective-permute-start.12 = (bf16[8,1152]{1,0:T(8,128)(2,1)S(1)}, bf16[8,1152]{1,0:T(8,128)(2,1)S(1)}, u32[]{:S(2)}, u32[]{:S(2)}) collective-permute-start(bf16[8,1152]{1,0:T(8,128)(2,1)S(1)} %copy-done.1), channel_id=1, source_target_pairs={{0,2},{1,3},{2,0},{3,1},{4,6},{5,7},{6,4},{7,5},{8,10},{9,11},{10,... | collective-permute-start | bytes 55304 | tf_op jit(solution)/shard_map/ppermute | solution.py:241
  20.5 5.6 %collective-permute-start.13 = (bf16[8,1152]{1,0:T(8,128)(2,1)S(1)}, bf16[8,1152]{1,0:T(8,128)(2,1)S(1)}, u32[]{:S(2)}, u32[]{:S(2)}) collective-permute-start(bf16[8,1152]{1,0:T(8,128)(2,1)S(1)} %copy-done.1), channel_id=1, source_target_pairs={{0,3},{1,0},{2,1},{3,2},{4,7},{5,4},{6,5},{7,6},{8,11},{9,8},{10,9... | collective-permute-start | bytes 55304 | tf_op jit(solution)/shard_map/ppermute | solution.py:241
  23.1 3.3 %collective-permute-start.10 = (bf16[8,1152]{1,0:T(8,128)(2,1)S(1)}, bf16[8,1152]{1,0:T(8,128)(2,1)S(1)}, u32[]{:S(2)}, u32[]{:S(2)}) collective-permute-start(bf16[8,1152]{1,0:T(8,128)(2,1)S(1)} %get-tuple-element.34), channel_id=1, source_target_pairs={{0,20},{4,16},{8,28},{12,24},{16,4},{20,0},{24,12},{28,8},{1,21},{... | collective-permute-start | bytes 55304 | tf_op jit(solution)/shard_map/ppermute | solution.py:236
  23.9 4.1 %collective-permute-start.11 = (bf16[8,1152]{1,0:T(8,128)(2,1)S(1)}, bf16[8,1152]{1,0:T(8,128)(2,1)S(1)}, u32[]{:S(2)}, u32[]{:S(2)}) collective-permute-start(bf16[8,1152]{1,0:T(8,128)(2,1)S(1)} %get-tuple-element.35), channel_id=1, source_target_pairs={{0,28},{4,24},{8,20},{12,16},{16,12},{20,8},{24,4},{28,0},{1,29},{... | collective-permute-start | bytes 55304 | tf_op jit(solution)/shard_map/ppermute | solution.py:236
  25.0 3.3 %collective-permute-start.9 = (bf16[8,1152]{1,0:T(8,128)(2,1)S(1)}, bf16[8,1152]{1,0:T(8,128)(2,1)S(1)}, u32[]{:S(2)}, u32[]{:S(2)}) collective-permute-start(bf16[8,1152]{1,0:T(8,128)(2,1)S(1)} %get-tuple-element.33), channel_id=1, source_target_pairs={{0,12},{4,8},{8,4},{12,0},{16,28},{20,24},{24,20},{28,16},{1,13},{... | collective-permute-start | bytes 55304 | tf_op jit(solution)/shard_map/ppermute | solution.py:236
  28.4 5.7 %collective-permute-start.14 = (bf16[8,1152]{1,0:T(8,128)(2,1)S(1)}, bf16[8,1152]{1,0:T(8,128)(2,1)S(1)}, u32[]{:S(2)}, u32[]{:S(2)}) collective-permute-start(bf16[8,1152]{1,0:T(8,128)(2,1)S(1)} %get-tuple-element.41.refs_0_), channel_id=1, source_target_pairs={{0,3},{1,2},{2,1},{3,0},{4,7},{5,6},{6,5},{7,4},{8,11},{9,10},{10,... | collective-permute-start | bytes 55304 | tf_op jit(solution)/shard_map/ppermute | solution.py:236
  31.2 4.7 %collective-permute-start.15 = (bf16[8,1152]{1,0:T(8,128)(2,1)S(1)}, bf16[8,1152]{1,0:T(8,128)(2,1)S(1)}, u32[]{:S(2)}, u32[]{:S(2)}) collective-permute-start(bf16[8,1152]{1,0:T(8,128)(2,1)S(1)} %get-tuple-element.41.refs_0_), channel_id=1, source_target_pairs={{0,2},{1,3},{2,0},{3,1},{4,6},{5,7},{6,4},{7,5},{8,10},{9,11},{10,... | collective-permute-start | bytes 55304 | tf_op jit(solution)/shard_map/ppermute | solution.py:236
  31.2 4.7 %collective-permute-start.16 = (bf16[8,1152]{1,0:T(8,128)(2,1)S(1)}, bf16[8,1152]{1,0:T(8,128)(2,1)S(1)}, u32[]{:S(2)}, u32[]{:S(2)}) collective-permute-start(bf16[8,1152]{1,0:T(8,128)(2,1)S(1)} %get-tuple-element.41.refs_0_), channel_id=1, source_target_pairs={{0,1},{1,0},{2,3},{3,2},{4,5},{5,4},{6,7},{7,6},{8,9},{9,8},{10,11... | collective-permute-start | bytes 55304 | tf_op jit(solution)/shard_map/ppermute | solution.py:236
